TPU v7x, 32 devices: a whole 2x2x4 slice. The times are simulated.
32 devices in a mesh: cohort: 8 (over z, y), feat: 4 (over x, core).
Axes of the slice: x: 2, y: 2, z: 4, core: 2. Of those that a mesh axis runs over, the one named last changes fastest.
Arguments:
- b_factors: float32 [32, 8192, 256], P('cohort', 'feat'), may hold values from -0.375 to 0.375
- a_factors: float32 [32, 256, 8192], P('cohort', None, 'feat'), may hold values from -0.0625 to 0.0625
- ranks: int32 [32], P('cohort'), may hold values from 8 to 256, as said below
- probes: float32 [8192, 256], P('feat'), may hold values from -6 to 6
Outputs:
- subspace: float32 [8192, 256], P('feat')
Inputs may be any that keep to these rules, and one draw needn't show every extreme that they name: `ranks`: each client's rank is 8 times a power of two; some client has rank 256 and some client has rank 8.
All inputs are finite; a program needn't handle non-finite values.
Results may differ from a plain program's by a relative error of at most 0.00011.
Values sent between devices are 32-bit elements; how exact they have to be, the bound alone decides.
No kernel may reach another device: no remote copies, remote signals or barrier semaphores. Data moves between devices by JAX's collectives and lax.ppermute only.
A program may use at most 64 MiB of HBM per device.

v0:
```python
import math

import jax
import jax.numpy as jnp
from jax import lax
from jax.sharding import PartitionSpec as P

D = 8192
ITERS = 2
NS_STEPS = 5


def product(left, right):
    return jnp.dot(left, right, precision=lax.Precision.HIGHEST, preferred_element_type=jnp.float32)


def coef_terms(a_factors, basis):
    return jnp.einsum(
        "crd,dp->crp",
        a_factors,
        basis,
        precision=lax.Precision.HIGHEST,
        preferred_element_type=jnp.float32,
    )


def panel_terms(b_factors, coef):
    return jnp.einsum(
        "cdr,crp->dp",
        b_factors,
        coef,
        precision=lax.Precision.HIGHEST,
        preferred_element_type=jnp.float32,
    )


def newton(panel, first_total):
    gram = first_total(product(panel.T, panel))
    scale = lax.rsqrt(jnp.trace(gram))
    mixing = jnp.eye(gram.shape[0], dtype=jnp.float32) * scale
    for turn in range(NS_STEPS):
        inner = product(mixing.T, product(gram, mixing))
        mixing = 1.5 * mixing - 0.5 * product(mixing, inner)
    return product(panel, mixing)


def feat_first(gram_part):
    return lax.psum(gram_part, "feat")


def on_device(b_factors, a_factors, ranks, probes):
    slots = jnp.arange(b_factors.shape[2], dtype=jnp.int32)
    live = (slots[None, :] < ranks[:, None]).astype(jnp.float32)
    basis = probes
    for turn in range(ITERS):
        coef_part = coef_terms(a_factors, basis)
        coef = lax.psum(coef_part, "feat") * live[:, :, None]
        panel_part = panel_terms(b_factors, coef)
        panel = lax.psum(panel_part, "cohort")
        basis = newton(panel, feat_first)
    return math.sqrt(D) * basis


def solution(mesh):
    in_specs = (P("cohort", "feat", None), P("cohort", None, "feat"), P("cohort"), P("feat", None))
    out_specs = P("feat", None)
    return jax.shard_map(
        on_device, mesh=mesh, in_specs=in_specs, out_specs=out_specs, check_vma=False
    )
```

profile of v0, /device:TPU:0, one launch (start us, length us, event | category | flops | bytes accessed | tf_op | source)
XLA Modules:
  0.0 455.0 jit_solution(5240760357087678039)
XLA Ops:
  6.5 1.6 copy-done
  8.1 10.7 %fusion = f32[4,256,256]{1,2,0:T(8,128)} fusion(f32[4,256,2048]{2,1,0:T(8,128)} %param.5, f32[2048,256]{1,0:T(8,128)S(1)} %copy-done), kind=kOutput, calls=%fused_computation.4 | convolution fusion | flops 6442450944 | bytes 11534336 | tf_op jit(solution)/shard_map/crd,dp->crp/dot_general | solution.py:18
  19.0 38.8 %all-reduce.7.cloned.1.call-done = f32[4,256,256]{1,2,0:T(8,128)} async-done(((f32[4,256,256]{1,2,0:T(8,128)}), f32[4,256,256]{1,2,0:T(8,128)}) %all-reduce.7.cloned.1.call-update) | async-done | bytes 1048592 | tf_op jit(solution)/shard_map/psum | solution.py:57
  57.9 10.9 %convolution_bitcast_fusion.2 = f32[2048,256]{0,1:T(8,128)} fusion(f32[4,2048,256]{2,1,0:T(8,128)} %param.4, f32[4,256,256]{1,2,0:T(8,128)} %all-reduce.7.cloned.1.call-done, f32[4,256]{1,0:T(4,128)S(1)} %fusion.38), kind=kOutput, calls=%fused_computation.3 | convolution fusion | flops 6442713088 | bytes 11538432 | tf_op jit(solution)/shard_map/cdr,crp->dp/dot_general | solution.py:28
  68.8 102.3 %all-reduce.9.cloned.1.call-done = f32[2048,256]{0,1:T(8,128)} async-done(((f32[2048,256]{0,1:T(8,128)}), f32[2048,256]{0,1:T(8,128)}) %all-reduce.9.cloned.1.call-update) | async-done | bytes 2097168 | tf_op jit(solution)/shard_map/psum | solution.py:59
  171.2 4.8 %fusion.45 = f32[256,256]{1,0:T(8,128)} fusion(f32[2048,256]{0,1:T(8,128)} %all-reduce.9.cloned.1.call-done), kind=kOutput, calls=%fused_computation.66 | convolution fusion | flops 1610612736 | bytes 2359296 | tf_op jit(solution)/shard_map/dot_general | solution.py:14
  176.0 0.3 all-reduce.13.cloned.1.call-start
  176.3 31.5 %all-reduce.11.cloned.1.call-done = f32[256,256]{1,0:T(8,128)} async-done(((f32[256,256]{1,0:T(8,128)}), f32[256,256]{1,0:T(8,128)}) %all-reduce.11.cloned.1.call-update) | async-done | bytes 262160 | tf_op jit(solution)/shard_map/psum | solution.py:48
  207.8 1.7 select_reduce_fusion.1
  210.2 1.5 fusion.24
  211.7 0.4 fusion.22
  212.1 0.4 fusion.11
  212.5 0.4 fusion.46
  212.9 0.6 fusion.47
  213.5 0.4 fusion.10
  213.9 0.4 fusion.48
  214.3 0.6 fusion.49
  214.9 0.4 fusion.9
  215.3 0.4 fusion.50
  215.7 0.6 fusion.51
  216.3 0.4 fusion.8
  216.7 0.4 fusion.52
  217.0 0.6 fusion.53
  217.7 0.4 fusion.7
  218.1 3.6 convolution_bitcast_fusion.1
  221.7 24.9 %convolution_bitcast_fusion.3 = f32[4,256,256]{1,2,0:T(8,128)} fusion(f32[2048,256,1]{1,0,2:T(8,128)S(1)} %convolution_bitcast_fusion.1, f32[4,256,2048]{2,1,0:T(8,128)S(1)} %bitcast.83), kind=kOutput, calls=%fused_computation.6 | convolution fusion | flops 6442450944 | bytes 11534336 | tf_op jit(solution)/shard_map/crd,dp->crp/dot_general | solution.py:18
  246.6 36.2 %all-reduce.13.cloned.1.call-done = f32[4,256,256]{1,2,0:T(8,128)} async-done(((f32[4,256,256]{1,2,0:T(8,128)}), f32[4,256,256]{1,2,0:T(8,128)}) %all-reduce.13.cloned.1.call-update) | async-done | bytes 1048592 | tf_op jit(solution)/shard_map/psum | solution.py:57
  282.8 10.9 %convolution_bitcast_fusion = f32[2048,256]{0,1:T(8,128)} fusion(f32[4,2048,256]{2,1,0:T(8,128)} %param.4, f32[4,256,256]{1,2,0:T(8,128)} %all-reduce.13.cloned.1.call-done, f32[4,256]{1,0:T(4,128)S(1)} %fusion.38), kind=kOutput, calls=%fused_computation.1 | convolution fusion | flops 6442713088 | bytes 11538432 | tf_op jit(solution)/shard_map/cdr,crp->dp/dot_general | solution.py:28
  294.0 102.1 %all-reduce.15.cloned.1.call-done = f32[2048,256]{0,1:T(8,128)} async-done(((f32[2048,256]{0,1:T(8,128)}), f32[2048,256]{0,1:T(8,128)}) %all-reduce.15.cloned.1.call-update) | async-done | bytes 2097168 | tf_op jit(solution)/shard_map/psum | solution.py:59
  396.1 4.8 %fusion.54 = f32[256,256]{1,0:T(8,128)} fusion(f32[2048,256]{0,1:T(8,128)} %all-reduce.15.cloned.1.call-done), kind=kOutput, calls=%fused_computation.75 | convolution fusion | flops 1610612736 | bytes 2359296 | tf_op jit(solution)/shard_map/dot_general | solution.py:14
  401.0 31.9 %all-reduce.17.cloned.1.call-done = f32[256,256]{1,0:T(8,128)} async-done(((f32[256,256]{1,0:T(8,128)}), f32[256,256]{1,0:T(8,128)}) %all-reduce.17.cloned.1.call-update) | async-done | bytes 262160 | tf_op jit(solution)/shard_map/psum | solution.py:48
  432.8 1.7 select_reduce_fusion
  435.2 1.3 fusion.19
  436.5 0.4 fusion.17
  436.9 0.4 fusion.6
  437.3 0.4 fusion.55
  437.7 0.6 fusion.56
  438.3 0.4 fusion.5
  438.7 0.4 fusion.57
  439.1 0.6 fusion.58
  439.7 0.4 fusion.4
  440.1 0.4 fusion.59
  440.5 0.6 fusion.60
  441.1 0.4 fusion.3
  441.5 0.4 fusion.61
  441.9 0.6 fusion.62
  442.5 0.4 fusion.2
  442.9 4.9 %convolution_multiply_fusion = f32[2048,256]{1,0:T(8,128)} fusion(f32[2048,256]{0,1:T(8,128)S(1)} %copy-done.2, f32[256,256]{1,0:T(8,128)S(1)} %fusion.2), kind=kOutput, calls=%fused_computation | convolution fusion | flops 1611137024 | bytes 4456448 | tf_op jit(solution)/shard_map/dot_general | solution.py:14
  (28 shorter events, 0.6 us)
Async XLA Ops:
  6.5 1.6 copy-start
  6.5 12.4 %copy-start.5 = (s32[4]{0:T(128)S(1)}, s32[4]{0:T(128)}, u32[]{:S(2)}) copy-start(s32[4]{0:T(128)} %param.6) | copy-start | bytes 52
  6.5 51.3 %all-reduce.7.cloned.1.call-start = ((), (), s32[]{:S(2)}) async-start(), calls=%async_computation | async-start | bytes 2097152 | tf_op jit(solution)/shard_map/psum | solution.py:57
  18.9 152.3 %all-reduce.9.cloned.1.call-start = ((), (), s32[]{:S(2)}) async-start(), calls=%async_computation.1 | async-start | bytes 4194304 | tf_op jit(solution)/shard_map/psum | solution.py:59
  68.8 139.1 %all-reduce.11.cloned.1.call-start = ((), (), s32[]{:S(2)}) async-start(), calls=%async_computation.2 | async-start | bytes 524288 | tf_op jit(solution)/shard_map/psum | solution.py:48
  176.0 106.9 %all-reduce.13.cloned.1.call-start = ((), (), s32[]{:S(2)}) async-start(), calls=%async_computation.3 | async-start | bytes 2097152 | tf_op jit(solution)/shard_map/psum | solution.py:57
  207.8 4.7 %copy-start.3 = (f32[256,256]{1,0:T(8,128)S(1)}, f32[256,256]{1,0:T(8,128)}, u32[]{:S(2)}) copy-start(f32[256,256]{1,0:T(8,128)} %all-reduce.11.cloned.1.call-done) | copy-start | bytes 786436
  210.2 11.5 %slice-start = ((s8[8388608]{0:T(1024)(128)(4,1)}), s8[4194304]{0:T(1024)(128)(4,1)S(1)}, s32[]{:S(2)}) async-start(s8[8388608]{0:T(1024)(128)(4,1)} %bitcast.82), calls=%async_computation.6 | async-start | bytes 8388608
  215.3 2.8 copy-start.1
  215.7 6.0 %slice-start.1 = ((s8[8388608]{0:T(1024)(128)(4,1)}), s8[4194304]{0:T(1024)(128)(4,1)S(1)}, s32[]{:S(2)}) async-start(s8[8388608]{0:T(1024)(128)(4,1)} %bitcast.82), calls=%async_computation.7 | async-start | bytes 8388608
  246.6 149.5 %all-reduce.15.cloned.1.call-start = ((), (), s32[]{:S(2)}) async-start(), calls=%async_computation.4 | async-start | bytes 4194304 | tf_op jit(solution)/shard_map/psum | solution.py:59
  293.7 139.1 %all-reduce.17.cloned.1.call-start = ((), (), s32[]{:S(2)}) async-start(), calls=%async_computation.5 | async-start | bytes 524288 | tf_op jit(solution)/shard_map/psum | solution.py:48
  432.8 4.5 copy-start.4
  440.5 2.4 copy-start.2
Sparse Core Ops, SparseCore 0:
  19.0 38.8 all-reduce.6
  68.9 102.2 all-reduce.8
  176.1 31.6 all-reduce.10
  246.7 36.0 all-reduce.12
  293.9 102.2 all-reduce.14
  401.1 31.6 all-reduce.16
where the time goes:
time: 462 us; the launch traced here: 455 us
  waiting for transfers between devices  343 us (74%)
  matrix products  90.7 us (20%)
  between operations  15.6 us (3%)
    psum x2, waiting for transfers between devices, on_device(): panel = lax.psum(panel_part, 'cohort')  204 us
    psum x2, waiting for transfers between devices, on_device(): coef = lax.psum(coef_part, 'feat') * live[:, :, None]  75 us
    psum x2, waiting for transfers between devices, feat_first(): return lax.psum(gram_part, 'feat')  63.4 us
    dot_general x2, matrix products, coef_terms(): jnp.einsum('crd,dp->crp', a_factors, basis, precision=lax.Precision.HIGHE...  35.6 us
    dot_general x34, matrix products, product(): jnp.dot(left, right, precision=lax.Precision.HIGHEST, preferred_element_t...  33.4 us
    dot_general x2, matrix products, panel_terms(): jnp.einsum('cdr,crp->dp', b_factors, coef, precision=lax.Precision.HIGHES...  21.7 us
  transfers between devices with their start and end apart: 6, of which 6 were waited for; matrix products, arithmetic and copies ran while one was open for 0% of the time, Pallas kernels for 0%

commit v1 on v0

v1 whole, which is shorter than its diff:
```python
import math

import jax
import jax.numpy as jnp
from jax import lax
from jax.sharding import PartitionSpec as P

ITERS = 2
NS_STEPS = 5
GROUPS = 2


def product(left, right):
    return jnp.dot(left, right, precision=lax.Precision.HIGH, preferred_element_type=jnp.float32)


def coef_terms(a_factors, basis):
    return jnp.einsum("crd,dp->crp", a_factors, basis, precision=lax.Precision.HIGH, preferred_element_type=jnp.float32)


def panel_terms(b_factors, coef):
    return jnp.einsum("cdr,crp->dp", b_factors, coef, precision=lax.Precision.HIGH, preferred_element_type=jnp.float32)


class Grid:
    def __init__(self, mesh):
        self.cohorts = mesh.shape["cohort"]
        self.feats = mesh.shape["feat"]
        self.places = self.cohorts // 2
        cohort = lax.axis_index("cohort")
        self.place, self.side = cohort // 2, cohort % 2
        self.half = lax.axis_index("feat") % 2

    def across(self, block):
        return lax.ppermute(block, "cohort", [(i, i ^ 1) for i in range(self.cohorts)])

    def along(self, block):
        return lax.ppermute(block, "cohort", [(i, (i + 2) % self.cohorts) for i in range(self.cohorts)])

    def feat_swap(self, block, bit):
        return lax.ppermute(block, "feat", [(i, i ^ bit) for i in range(self.feats)])

    def feat_sum(self, part):
        rows = part.shape[0] // 2
        mine = lax.dynamic_slice(part, (self.half * rows, 0), (rows, part.shape[1]))
        other = lax.dynamic_slice(part, ((1 - self.half) * rows, 0), (rows, part.shape[1]))
        total = mine + self.feat_swap(other, 1)
        bit = 2
        while bit < self.feats:
            total = total + self.feat_swap(total, bit)
            bit *= 2
        partner = self.feat_swap(total, 1)
        low = jnp.where(self.half == 0, total, partner)
        high = jnp.where(self.half == 0, partner, total)
        return jnp.concatenate([low, high], 0)

    def scatter_sum(self, part):
        rows = part.shape[0] // self.cohorts

        def block(place, side):
            index = lax.rem(place + self.places, self.places) * 2 + side
            return lax.dynamic_slice(part, (index * rows, 0), (rows, part.shape[1]))

        total = None
        for step in range(1, self.places + 1):
            fresh = self.across(block(self.place - step, 1 - self.side)) + block(self.place - step, self.side)
            total = fresh if total is None else fresh + self.along(total)
        return total

    def gather(self, block):
        rows, columns = block.shape
        whole = jnp.zeros((self.cohorts * rows, columns), block.dtype)
        for step in range(self.places):
            place = lax.rem(self.place - step + self.places, self.places)
            whole = lax.dynamic_update_slice(whole, block, ((place * 2 + self.side) * rows, 0))
            whole = lax.dynamic_update_slice(whole, self.across(block), ((place * 2 + 1 - self.side) * rows, 0))
            if step < self.places - 1:
                block = self.along(block)
        return whole


def newton(gram):
    size = gram.shape[0]
    eye = jnp.eye(size, dtype=jnp.float32)
    scale = lax.rsqrt(jnp.trace(gram))
    inner = gram * (scale * scale)
    mixing = eye * scale
    for turn in range(NS_STEPS):
        factor = 1.5 * eye - 0.5 * inner
        mixing = product(mixing, factor) if turn else factor * scale
        if turn < NS_STEPS - 1:
            inner = product(product(inner, factor), factor)
    return mixing


def solution(mesh):
    def on_device(b_factors, a_factors, ranks, probes):
        grid = Grid(mesh)
        clients, rows, slots = b_factors.shape
        features = rows * grid.feats
        columns = probes.shape[1] // GROUPS
        live = (jnp.arange(slots, dtype=jnp.int32)[None, :] < ranks[:, None]).astype(jnp.float32)
        live = live.reshape(clients * slots, 1)

        def apply(basis, normalize):
            part = coef_terms(a_factors, basis).reshape(clients * slots, -1)
            scale = jnp.ones((), jnp.float32)
            if normalize:
                squares = jnp.full((16, part.shape[1]), jnp.sum(basis * basis), jnp.float32)
                part = jnp.concatenate([part, squares], 0)
            total = grid.feat_sum(part)
            if normalize:
                square = total[clients * slots, 0]
                scale = jnp.where(square > 0, lax.rsqrt(square), 1.0)
            coef = (total[: clients * slots] * (live * scale)).reshape(clients, slots, -1)
            return grid.gather(grid.scatter_sum(panel_terms(b_factors, coef))), scale

        mixing = None
        panels = [probes[:, g * columns : (g + 1) * columns] for g in range(GROUPS)]
        for turn in range(ITERS):
            done = [apply(panel, turn > 0) for panel in panels]
            panels = [panel for panel, scale in done]
            scales = jnp.concatenate([jnp.full((columns, 1), 1.0 / scale) for panel, scale in done], 0)
            panel = jnp.concatenate(panels, 1)
            gram = grid.feat_sum(product(panel.T, panel))
            if mixing is None:
                mixing = newton(gram)
            else:
                mixing = scales * mixing
                mixing = product(mixing, newton(product(mixing.T, product(gram, mixing))))
        return product(panel, mixing * math.sqrt(features))

    in_specs = (P("cohort", "feat", None), P("cohort", None, "feat"), P("cohort"), P("feat", None))
    return jax.shard_map(on_device, mesh=mesh, in_specs=in_specs, out_specs=P("feat", None), check_vma=False)
```

time: 462 us -> 267 us (0.58)
  waiting for transfers between devices: 343 us -> 135 us
  starting transfers between devices: 0.68 us -> 47.1 us
  matrix products: 90.7 us -> 65.3 us
  between operations: 15.6 us -> 5.71 us
    psum x6 -> x0, waiting for transfers between devices: 343 us -> none  [the longest x2 204 us: on_device(): panel = lax.psum(panel_part, 'cohort')]
    ppermute x0 -> x74, waiting for transfers between devices: none -> 135 us  [the longest x24 87.3 us: along(): lax.ppermute(block, 'cohort', [(i, (i + 2) % self.cohorts) for i in range...]
    ppermute x0 -> x74, starting transfers between devices: none -> 47.1 us  [the longest x32 33.4 us: across(): lax.ppermute(block, 'cohort', [(i, i ^ 1) for i in range(self.cohorts)])]
    dot_general x38, matrix products: 90.7 us -> 65.3 us  [the longest x4 26.9 us: panel_terms(): jnp.einsum('cdr,crp->dp', b_factors, coef, precision=lax.Precision.HIGH,...]
  transfers between devices with their start and end apart: 6 -> 74, of which waited for: 6 -> 36; matrix products, arithmetic and copies ran while one was open for 0% -> 17% of each run, Pallas kernels for 0% -> 0%
where the time goes in v1:
time: 267 us; the launch traced here: 264 us
  waiting for transfers between devices  135 us (51%)
  matrix products  65.3 us (24%)
  starting transfers between devices  47.1 us (18%)
  other arithmetic  6.32 us (2%)
  between operations  5.71 us (2%)
  local copies, waits for them, and re-layouts  4.51 us (2%)
    ppermute x24, waiting for transfers between devices, along(): lax.ppermute(block, 'cohort', [(i, (i + 2) % self.cohorts) for i in range...  87.3 us
    ppermute x32, starting transfers between devices, across(): lax.ppermute(block, 'cohort', [(i, i ^ 1) for i in range(self.cohorts)])  33.4 us
    ppermute x18, waiting for transfers between devices, feat_swap(): lax.ppermute(block, 'feat', [(i, i ^ bit) for i in range(self.feats)])  28.4 us
    dot_general x4, matrix products, panel_terms(): jnp.einsum('cdr,crp->dp', b_factors, coef, precision=lax.Precision.HIGH,...  26.9 us
    dot_general x4, matrix products, coef_terms(): jnp.einsum('crd,dp->crp', a_factors, basis, precision=lax.Precision.HIGH,...  24.6 us
    ppermute x32, waiting for transfers between devices, across(): lax.ppermute(block, 'cohort', [(i, i ^ 1) for i in range(self.cohorts)])  19.1 us
    dot_general x30, matrix products, product(): jnp.dot(left, right, precision=lax.Precision.HIGH, preferred_element_type...  13.8 us
    ppermute x18, starting transfers between devices, feat_swap(): lax.ppermute(block, 'feat', [(i, i ^ bit) for i in range(self.feats)])  10.6 us
  transfers between devices with their start and end apart: 74, of which 36 were waited for; matrix products, arithmetic and copies ran while one was open for 17% of the time, Pallas kernels for 0%

profile of v1, /device:TPU:0, one launch (start us, length us, event | category | flops | bytes accessed | tf_op | source)
XLA Modules:
  0.0 263.7 jit_solution(854159904981662486)
XLA Ops:
  0.0 6.3 %fusion.9 = f32[4,256,128]{2,1,0:T(8,128)S(1)} fusion(f32[4,256,2048]{2,1,0:T(8,128)} %param.5, f32[2048,256]{1,0:T(8,128)} %param.7), kind=kOutput, calls=%fused_computation.20 | convolution fusion | flops 1610612736 | bytes 9961472 | tf_op jit(solution)/shard_map/crd,dp->crp/dot_general | solution.py:18
  6.8 6.0 %fusion.12 = f32[4,256,128]{2,1,0:T(8,128)S(1)} fusion(f32[4,256,2048]{2,1,0:T(8,128)} %param.5, f32[2048,256]{1,0:T(8,128)S(1)} %copy-done), kind=kOutput, calls=%fused_computation.23 | convolution fusion | flops 1610612736 | bytes 9961472 | tf_op jit(solution)/shard_map/crd,dp->crp/dot_general | solution.py:18
  14.0 3.0 %collective-permute-start.35 = (f32[512,128]{1,0:T(8,128)S(1)}, f32[512,128]{1,0:T(8,128)S(1)}, u32[]{:S(2)}, u32[]{:S(2)}) collective-permute-start(f32[512,128]{1,0:T(8,128)S(1)} %dynamic-slice_add_fusion), channel_id=1, source_target_pairs={{0,2},{1,3},{2,0},{3,1},{4,6},{5,7},{6,4},{7,5},{8,10},{9,11},{10,... | collective-permute-start | bytes 786440 | tf_op jit(solution)/shard_map/ppermute | solution.py:41
  17.2 6.9 %collective-permute-done.35 = f32[512,128]{1,0:T(8,128)S(1)} collective-permute-done((f32[512,128]{1,0:T(8,128)S(1)}, f32[512,128]{1,0:T(8,128)S(1)}, u32[]{:S(2)}, u32[]{:S(2)}) %collective-permute-start.35) | collective-permute-done | bytes 262176 | tf_op jit(solution)/shard_map/ppermute | solution.py:41
  24.4 4.7 %collective-permute-done.1 = f32[512,128]{1,0:T(8,128)S(1)} collective-permute-done((f32[512,128]{1,0:T(8,128)S(1)}, f32[512,128]{1,0:T(8,128)S(1)}, u32[]{:S(2)}, u32[]{:S(2)}) %collective-permute-start.1) | collective-permute-done | bytes 262176 | tf_op jit(solution)/shard_map/ppermute | solution.py:41
  29.3 7.0 %convolution_bitcast_fusion.1 = f32[128,2048]{1,0:T(8,128)S(1)} fusion(f32[4,2048,256]{2,1,0:T(8,128)} %param.4, f32[4,256,128]{2,1,0:T(8,128)S(1)} %bitcast.185, f32[4,256]{1,0:T(4,128)S(1)} %fusion.142), kind=kOutput, calls=%fused_computation.1 | convolution fusion | flops 1610743808 | bytes 9965568 | tf_op jit(solution)/shard_map/cdr,crp->dp/dot_general | solution.py:22
  36.4 1.8 collective-permute-start.40
  40.7 7.0 %convolution_bitcast_fusion.3 = f32[128,2048]{1,0:T(8,128)S(1)} fusion(f32[4,2048,256]{2,1,0:T(8,128)} %param.4, f32[4,256,128]{2,1,0:T(8,128)S(1)} %bitcast.182, f32[4,256]{1,0:T(4,128)S(1)} %fusion.142), kind=kOutput, calls=%fused_computation.3 | convolution fusion | flops 1610743808 | bytes 9965568 | tf_op jit(solution)/shard_map/cdr,crp->dp/dot_general | solution.py:22
  47.8 1.8 collective-permute-start.6
  49.9 4.4 %collective-permute-done.6 = f32[256,128]{0,1:T(8,128)S(1)} collective-permute-done((f32[256,128]{0,1:T(8,128)S(1)}, f32[256,128]{0,1:T(8,128)S(1)}, u32[]{:S(2)}, u32[]{:S(2)}) %collective-permute-start.6) | collective-permute-done | bytes 131104 | tf_op jit(solution)/shard_map/ppermute | solution.py:35
  54.3 1.8 collective-permute-start.41
  57.7 3.4 %collective-permute-done.41 = f32[256,128]{0,1:T(8,128)S(1)} collective-permute-done((f32[256,128]{0,1:T(8,128)S(1)}, f32[256,128]{0,1:T(8,128)S(1)}, u32[]{:S(2)}, u32[]{:S(2)}) %collective-permute-start.41) | collective-permute-done | bytes 131104 | tf_op jit(solution)/shard_map/ppermute | solution.py:38
  61.1 1.8 collective-permute-start.3
  62.9 4.9 %collective-permute-done.7 = f32[256,128]{0,1:T(8,128)S(1)} collective-permute-done((f32[256,128]{0,1:T(8,128)S(1)}, f32[256,128]{0,1:T(8,128)S(1)}, u32[]{:S(2)}, u32[]{:S(2)}) %collective-permute-start.7) | collective-permute-done | bytes 131104 | tf_op jit(solution)/shard_map/ppermute | solution.py:38
  68.3 6.3 %collective-permute-done.42 = f32[256,128]{0,1:T(8,128)S(1)} collective-permute-done((f32[256,128]{0,1:T(8,128)S(1)}, f32[256,128]{0,1:T(8,128)S(1)}, u32[]{:S(2)}, u32[]{:S(2)}) %collective-permute-start.42) | collective-permute-done | bytes 131104 | tf_op jit(solution)/shard_map/ppermute | solution.py:38
  74.7 2.5 collective-permute-done.8
  77.3 4.1 %collective-permute-done.43 = f32[256,128]{0,1:T(8,128)S(1)} collective-permute-done((f32[256,128]{0,1:T(8,128)S(1)}, f32[256,128]{0,1:T(8,128)S(1)}, u32[]{:S(2)}, u32[]{:S(2)}) %collective-permute-start.43) | collective-permute-done | bytes 131104 | tf_op jit(solution)/shard_map/ppermute | solution.py:38
  81.7 3.8 %collective-permute-done.9 = f32[256,128]{0,1:T(8,128)S(1)} collective-permute-done((f32[256,128]{0,1:T(8,128)S(1)}, f32[256,128]{0,1:T(8,128)S(1)}, u32[]{:S(2)}, u32[]{:S(2)}) %collective-permute-start.9) | collective-permute-done | bytes 131104 | tf_op jit(solution)/shard_map/ppermute | solution.py:38
  85.6 2.1 collective-permute-start.44
  90.2 3.4 %collective-permute-done.11 = f32[256,128]{0,1:T(8,128)S(1)} collective-permute-done((f32[256,128]{0,1:T(8,128)S(1)}, f32[256,128]{0,1:T(8,128)S(1)}, u32[]{:S(2)}, u32[]{:S(2)}) %collective-permute-start.11) | collective-permute-done | bytes 131104 | tf_op jit(solution)/shard_map/ppermute | solution.py:38
  95.1 2.5 collective-permute-done.47
  97.7 4.1 %collective-permute-done.13 = f32[256,128]{0,1:T(8,128)S(1)} collective-permute-done((f32[256,128]{0,1:T(8,128)S(1)}, f32[256,128]{0,1:T(8,128)S(1)}, u32[]{:S(2)}, u32[]{:S(2)}) %collective-permute-start.13) | collective-permute-done | bytes 131104 | tf_op jit(solution)/shard_map/ppermute | solution.py:38
  104.4 2.0 collective-permute-start.50
  106.4 3.7 %collective-permute-done.15 = f32[256,128]{0,1:T(8,128)S(1)} collective-permute-done((f32[256,128]{0,1:T(8,128)S(1)}, f32[256,128]{0,1:T(8,128)S(1)}, u32[]{:S(2)}, u32[]{:S(2)}) %collective-permute-start.15) | collective-permute-done | bytes 131104 | tf_op jit(solution)/shard_map/ppermute | solution.py:38
  110.9 4.2 %collective-permute-done.16 = f32[256,128]{0,1:T(8,128)S(1)} collective-permute-done((f32[256,128]{0,1:T(8,128)S(1)}, f32[256,128]{0,1:T(8,128)S(1)}, u32[]{:S(2)}, u32[]{:S(2)}) %collective-permute-start.16) | collective-permute-done | bytes 131104 | tf_op jit(solution)/shard_map/ppermute | solution.py:35
  115.1 7.8 %convolution_bitcast_fusion.5 = f32[4,256,128]{1,2,0:T(8,128)S(1)} fusion(f32[4,256,2048]{2,1,0:T(8,128)} %param.5, f32[2048,128]{0,1:T(8,128)S(1)} %constant_dynamic-update-slice_fusion.24), kind=kOutput, calls=%fused_computation.12 | convolution fusion | flops 1610612736 | bytes 9961472 | tf_op jit(solution)/shard_map/crd,dp->crp/dot_general | solution.py:18
  125.0 4.5 %convolution_bitcast_fusion.4 = f32[4,256,128]{1,2,0:T(8,128)S(1)} fusion(f32[4,256,2048]{2,1,0:T(8,128)S(1)} %bitcast.171, f32[2048,128]{0,1:T(8,128)S(1)} %constant_dynamic-update-slice_fusion.8), kind=kOutput, calls=%fused_computation.11 | convolution fusion | flops 1610612736 | bytes 9961472 | tf_op jit(solution)/shard_map/crd,dp->crp/dot_general | solution.py:18
  135.1 3.1 %collective-permute-done.69 = f32[128,256]{1,0:T(8,128)S(1)} collective-permute-done((f32[128,256]{1,0:T(8,128)S(1)}, f32[128,256]{1,0:T(8,128)S(1)}, u32[]{:S(2)}, u32[]{:S(2)}) %collective-permute-start.69) | collective-permute-done | bytes 131104 | tf_op jit(solution)/shard_map/ppermute | solution.py:41
  145.0 3.3 %collective-permute-done.18 = f32[520,128]{1,0:T(8,128)S(1)} collective-permute-done((f32[520,128]{1,0:T(8,128)S(1)}, f32[520,128]{1,0:T(8,128)S(1)}, u32[]{:S(2)}, u32[]{:S(2)}) %collective-permute-start.18) | collective-permute-done | bytes 266272 | tf_op jit(solution)/shard_map/ppermute | solution.py:41
  148.7 4.9 %collective-permute-done.52 = f32[520,128]{1,0:T(8,128)S(1)} collective-permute-done((f32[520,128]{1,0:T(8,128)S(1)}, f32[520,128]{1,0:T(8,128)S(1)}, u32[]{:S(2)}, u32[]{:S(2)}) %collective-permute-start.52) | collective-permute-done | bytes 266272 | tf_op jit(solution)/shard_map/ppermute | solution.py:41
  158.2 8.5 %convolution_bitcast_fusion = f32[128,2048]{1,0:T(8,128)S(1)} fusion(f32[4,256,128]{2,1,0:T(8,128)S(1)} %bitcast.183, f32[4,2048,256]{2,1,0:T(8,128)} %param.4), kind=kOutput, calls=%fused_computation | convolution fusion | flops 1610612736 | bytes 9961472 | tf_op jit(solution)/shard_map/cdr,crp->dp/dot_general | solution.py:22
  171.0 4.4 %convolution_bitcast_fusion.2 = f32[128,2048]{1,0:T(8,128)S(1)} fusion(f32[4,256,128]{2,1,0:T(8,128)S(1)} %bitcast.184, f32[4,2048,256]{2,1,0:T(8,128)S(1)} %bitcast.173), kind=kOutput, calls=%fused_computation.2 | convolution fusion | flops 1610612736 | bytes 9961472 | tf_op jit(solution)/shard_map/cdr,crp->dp/dot_general | solution.py:22
  177.6 6.7 %collective-permute-done.23 = f32[256,128]{0,1:T(8,128)S(1)} collective-permute-done((f32[256,128]{0,1:T(8,128)S(1)}, f32[256,128]{0,1:T(8,128)S(1)}, u32[]{:S(2)}, u32[]{:S(2)}) %collective-permute-start.23) | collective-permute-done | bytes 131104 | tf_op jit(solution)/shard_map/ppermute | solution.py:35
  185.0 6.0 %collective-permute-done.58 = f32[256,128]{0,1:T(8,128)S(1)} collective-permute-done((f32[256,128]{0,1:T(8,128)S(1)}, f32[256,128]{0,1:T(8,128)S(1)}, u32[]{:S(2)}, u32[]{:S(2)}) %collective-permute-start.58) | collective-permute-done | bytes 131104 | tf_op jit(solution)/shard_map/ppermute | solution.py:38
  191.8 6.0 %collective-permute-done.24 = f32[256,128]{0,1:T(8,128)S(1)} collective-permute-done((f32[256,128]{0,1:T(8,128)S(1)}, f32[256,128]{0,1:T(8,128)S(1)}, u32[]{:S(2)}, u32[]{:S(2)}) %collective-permute-start.24) | collective-permute-done | bytes 131104 | tf_op jit(solution)/shard_map/ppermute | solution.py:38
  197.9 6.7 %collective-permute-done.59 = f32[256,128]{0,1:T(8,128)S(1)} collective-permute-done((f32[256,128]{0,1:T(8,128)S(1)}, f32[256,128]{0,1:T(8,128)S(1)}, u32[]{:S(2)}, u32[]{:S(2)}) %collective-permute-start.59) | collective-permute-done | bytes 131104 | tf_op jit(solution)/shard_map/ppermute | solution.py:38
  204.7 2.3 collective-permute-done.25
  207.1 4.3 %collective-permute-done.60 = f32[256,128]{0,1:T(8,128)S(1)} collective-permute-done((f32[256,128]{0,1:T(8,128)S(1)}, f32[256,128]{0,1:T(8,128)S(1)}, u32[]{:S(2)}, u32[]{:S(2)}) %collective-permute-start.60) | collective-permute-done | bytes 131104 | tf_op jit(solution)/shard_map/ppermute | solution.py:38
  212.3 2.9 %collective-permute-done.26 = f32[256,128]{0,1:T(8,128)S(1)} collective-permute-done((f32[256,128]{0,1:T(8,128)S(1)}, f32[256,128]{0,1:T(8,128)S(1)}, u32[]{:S(2)}, u32[]{:S(2)}) %collective-permute-start.26) | collective-permute-done | bytes 131104 | tf_op jit(solution)/shard_map/ppermute | solution.py:38
  216.0 3.0 %collective-permute-done.62 = f32[256,128]{0,1:T(8,128)S(1)} collective-permute-done((f32[256,128]{0,1:T(8,128)S(1)}, f32[256,128]{0,1:T(8,128)S(1)}, u32[]{:S(2)}, u32[]{:S(2)}) %collective-permute-start.62) | collective-permute-done | bytes 131104 | tf_op jit(solution)/shard_map/ppermute | solution.py:38
  220.4 3.2 %collective-permute-done.28 = f32[256,128]{0,1:T(8,128)S(1)} collective-permute-done((f32[256,128]{0,1:T(8,128)S(1)}, f32[256,128]{0,1:T(8,128)S(1)}, u32[]{:S(2)}, u32[]{:S(2)}) %collective-permute-start.28) | collective-permute-done | bytes 131104 | tf_op jit(solution)/shard_map/ppermute | solution.py:38
  223.9 3.2 %collective-permute-done.64 = f32[256,128]{0,1:T(8,128)S(1)} collective-permute-done((f32[256,128]{0,1:T(8,128)S(1)}, f32[256,128]{0,1:T(8,128)S(1)}, u32[]{:S(2)}, u32[]{:S(2)}) %collective-permute-start.64) | collective-permute-done | bytes 131104 | tf_op jit(solution)/shard_map/ppermute | solution.py:38
  227.9 4.2 %collective-permute-done.30 = f32[256,128]{0,1:T(8,128)S(1)} collective-permute-done((f32[256,128]{0,1:T(8,128)S(1)}, f32[256,128]{0,1:T(8,128)S(1)}, u32[]{:S(2)}, u32[]{:S(2)}) %collective-permute-start.30) | collective-permute-done | bytes 131104 | tf_op jit(solution)/shard_map/ppermute | solution.py:38
  236.0 3.9 %collective-permute-done.32 = f32[256,128]{0,1:T(8,128)S(1)} collective-permute-done((f32[256,128]{0,1:T(8,128)S(1)}, f32[256,128]{0,1:T(8,128)S(1)}, u32[]{:S(2)}, u32[]{:S(2)}) %collective-permute-start.32) | collective-permute-done | bytes 131104 | tf_op jit(solution)/shard_map/ppermute | solution.py:38
  241.1 3.7 %collective-permute-done.33 = f32[256,128]{0,1:T(8,128)S(1)} collective-permute-done((f32[256,128]{0,1:T(8,128)S(1)}, f32[256,128]{0,1:T(8,128)S(1)}, u32[]{:S(2)}, u32[]{:S(2)}) %collective-permute-start.33) | collective-permute-done | bytes 131104 | tf_op jit(solution)/shard_map/ppermute | solution.py:35
  247.4 1.8 collective-permute-start.72
  249.6 3.4 %collective-permute-done.72 = f32[128,256]{1,0:T(8,128)S(1)} collective-permute-done((f32[128,256]{1,0:T(8,128)S(1)}, f32[128,256]{1,0:T(8,128)S(1)}, u32[]{:S(2)}, u32[]{:S(2)}) %collective-permute-start.72) | collective-permute-done | bytes 131104 | tf_op jit(solution)/shard_map/ppermute | solution.py:41
  260.3 3.2 %fusion.4 = f32[2048,256]{1,0:T(8,128)} fusion(f32[256,256]{1,0:T(8,128)S(1)} %convolution_multiply_fusion, f32[2048,128]{0,1:T(8,128)S(1)} %constant_dynamic-update-slice_fusion, f32[2048,128]{0,1:T(8,128)S(1)} %constant_dynamic-update-slice_fusion.16), kind=kOutput, calls=%fused_computation.9 | convolution fusion | flops 805830656 | bytes 4456448 | tf_op jit(solution)/shard_map/dot_general | solution.py:14
  (245 shorter events, 57.5 us)
Async XLA Ops:
  14.0 10.1 %collective-permute-start.35 = (f32[512,128]{1,0:T(8,128)S(1)}, f32[512,128]{1,0:T(8,128)S(1)}, u32[]{:S(2)}, u32[]{:S(2)}) collective-permute-start(f32[512,128]{1,0:T(8,128)S(1)} %dynamic-slice_add_fusion), channel_id=1, source_target_pairs={{0,2},{1,3},{2,0},{3,1},{4,6},{5,7},{6,4},{7,5},{8,10},{9,11},{10,... | collective-permute-start | bytes 786440 | tf_op jit(solution)/shard_map/ppermute | solution.py:41
  17.0 12.1 %collective-permute-start.1 = (f32[512,128]{1,0:T(8,128)S(1)}, f32[512,128]{1,0:T(8,128)S(1)}, u32[]{:S(2)}, u32[]{:S(2)}) collective-permute-start(f32[512,128]{1,0:T(8,128)S(1)} %dynamic-slice_add_fusion.1), channel_id=1, source_target_pairs={{0,2},{1,3},{2,0},{3,1},{4,6},{5,7},{6,4},{7,5},{8,10},{9,11},{10,... | collective-permute-start | bytes 786440 | tf_op jit(solution)/shard_map/ppermute | solution.py:41
  29.2 11.4 %collective-permute-start.2 = (f32[512,128]{1,0:T(8,128)S(1)}, f32[512,128]{1,0:T(8,128)S(1)}, u32[]{:S(2)}, u32[]{:S(2)}) collective-permute-start(f32[512,128]{1,0:T(8,128)S(1)} %add.182), channel_id=1, source_target_pairs={{0,1},{1,0},{2,3},{3,2},{4,5},{5,4},{6,7},{7,6},{8,9},{9,8},{10,11... | collective-permute-start | bytes 786440 | tf_op jit(solution)/shard_map/ppermute | solution.py:41
  36.4 13.2 %collective-permute-start.40 = (f32[256,128]{0,1:T(8,128)S(1)}, f32[256,128]{0,1:T(8,128)S(1)}, u32[]{:S(2)}, u32[]{:S(2)}) collective-permute-start(f32[256,128]{0,1:T(8,128)S(1)} %get-tuple-element.26), channel_id=1, source_target_pairs={{0,4},{4,0},{8,12},{12,8},{16,20},{20,16},{24,28},{28,24},{1,5},{5... | collective-permute-start | bytes 393224 | tf_op jit(solution)/shard_map/ppermute | solution.py:35
  38.3 17.8 %collective-permute-start.39 = (f32[256,128]{0,1:T(8,128)S(1)}, f32[256,128]{0,1:T(8,128)S(1)}, u32[]{:S(2)}, u32[]{:S(2)}) collective-permute-start(f32[256,128]{0,1:T(8,128)S(1)} %get-tuple-element.27), channel_id=1, source_target_pairs={{0,4},{4,0},{8,12},{12,8},{16,20},{20,16},{24,28},{28,24},{1,5},{5... | collective-permute-start | bytes 393224 | tf_op jit(solution)/shard_map/ppermute | solution.py:35
  38.5 29.3 %collective-permute-start.38 = (f32[256,128]{0,1:T(8,128)S(1)}, f32[256,128]{0,1:T(8,128)S(1)}, u32[]{:S(2)}, u32[]{:S(2)}) collective-permute-start(f32[256,128]{0,1:T(8,128)S(1)} %get-tuple-element.28), channel_id=1, source_target_pairs={{0,4},{4,0},{8,12},{12,8},{16,20},{20,16},{24,28},{28,24},{1,5},{5... | collective-permute-start | bytes 393224 | tf_op jit(solution)/shard_map/ppermute | solution.py:35
  40.3 37.0 %collective-permute-start.37 = (f32[256,128]{0,1:T(8,128)S(1)}, f32[256,128]{0,1:T(8,128)S(1)}, u32[]{:S(2)}, u32[]{:S(2)}) collective-permute-start(f32[256,128]{0,1:T(8,128)S(1)} %get-tuple-element.25), channel_id=1, source_target_pairs={{0,4},{4,0},{8,12},{12,8},{16,20},{20,16},{24,28},{28,24},{1,5},{5... | collective-permute-start | bytes 393224 | tf_op jit(solution)/shard_map/ppermute | solution.py:35
  49.6 11.5 %collective-permute-start.5 = (f32[256,128]{0,1:T(8,128)S(1)}, f32[256,128]{0,1:T(8,128)S(1)}, u32[]{:S(2)}, u32[]{:S(2)}) collective-permute-start(f32[256,128]{0,1:T(8,128)S(1)} %get-tuple-element.23), channel_id=1, source_target_pairs={{0,4},{4,0},{8,12},{12,8},{16,20},{20,16},{24,28},{28,24},{1,5},{5... | collective-permute-start | bytes 393224 | tf_op jit(solution)/shard_map/ppermute | solution.py:35
  54.3 6.8 %collective-permute-start.41 = (f32[256,128]{0,1:T(8,128)S(1)}, f32[256,128]{0,1:T(8,128)S(1)}, u32[]{:S(2)}, u32[]{:S(2)}) collective-permute-start(f32[256,128]{0,1:T(8,128)S(1)} %bitcast_add_fusion.4), channel_id=1, source_target_pairs={{0,8},{4,12},{8,16},{12,20},{16,24},{20,28},{24,0},{28,4},{1,9},{5... | collective-permute-start | bytes 393224 | tf_op jit(solution)/shard_map/ppermute | solution.py:38
  56.1 18.6 %collective-permute-start.4 = (f32[256,128]{0,1:T(8,128)S(1)}, f32[256,128]{0,1:T(8,128)S(1)}, u32[]{:S(2)}, u32[]{:S(2)}) collective-permute-start(f32[256,128]{0,1:T(8,128)S(1)} %get-tuple-element.24), channel_id=1, source_target_pairs={{0,4},{4,0},{8,12},{12,8},{16,20},{20,16},{24,28},{28,24},{1,5},{5... | collective-permute-start | bytes 393224 | tf_op jit(solution)/shard_map/ppermute | solution.py:35
  61.1 20.5 %collective-permute-start.3 = (f32[256,128]{0,1:T(8,128)S(1)}, f32[256,128]{0,1:T(8,128)S(1)}, u32[]{:S(2)}, u32[]{:S(2)}) collective-permute-start(f32[256,128]{0,1:T(8,128)S(1)} %get-tuple-element.21), channel_id=1, source_target_pairs={{0,4},{4,0},{8,12},{12,8},{16,20},{20,16},{24,28},{28,24},{1,5},{5... | collective-permute-start | bytes 393224 | tf_op jit(solution)/shard_map/ppermute | solution.py:35
  67.9 9.3 %collective-permute-start.8 = (f32[256,128]{0,1:T(8,128)S(1)}, f32[256,128]{0,1:T(8,128)S(1)}, u32[]{:S(2)}, u32[]{:S(2)}) collective-permute-start(f32[256,128]{0,1:T(8,128)S(1)} %fusion.65), channel_id=1, source_target_pairs={{0,8},{4,12},{8,16},{12,20},{16,24},{20,28},{24,0},{28,4},{1,9},{5... | collective-permute-start | bytes 393224 | tf_op jit(solution)/shard_map/ppermute | solution.py:38
  74.6 6.8 %collective-permute-start.43 = (f32[256,128]{0,1:T(8,128)S(1)}, f32[256,128]{0,1:T(8,128)S(1)}, u32[]{:S(2)}, u32[]{:S(2)}) collective-permute-start(f32[256,128]{0,1:T(8,128)S(1)} %fusion.60), channel_id=1, source_target_pairs={{0,8},{4,12},{8,16},{12,20},{16,24},{20,28},{24,0},{28,4},{1,9},{5... | collective-permute-start | bytes 393224 | tf_op jit(solution)/shard_map/ppermute | solution.py:38
  77.2 8.2 %collective-permute-start.9 = (f32[256,128]{0,1:T(8,128)S(1)}, f32[256,128]{0,1:T(8,128)S(1)}, u32[]{:S(2)}, u32[]{:S(2)}) collective-permute-start(f32[256,128]{0,1:T(8,128)S(1)} %fusion.66), channel_id=1, source_target_pairs={{0,8},{4,12},{8,16},{12,20},{16,24},{20,28},{24,0},{28,4},{1,9},{5... | collective-permute-start | bytes 393224 | tf_op jit(solution)/shard_map/ppermute | solution.py:38
  81.6 6.8 %collective-permute-start.45 = (f32[256,128]{0,1:T(8,128)S(1)}, f32[256,128]{0,1:T(8,128)S(1)}, u32[]{:S(2)}, u32[]{:S(2)}) collective-permute-start(f32[256,128]{0,1:T(8,128)S(1)} %get-tuple-element.12), channel_id=1, source_target_pairs={{0,8},{4,12},{8,16},{12,20},{16,24},{20,28},{24,0},{28,4},{1,9},{5... | collective-permute-start | bytes 393224 | tf_op jit(solution)/shard_map/ppermute | solution.py:38
  85.6 8.1 %collective-permute-start.11 = (f32[256,128]{0,1:T(8,128)S(1)}, f32[256,128]{0,1:T(8,128)S(1)}, u32[]{:S(2)}, u32[]{:S(2)}) collective-permute-start(f32[256,128]{0,1:T(8,128)S(1)} %get-tuple-element.10), channel_id=1, source_target_pairs={{0,8},{4,12},{8,16},{12,20},{16,24},{20,28},{24,0},{28,4},{1,9},{5... | collective-permute-start | bytes 393224 | tf_op jit(solution)/shard_map/ppermute | solution.py:38
  85.6 9.4 %collective-permute-start.44 = (f32[256,128]{0,1:T(8,128)S(1)}, f32[256,128]{0,1:T(8,128)S(1)}, u32[]{:S(2)}, u32[]{:S(2)}) collective-permute-start(f32[256,128]{0,1:T(8,128)S(1)} %get-tuple-element.12), channel_id=1, source_target_pairs={{0,4},{4,0},{8,12},{12,8},{16,20},{20,16},{24,28},{28,24},{1,5},{5... | collective-permute-start | bytes 393224 | tf_op jit(solution)/shard_map/ppermute | solution.py:35
  87.7 7.4 %collective-permute-start.10 = (f32[256,128]{0,1:T(8,128)S(1)}, f32[256,128]{0,1:T(8,128)S(1)}, u32[]{:S(2)}, u32[]{:S(2)}) collective-permute-start(f32[256,128]{0,1:T(8,128)S(1)} %get-tuple-element.10), channel_id=1, source_target_pairs={{0,4},{4,0},{8,12},{12,8},{16,20},{20,16},{24,28},{28,24},{1,5},{5... | collective-permute-start | bytes 393224 | tf_op jit(solution)/shard_map/ppermute | solution.py:35
  88.4 14.8 %collective-permute-start.46 = (f32[256,128]{0,1:T(8,128)S(1)}, f32[256,128]{0,1:T(8,128)S(1)}, u32[]{:S(2)}, u32[]{:S(2)}) collective-permute-start(f32[256,128]{0,1:T(8,128)S(1)} %collective-permute-done.45), channel_id=1, source_target_pairs={{0,4},{4,0},{8,12},{12,8},{16,20},{20,16},{24,28},{28,24},{1,5},{5... | collective-permute-start | bytes 393224 | tf_op jit(solution)/shard_map/ppermute | solution.py:35
  90.2 7.5 %collective-permute-start.47 = (f32[256,128]{0,1:T(8,128)S(1)}, f32[256,128]{0,1:T(8,128)S(1)}, u32[]{:S(2)}, u32[]{:S(2)}) collective-permute-start(f32[256,128]{0,1:T(8,128)S(1)} %collective-permute-done.45), channel_id=1, source_target_pairs={{0,8},{4,12},{8,16},{12,20},{16,24},{20,28},{24,0},{28,4},{1,9},{5... | collective-permute-start | bytes 393224 | tf_op jit(solution)/shard_map/ppermute | solution.py:38
  93.7 9.8 %collective-permute-start.12 = (f32[256,128]{0,1:T(8,128)S(1)}, f32[256,128]{0,1:T(8,128)S(1)}, u32[]{:S(2)}, u32[]{:S(2)}) collective-permute-start(f32[256,128]{0,1:T(8,128)S(1)} %collective-permute-done.11), channel_id=1, source_target_pairs={{0,4},{4,0},{8,12},{12,8},{16,20},{20,16},{24,28},{28,24},{1,5},{5... | collective-permute-start | bytes 393224 | tf_op jit(solution)/shard_map/ppermute | solution.py:35
  97.7 13.1 %collective-permute-start.48 = (f32[256,128]{0,1:T(8,128)S(1)}, f32[256,128]{0,1:T(8,128)S(1)}, u32[]{:S(2)}, u32[]{:S(2)}) collective-permute-start(f32[256,128]{0,1:T(8,128)S(1)} %collective-permute-done.47), channel_id=1, source_target_pairs={{0,4},{4,0},{8,12},{12,8},{16,20},{20,16},{24,28},{28,24},{1,5},{5... | collective-permute-start | bytes 393224 | tf_op jit(solution)/shard_map/ppermute | solution.py:35
  101.8 9.0 %collective-permute-start.14 = (f32[256,128]{0,1:T(8,128)S(1)}, f32[256,128]{0,1:T(8,128)S(1)}, u32[]{:S(2)}, u32[]{:S(2)}) collective-permute-start(f32[256,128]{0,1:T(8,128)S(1)} %collective-permute-done.13), channel_id=1, source_target_pairs={{0,4},{4,0},{8,12},{12,8},{16,20},{20,16},{24,28},{28,24},{1,5},{5... | collective-permute-start | bytes 393224 | tf_op jit(solution)/shard_map/ppermute | solution.py:35
  103.2 7.0 %collective-permute-start.15 = (f32[256,128]{0,1:T(8,128)S(1)}, f32[256,128]{0,1:T(8,128)S(1)}, u32[]{:S(2)}, u32[]{:S(2)}) collective-permute-start(f32[256,128]{0,1:T(8,128)S(1)} %collective-permute-done.13), channel_id=1, source_target_pairs={{0,8},{4,12},{8,16},{12,20},{16,24},{20,28},{24,0},{28,4},{1,9},{5... | collective-permute-start | bytes 393224 | tf_op jit(solution)/shard_map/ppermute | solution.py:38
  104.4 19.4 %collective-permute-start.50 = (f32[256,128]{0,1:T(8,128)S(1)}, f32[256,128]{0,1:T(8,128)S(1)}, u32[]{:S(2)}, u32[]{:S(2)}) collective-permute-start(f32[256,128]{0,1:T(8,128)S(1)} %collective-permute-done.49), channel_id=1, source_target_pairs={{0,4},{4,0},{8,12},{12,8},{16,20},{20,16},{24,28},{28,24},{1,5},{5... | collective-permute-start | bytes 393224 | tf_op jit(solution)/shard_map/ppermute | solution.py:35
  131.1 7.3 %collective-permute-start.17 = (f32[520,128]{1,0:T(8,128)S(1)}, f32[520,128]{1,0:T(8,128)S(1)}, u32[]{:S(2)}, u32[]{:S(2)}) collective-permute-start(f32[520,128]{1,0:T(8,128)S(1)} %pad_dynamic-slice_fusion.2), channel_id=1, source_target_pairs={{0,1},{1,0},{2,3},{3,2},{4,5},{5,4},{6,7},{7,6},{8,9},{9,8},{10,11... | collective-permute-start | bytes 798728 | tf_op jit(solution)/shard_map/ppermute | solution.py:41
  139.0 9.3 %collective-permute-start.18 = (f32[520,128]{1,0:T(8,128)S(1)}, f32[520,128]{1,0:T(8,128)S(1)}, u32[]{:S(2)}, u32[]{:S(2)}) collective-permute-start(f32[520,128]{1,0:T(8,128)S(1)} %fusion.20), channel_id=1, source_target_pairs={{0,2},{1,3},{2,0},{3,1},{4,6},{5,7},{6,4},{7,5},{8,10},{9,11},{10,... | collective-permute-start | bytes 798728 | tf_op jit(solution)/shard_map/ppermute | solution.py:41
  141.3 12.3 %collective-permute-start.52 = (f32[520,128]{1,0:T(8,128)S(1)}, f32[520,128]{1,0:T(8,128)S(1)}, u32[]{:S(2)}, u32[]{:S(2)}) collective-permute-start(f32[520,128]{1,0:T(8,128)S(1)} %fusion.21), channel_id=1, source_target_pairs={{0,2},{1,3},{2,0},{3,1},{4,6},{5,7},{6,4},{7,5},{8,10},{9,11},{10,... | collective-permute-start | bytes 798728 | tf_op jit(solution)/shard_map/ppermute | solution.py:41
  166.7 9.5 %collective-permute-start.57 = (f32[256,128]{0,1:T(8,128)S(1)}, f32[256,128]{0,1:T(8,128)S(1)}, u32[]{:S(2)}, u32[]{:S(2)}) collective-permute-start(f32[256,128]{0,1:T(8,128)S(1)} %get-tuple-element.18), channel_id=1, source_target_pairs={{0,4},{4,0},{8,12},{12,8},{16,20},{20,16},{24,28},{28,24},{1,5},{5... | collective-permute-start | bytes 393224 | tf_op jit(solution)/shard_map/ppermute | solution.py:35
  167.4 16.9 %collective-permute-start.56 = (f32[256,128]{0,1:T(8,128)S(1)}, f32[256,128]{0,1:T(8,128)S(1)}, u32[]{:S(2)}, u32[]{:S(2)}) collective-permute-start(f32[256,128]{0,1:T(8,128)S(1)} %get-tuple-element.19), channel_id=1, source_target_pairs={{0,4},{4,0},{8,12},{12,8},{16,20},{20,16},{24,28},{28,24},{1,5},{5... | collective-permute-start | bytes 393224 | tf_op jit(solution)/shard_map/ppermute | solution.py:35
  168.8 29.1 %collective-permute-start.55 = (f32[256,128]{0,1:T(8,128)S(1)}, f32[256,128]{0,1:T(8,128)S(1)}, u32[]{:S(2)}, u32[]{:S(2)}) collective-permute-start(f32[256,128]{0,1:T(8,128)S(1)} %get-tuple-element.20), channel_id=1, source_target_pairs={{0,4},{4,0},{8,12},{12,8},{16,20},{20,16},{24,28},{28,24},{1,5},{5... | collective-permute-start | bytes 393224 | tf_op jit(solution)/shard_map/ppermute | solution.py:35
  169.4 37.6 %collective-permute-start.54 = (f32[256,128]{0,1:T(8,128)S(1)}, f32[256,128]{0,1:T(8,128)S(1)}, u32[]{:S(2)}, u32[]{:S(2)}) collective-permute-start(f32[256,128]{0,1:T(8,128)S(1)} %get-tuple-element.17), channel_id=1, source_target_pairs={{0,4},{4,0},{8,12},{12,8},{16,20},{20,16},{24,28},{28,24},{1,5},{5... | collective-permute-start | bytes 393224 | tf_op jit(solution)/shard_map/ppermute | solution.py:35
  175.5 8.8 %collective-permute-start.23 = (f32[256,128]{0,1:T(8,128)S(1)}, f32[256,128]{0,1:T(8,128)S(1)}, u32[]{:S(2)}, u32[]{:S(2)}) collective-permute-start(f32[256,128]{0,1:T(8,128)S(1)} %get-tuple-element.14), channel_id=1, source_target_pairs={{0,4},{4,0},{8,12},{12,8},{16,20},{20,16},{24,28},{28,24},{1,5},{5... | collective-permute-start | bytes 393224 | tf_op jit(solution)/shard_map/ppermute | solution.py:35
  176.2 14.9 %collective-permute-start.22 = (f32[256,128]{0,1:T(8,128)S(1)}, f32[256,128]{0,1:T(8,128)S(1)}, u32[]{:S(2)}, u32[]{:S(2)}) collective-permute-start(f32[256,128]{0,1:T(8,128)S(1)} %get-tuple-element.15), channel_id=1, source_target_pairs={{0,4},{4,0},{8,12},{12,8},{16,20},{20,16},{24,28},{28,24},{1,5},{5... | collective-permute-start | bytes 393224 | tf_op jit(solution)/shard_map/ppermute | solution.py:35
  184.3 20.4 %collective-permute-start.21 = (f32[256,128]{0,1:T(8,128)S(1)}, f32[256,128]{0,1:T(8,128)S(1)}, u32[]{:S(2)}, u32[]{:S(2)}) collective-permute-start(f32[256,128]{0,1:T(8,128)S(1)} %get-tuple-element.16), channel_id=1, source_target_pairs={{0,4},{4,0},{8,12},{12,8},{16,20},{20,16},{24,28},{28,24},{1,5},{5... | collective-permute-start | bytes 393224 | tf_op jit(solution)/shard_map/ppermute | solution.py:35
  191.1 21.2 %collective-permute-start.20 = (f32[256,128]{0,1:T(8,128)S(1)}, f32[256,128]{0,1:T(8,128)S(1)}, u32[]{:S(2)}, u32[]{:S(2)}) collective-permute-start(f32[256,128]{0,1:T(8,128)S(1)} %get-tuple-element.13), channel_id=1, source_target_pairs={{0,4},{4,0},{8,12},{12,8},{16,20},{20,16},{24,28},{28,24},{1,5},{5... | collective-permute-start | bytes 393224 | tf_op jit(solution)/shard_map/ppermute | solution.py:35
  197.8 9.1 %collective-permute-start.25 = (f32[256,128]{0,1:T(8,128)S(1)}, f32[256,128]{0,1:T(8,128)S(1)}, u32[]{:S(2)}, u32[]{:S(2)}) collective-permute-start(f32[256,128]{0,1:T(8,128)S(1)} %fusion.62), channel_id=1, source_target_pairs={{0,8},{4,12},{8,16},{12,20},{16,24},{20,28},{24,0},{28,4},{1,9},{5... | collective-permute-start | bytes 393224 | tf_op jit(solution)/shard_map/ppermute | solution.py:38
  204.6 6.8 %collective-permute-start.60 = (f32[256,128]{0,1:T(8,128)S(1)}, f32[256,128]{0,1:T(8,128)S(1)}, u32[]{:S(2)}, u32[]{:S(2)}) collective-permute-start(f32[256,128]{0,1:T(8,128)S(1)} %fusion.57), channel_id=1, source_target_pairs={{0,8},{4,12},{8,16},{12,20},{16,24},{20,28},{24,0},{28,4},{1,9},{5... | collective-permute-start | bytes 393224 | tf_op jit(solution)/shard_map/ppermute | solution.py:38
  207.0 8.2 %collective-permute-start.26 = (f32[256,128]{0,1:T(8,128)S(1)}, f32[256,128]{0,1:T(8,128)S(1)}, u32[]{:S(2)}, u32[]{:S(2)}) collective-permute-start(f32[256,128]{0,1:T(8,128)S(1)} %fusion.63), channel_id=1, source_target_pairs={{0,8},{4,12},{8,16},{12,20},{16,24},{20,28},{24,0},{28,4},{1,9},{5... | collective-permute-start | bytes 393224 | tf_op jit(solution)/shard_map/ppermute | solution.py:38
  211.6 12.3 %collective-permute-start.61 = (f32[256,128]{0,1:T(8,128)S(1)}, f32[256,128]{0,1:T(8,128)S(1)}, u32[]{:S(2)}, u32[]{:S(2)}) collective-permute-start(f32[256,128]{0,1:T(8,128)S(1)} %get-tuple-element.8), channel_id=1, source_target_pairs={{0,4},{4,0},{8,12},{12,8},{16,20},{20,16},{24,28},{28,24},{1,5},{5... | collective-permute-start | bytes 393224 | tf_op jit(solution)/shard_map/ppermute | solution.py:35
  215.4 8.2 %collective-permute-start.28 = (f32[256,128]{0,1:T(8,128)S(1)}, f32[256,128]{0,1:T(8,128)S(1)}, u32[]{:S(2)}, u32[]{:S(2)}) collective-permute-start(f32[256,128]{0,1:T(8,128)S(1)} %get-tuple-element.6), channel_id=1, source_target_pairs={{0,8},{4,12},{8,16},{12,20},{16,24},{20,28},{24,0},{28,4},{1,9},{5... | collective-permute-start | bytes 393224 | tf_op jit(solution)/shard_map/ppermute | solution.py:38
  215.7 8.2 %collective-permute-start.27 = (f32[256,128]{0,1:T(8,128)S(1)}, f32[256,128]{0,1:T(8,128)S(1)}, u32[]{:S(2)}, u32[]{:S(2)}) collective-permute-start(f32[256,128]{0,1:T(8,128)S(1)} %get-tuple-element.6), channel_id=1, source_target_pairs={{0,4},{4,0},{8,12},{12,8},{16,20},{20,16},{24,28},{28,24},{1,5},{5... | collective-permute-start | bytes 393224 | tf_op jit(solution)/shard_map/ppermute | solution.py:35
  219.1 13.9 %collective-permute-start.63 = (f32[256,128]{0,1:T(8,128)S(1)}, f32[256,128]{0,1:T(8,128)S(1)}, u32[]{:S(2)}, u32[]{:S(2)}) collective-permute-start(f32[256,128]{0,1:T(8,128)S(1)} %collective-permute-done.62), channel_id=1, source_target_pairs={{0,4},{4,0},{8,12},{12,8},{16,20},{20,16},{24,28},{28,24},{1,5},{5... | collective-permute-start | bytes 393224 | tf_op jit(solution)/shard_map/ppermute | solution.py:35
  223.6 9.6 %collective-permute-start.29 = (f32[256,128]{0,1:T(8,128)S(1)}, f32[256,128]{0,1:T(8,128)S(1)}, u32[]{:S(2)}, u32[]{:S(2)}) collective-permute-start(f32[256,128]{0,1:T(8,128)S(1)} %collective-permute-done.28), channel_id=1, source_target_pairs={{0,4},{4,0},{8,12},{12,8},{16,20},{20,16},{24,28},{28,24},{1,5},{5... | collective-permute-start | bytes 393224 | tf_op jit(solution)/shard_map/ppermute | solution.py:35
  223.8 8.2 %collective-permute-start.30 = (f32[256,128]{0,1:T(8,128)S(1)}, f32[256,128]{0,1:T(8,128)S(1)}, u32[]{:S(2)}, u32[]{:S(2)}) collective-permute-start(f32[256,128]{0,1:T(8,128)S(1)} %collective-permute-done.28), channel_id=1, source_target_pairs={{0,8},{4,12},{8,16},{12,20},{16,24},{20,28},{24,0},{28,4},{1,9},{5... | collective-permute-start | bytes 393224 | tf_op jit(solution)/shard_map/ppermute | solution.py:38
  227.2 13.8 %collective-permute-start.65 = (f32[256,128]{0,1:T(8,128)S(1)}, f32[256,128]{0,1:T(8,128)S(1)}, u32[]{:S(2)}, u32[]{:S(2)}) collective-permute-start(f32[256,128]{0,1:T(8,128)S(1)} %collective-permute-done.64), channel_id=1, source_target_pairs={{0,4},{4,0},{8,12},{12,8},{16,20},{20,16},{24,28},{28,24},{1,5},{5... | collective-permute-start | bytes 393224 | tf_op jit(solution)/shard_map/ppermute | solution.py:35
  232.0 9.0 %collective-permute-start.31 = (f32[256,128]{0,1:T(8,128)S(1)}, f32[256,128]{0,1:T(8,128)S(1)}, u32[]{:S(2)}, u32[]{:S(2)}) collective-permute-start(f32[256,128]{0,1:T(8,128)S(1)} %collective-permute-done.30), channel_id=1, source_target_pairs={{0,4},{4,0},{8,12},{12,8},{16,20},{20,16},{24,28},{28,24},{1,5},{5... | collective-permute-start | bytes 393224 | tf_op jit(solution)/shard_map/ppermute | solution.py:35
  232.9 6.9 %collective-permute-start.32 = (f32[256,128]{0,1:T(8,128)S(1)}, f32[256,128]{0,1:T(8,128)S(1)}, u32[]{:S(2)}, u32[]{:S(2)}) collective-permute-start(f32[256,128]{0,1:T(8,128)S(1)} %collective-permute-done.30), channel_id=1, source_target_pairs={{0,8},{4,12},{8,16},{12,20},{16,24},{20,28},{24,0},{28,4},{1,9},{5... | collective-permute-start | bytes 393224 | tf_op jit(solution)/shard_map/ppermute | solution.py:38
  (32 other events, 240.0 us)

commit v2 on v1

v2 whole, which is shorter than its diff:
```python
import functools
import math

import jax
import jax.numpy as jnp
from jax import lax
from jax.experimental import pallas as pl
from jax.experimental.pallas import tpu as pltpu
from jax.sharding import PartitionSpec as P

ITERS = 2
NS_STEPS = 5
GROUPS = 2
EXTRA = 8
ROW_BLOCKS = 8
WHOLE = pl.BlockSpec(memory_space=pltpu.VMEM)
F32 = jnp.float32
BF16 = jnp.bfloat16


def split(value):
    high = value.astype(BF16)
    return high, (value - high.astype(F32)).astype(BF16)


def dot(left, right):
    return jnp.dot(left, right, preferred_element_type=F32)


def product(left, right):
    left_high, left_low = split(left)
    right_high, right_low = split(right)
    return dot(left_high, right_high) + (dot(left_high, right_low) + dot(left_low, right_high))


def wide_product(left, pair, width):
    high, low = split(left)
    both = dot(high, pair)
    return both[:, :width] + (both[:, width:] + dot(low, pair[:, :width]))


def params(mib):
    return pltpu.CompilerParams(vmem_limit_bytes=mib * 2**20)


def cost(flops, moved):
    return pl.CostEstimate(flops=int(flops), bytes_accessed=int(moved), transcendentals=0)


def coef_kernel(blocks, groups, squares, where, half, a_ref, *refs):
    step = pl.program_id(0)
    inputs, outputs, (pair, sums) = refs[:blocks], refs[blocks:-2], refs[-2:]
    rows, columns = inputs[0].shape

    @pl.when(step == 0)
    def _():
        for k in range(blocks):
            value = inputs[k][...]
            high, low = split(value)
            at = pl.ds(pl.multiple_of(where[k] * rows, rows), rows)
            pair[at, :columns] = high
            pair[at, columns:] = low
            if squares:
                sums[pl.ds(where[k], 1), :] = jnp.sum(value * value, axis=0, keepdims=True)
        if squares:
            total = jnp.sum(sums[...], axis=0, keepdims=True)
            total = jnp.sum(total, axis=1, keepdims=True)
            for out in outputs:
                out[out.shape[0] - EXTRA :, :] = jnp.broadcast_to(total, (EXTRA, out.shape[1]))

    result = wide_product(a_ref[...], pair[...], columns)
    tall = result.shape[0]
    each = columns // groups
    steps = pl.num_programs(0) // 2
    at = pl.ds(pl.multiple_of(lax.rem(step, steps) * tall, tall), tall)

    @pl.when(step < steps)
    def _():
        for g in range(groups):
            outputs[2 * g][at, :] = result[:, g * each : (g + 1) * each]

    @pl.when(step >= steps)
    def _():
        for g in range(groups):
            outputs[2 * g + 1][at, :] = result[:, g * each : (g + 1) * each]


def coef_terms(a_rows, basis, where, half, groups, squares):
    total, depth = a_rows.shape
    tall = total // ROW_BLOCKS
    steps = ROW_BLOCKS // 2
    columns = basis[0].shape[1]
    out_rows = total // 2 + (EXTRA if squares else 0)
    kernel = functools.partial(coef_kernel, len(basis), groups, squares)

    def a_place(step, where, half):
        return (lax.rem(step + (1 - half[0]) * steps, ROW_BLOCKS), 0)

    whole = lambda array: pl.BlockSpec(array.shape, lambda step, where, half: (0, 0))
    outs = [jax.ShapeDtypeStruct((out_rows, columns // groups), F32)] * (2 * groups)
    return pl.pallas_call(
        kernel,
        grid_spec=pltpu.PrefetchScalarGridSpec(
            num_scalar_prefetch=2,
            grid=(ROW_BLOCKS,),
            in_specs=[pl.BlockSpec((tall, depth), a_place)] + [whole(b) for b in basis],
            out_specs=[whole(out) for out in outs],
            scratch_shapes=[
                pltpu.VMEM((depth, 2 * columns), BF16),
                pltpu.VMEM((max(len(basis), 8), columns), F32),
            ],
        ),
        out_shape=outs,
        compiler_params=params(32),
        cost_estimate=cost(8 * total * depth * columns, 4 * total * depth),
        name="coef",
    )(where, half, a_rows, *basis)


def panel_kernel(squares, where, half, ranks, b_ref, mine_ref, partner_ref, *refs):
    step = pl.program_id(0)
    pair = refs[-1]
    clients, slots, width = pair.shape
    columns = width // 2

    @pl.when(step == 0)
    def _():
        scale = jnp.ones((1, columns), F32)
        if squares:
            square = mine_ref[mine_ref.shape[0] - EXTRA : mine_ref.shape[0] - EXTRA + 1, :]
            scale = jnp.where(square > 0, lax.rsqrt(square), 1.0)
            refs[-2][...] = jnp.broadcast_to(scale, refs[-2].shape)
        first = half[0] == 0
        for c in range(clients):
            at = pl.ds((c % (clients // 2)) * slots, slots)
            mine, partner = mine_ref[at, :], partner_ref[at, :]
            value = jnp.where(first, mine, partner) if c < clients // 2 else jnp.where(first, partner, mine)
            slot = lax.broadcasted_iota(jnp.int32, value.shape, 0)
            value = jnp.where(slot < ranks[c], value * scale, 0.0)
            high, low = split(value)
            pair[c, :, :columns] = high
            pair[c, :, columns:] = low

    total = wide_product(b_ref[0], pair[0], columns)
    for c in range(1, clients):
        total = total + wide_product(b_ref[c], pair[c], columns)
    for k in range(pl.num_programs(0)):

        @pl.when(step == k)
        def _():
            refs[k][...] = total


def panel_terms(b_factors, mine, partner, where, half, ranks, blocks, squares):
    clients, rows, slots = b_factors.shape
    columns = mine.shape[1]
    tall = rows // blocks
    outs = [jax.ShapeDtypeStruct((tall, columns), F32)] * blocks
    if squares:
        outs = outs + [jax.ShapeDtypeStruct((EXTRA, columns), F32)]
    whole = lambda array: pl.BlockSpec(array.shape, lambda step, where, half, ranks: (0, 0))
    return pl.pallas_call(
        functools.partial(panel_kernel, squares),
        grid_spec=pltpu.PrefetchScalarGridSpec(
            num_scalar_prefetch=3,
            grid=(blocks,),
            in_specs=[
                pl.BlockSpec((clients, tall, slots), lambda step, where, half, ranks: (0, where[step], 0)),
                whole(mine),
                whole(partner),
            ],
            out_specs=[whole(out) for out in outs],
            scratch_shapes=[pltpu.VMEM((clients, slots, 2 * columns), BF16)],
        ),
        out_shape=outs,
        compiler_params=params(32),
        cost_estimate=cost(8 * clients * slots * rows * columns, 4 * clients * slots * rows),
        name="panel",
    )(where, half, ranks, b_factors, mine, partner)


def gram_kernel(blocks, where, half, *refs):
    inputs, (other, mine), (highs, lows) = refs[: GROUPS * blocks], refs[-4:-2], refs[-2:]
    rows, columns = inputs[0].shape
    for g in range(GROUPS):
        for k in range(blocks):
            high, low = split(inputs[g * blocks + k][...])
            at = pl.ds(pl.multiple_of(where[k] * rows, rows), rows)
            highs[at, g * columns : (g + 1) * columns] = high
            lows[at, g * columns : (g + 1) * columns] = low
    contract = (((0,), (0,)), ((), ()))
    high = highs[...]
    cross = lax.dot_general(high, lows[...], contract, preferred_element_type=F32)
    gram = lax.dot_general(high, high, contract, preferred_element_type=F32) + (cross + cross.T)
    tall = other.shape[0]
    first = half[0] == 0
    other[...] = jnp.where(first, gram[tall:], gram[:tall])
    mine[...] = jnp.where(first, gram[:tall], gram[tall:])


def gram_terms(panels, where, half):
    blocks = len(panels[0])
    rows, columns = panels[0][0].shape
    size = GROUPS * columns
    smem = pl.BlockSpec(memory_space=pltpu.SMEM)
    return pl.pallas_call(
        functools.partial(gram_kernel, blocks),
        in_specs=[smem, smem] + [WHOLE] * (GROUPS * blocks),
        out_specs=[WHOLE] * 2,
        out_shape=[jax.ShapeDtypeStruct((size // 2, size), F32)] * 2,
        scratch_shapes=[pltpu.VMEM((blocks * rows, size), BF16)] * 2,
        compiler_params=params(32),
        cost_estimate=cost(4 * blocks * rows * size * size, 4 * blocks * rows * size),
        name="gram",
    )(where, half, *[block for panel in panels for block in panel])


def iterate(gram):
    size = gram.shape[0]
    row = lax.broadcasted_iota(jnp.int32, gram.shape, 0)
    column = lax.broadcasted_iota(jnp.int32, gram.shape, 1)
    eye = jnp.where(row == column, 1.0, 0.0).astype(F32)
    trace = jnp.sum(jnp.sum(gram * eye, axis=0, keepdims=True), axis=1, keepdims=True)
    scale = lax.rsqrt(trace)
    inner = gram * scale * scale
    mixing = None
    for turn in range(NS_STEPS):
        factor = 1.5 * eye - 0.5 * inner
        mixing = product(mixing, factor) if turn else factor * scale
        if turn < NS_STEPS - 1:
            inner = product(product(inner, factor), factor)
    return mixing


def joined(half, mine, partner):
    first = half[0] == 0
    low = jnp.where(first, mine[...], partner[...])
    high = jnp.where(first, partner[...], mine[...])
    return jnp.concatenate([low, high], axis=0)


def first_kernel(half, mine, partner, out):
    out[...] = iterate(joined(half, mine, partner))


def next_kernel(factor, half, mine, partner, before, *refs):
    scales, out = refs[:-1], refs[-1]
    columns = scales[0].shape[1]
    mixing = jnp.concatenate(
        [before[g * columns : (g + 1) * columns, :] / scales[g][0:1, 0:1] for g in range(GROUPS)], axis=0
    )
    gram = joined(half, mine, partner)
    out[...] = product(mixing, iterate(product(mixing.T, product(gram, mixing)))) * factor


def mixing_of(half, mine, partner, before=None, scales=(), factor=1.0):
    size = mine.shape[1]
    smem = pl.BlockSpec(memory_space=pltpu.SMEM)
    operands = (half, mine, partner) + (() if before is None else (before,) + tuple(scales))
    return pl.pallas_call(
        first_kernel if before is None else functools.partial(next_kernel, factor),
        in_specs=[smem] + [WHOLE] * (len(operands) - 1),
        out_specs=WHOLE,
        out_shape=jax.ShapeDtypeStruct((size, size), F32),
        compiler_params=params(32),
        cost_estimate=cost(90 * size**3, 12 * size * size),
        name="mixing",
    )(*operands)


def apply_kernel(blocks, where, mixing, *refs):
    inputs, (out,) = refs[: GROUPS * blocks], refs[GROUPS * blocks :]
    rows, columns = inputs[0].shape
    high, low = split(mixing[...])
    for k in range(blocks):
        value = jnp.concatenate([inputs[g * blocks + k][...] for g in range(GROUPS)], axis=1)
        value_high, value_low = split(value)
        at = pl.ds(pl.multiple_of(where[k] * rows, rows), rows)
        out[at, :] = dot(value_high, high) + (dot(value_high, low) + dot(value_low, high))


def apply_mixing(panels, where, mixing):
    blocks = len(panels[0])
    rows, columns = panels[0][0].shape
    size = GROUPS * columns
    smem = pl.BlockSpec(memory_space=pltpu.SMEM)
    return pl.pallas_call(
        functools.partial(apply_kernel, blocks),
        in_specs=[smem] + [WHOLE] * (1 + GROUPS * blocks),
        out_specs=WHOLE,
        out_shape=jax.ShapeDtypeStruct((blocks * rows, size), F32),
        compiler_params=params(32),
        cost_estimate=cost(6 * blocks * rows * size * size, 8 * blocks * rows * size),
        name="apply",
    )(where, mixing, *[block for panel in panels for block in panel])


class Grid:
    def __init__(self, mesh):
        self.cohorts = mesh.shape["cohort"]
        self.feats = mesh.shape["feat"]
        self.places = self.cohorts // 2
        cohort = lax.axis_index("cohort")
        place, side = cohort // 2, cohort % 2
        self.half = (lax.axis_index("feat") % 2).astype(jnp.int32).reshape(1)

        def block(step, side):
            return lax.rem(place - step + self.places, self.places) * 2 + side

        steps = range(self.places)
        self.scatter_order = jnp.stack([block(s + 1, i) for s in steps for i in (1 - side, side)]).astype(jnp.int32)
        self.gather_order = jnp.stack([block(s, i) for s in steps for i in (side, 1 - side)]).astype(jnp.int32)

    def across(self, block):
        return lax.ppermute(block, "cohort", [(i, i ^ 1) for i in range(self.cohorts)])

    def along(self, block):
        return lax.ppermute(block, "cohort", [(i, (i + 2) % self.cohorts) for i in range(self.cohorts)])

    def feat_swap(self, block, bit):
        return lax.ppermute(block, "feat", [(i, i ^ bit) for i in range(self.feats)])

    def feat_sum(self, other, mine):
        total = mine + self.feat_swap(other, 1)
        bit = 2
        while bit < self.feats:
            total = total + self.feat_swap(total, bit)
            bit *= 2
        return total, self.feat_swap(total, 1)

    def scatter_sum(self, blocks):
        total, arrived = None, []
        for step in range(self.places):
            send, keep = blocks[2 * step], blocks[2 * step + 1]
            if step > 1:
                send, arrived[step - 2] = lax.optimization_barrier((send, arrived[step - 2]))
            arrived.append(self.across(send))
        for step in range(self.places):
            fresh = arrived[step] + blocks[2 * step + 1]
            total = fresh if total is None else fresh + self.along(total)
        return total

    def gather(self, block):
        blocks = []
        for step in range(self.places):
            blocks += [block, self.across(block)]
            if step < self.places - 1:
                block = self.along(block)
        return blocks


def solution(mesh):
    def on_device(b_factors, a_factors, ranks, probes):
        grid = Grid(mesh)
        clients, rows, slots = b_factors.shape
        a_rows = a_factors.reshape(clients * slots, rows)
        origin = jnp.zeros((1,), jnp.int32)
        mixing = None
        for turn in range(ITERS):
            squares = turn > 0
            if turn == 0:
                halves = coef_terms(a_rows, [probes], origin, grid.half, GROUPS, squares)
                halves = [halves[2 * g : 2 * g + 2] for g in range(GROUPS)]
            panels, scales = [], []
            for g in range(GROUPS):
                if turn > 0:
                    halves[g] = coef_terms(a_rows, before[g], grid.gather_order, grid.half, 1, squares)
                mine, partner = grid.feat_sum(*halves[g])
                terms = panel_terms(
                    b_factors, mine, partner, grid.scatter_order, grid.half, ranks, grid.cohorts, squares
                )
                scales += terms[grid.cohorts :]
                panels.append(grid.gather(grid.scatter_sum(terms[: grid.cohorts])))
            gram = grid.feat_sum(*gram_terms(panels, grid.gather_order, grid.half))
            if turn == 0:
                mixing = mixing_of(grid.half, *gram)
            else:
                last = turn == ITERS - 1
                factor = math.sqrt(rows * grid.feats) if last else 1.0
                mixing = mixing_of(grid.half, *gram, mixing, scales, factor)
            before = panels
        return apply_mixing(panels, grid.gather_order, mixing)

    in_specs = (P("cohort", "feat", None), P("cohort", None, "feat"), P("cohort"), P("feat", None))
    return jax.shard_map(on_device, mesh=mesh, in_specs=in_specs, out_specs=P("feat", None), check_vma=False)
```

time: 267 us -> 229 us (0.86); the launches traced: 264 us -> 229 us
  matrix products: 65.3 us -> 0 us
  Pallas kernels: 0 us -> 48.6 us
  waiting for transfers between devices: 135 us -> 119 us
  local copies, waits for them, and re-layouts: 4.51 us -> 11.9 us
  other arithmetic: 6.32 us -> 0.68 us
  between operations: 5.71 us -> 0.6 us
    dot_general x38 -> x0, matrix products: 65.3 us -> none  [the longest x4 26.9 us: panel_terms(): jnp.einsum('cdr,crp->dp', b_factors, coef, precision=lax.Precision.HIGH,...]
    pallas_call x0 -> x12, Pallas kernels: none -> 48.6 us  [the longest x4 20.6 us: panel_terms(): pl.pallas_call(functools.partial(panel_kernel, squares), grid_spec=pltpu....]
    ppermute x24, waiting for transfers between devices: 87.3 us -> 61.6 us  [along(): lax.ppermute(block, 'cohort', [(i, (i + 2) % self.cohorts) for i in range...]
    unnamed x14, local copies, waits for them, and re-layouts: 0.05 us -> 11.7 us
    ppermute x32, waiting for transfers between devices: 19.1 us -> 27.6 us  [across(): lax.ppermute(block, 'cohort', [(i, i ^ 1) for i in range(self.cohorts)])]
    ppermute x24, starting transfers between devices: 3.11 us -> 9.01 us  [along(): lax.ppermute(block, 'cohort', [(i, (i + 2) % self.cohorts) for i in range...]
    ppermute x32, starting transfers between devices: 33.4 us -> 28.4 us  [across(): lax.ppermute(block, 'cohort', [(i, i ^ 1) for i in range(self.cohorts)])]
  transfers between devices with their start and end apart: 74 -> 74, of which waited for: 36 -> 39; matrix products, arithmetic and copies ran while one was open for 17% -> 0% of each run, Pallas kernels for 0% -> 16%
where the time goes in v2:
time: 229 us
  waiting for transfers between devices  119 us (52%)
  Pallas kernels  48.6 us (21%)
  starting transfers between devices  48 us (21%)
  local copies, waits for them, and re-layouts  11.9 us (5%)
    ppermute x24, waiting for transfers between devices, along(): lax.ppermute(block, 'cohort', [(i, (i + 2) % self.cohorts) for i in range...  61.6 us
    ppermute x18, waiting for transfers between devices, feat_swap(): lax.ppermute(block, 'feat', [(i, i ^ bit) for i in range(self.feats)])  29.9 us
    ppermute x32, starting transfers between devices, across(): lax.ppermute(block, 'cohort', [(i, i ^ 1) for i in range(self.cohorts)])  28.4 us
    ppermute x32, waiting for transfers between devices, across(): lax.ppermute(block, 'cohort', [(i, i ^ 1) for i in range(self.cohorts)])  27.6 us
    pallas_call x4, Pallas kernels, panel_terms(): pl.pallas_call(functools.partial(panel_kernel, squares), grid_spec=pltpu....  20.6 us
    pallas_call x3, Pallas kernels, coef_terms(): pl.pallas_call(kernel, grid_spec=pltpu.PrefetchScalarGridSpec(num_scalar_...  14.8 us
    unnamed x14, local copies, waits for them, and re-layouts  11.7 us
    ppermute x18, starting transfers between devices, feat_swap(): lax.ppermute(block, 'feat', [(i, i ^ bit) for i in range(self.feats)])  10.6 us
  transfers between devices with their start and end apart: 74, of which 39 were waited for; matrix products, arithmetic and copies ran while one was open for 0% of the time, Pallas kernels for 16%

profile of v2, /device:TPU:0, one launch (start us, length us, event | category | flops | bytes accessed | tf_op | source)
XLA Modules:
  0.0 228.9 jit_solution(13959073782142018996)
XLA Ops:
  0.0 3.4 %copy-done.1 = f32[4,256,2048]{2,1,0:T(8,128)S(1)} copy-done((f32[4,256,2048]{2,1,0:T(8,128)S(1)}, f32[4,256,2048]{2,1,0:T(8,128)}, u32[]{:S(2)}) %copy-start.1) | copy-done | bytes 8388632
  5.0 5.4 %coef.3 = (f32[512,128]{1,0:T(8,128)S(1)}, f32[512,128]{1,0:T(8,128)S(1)}, f32[512,128]{1,0:T(8,128)S(1)}, f32[512,128]{1,0:T(8,128)S(1)}) custom-call(s32[1]{0:T(128)} %constant.61.clone.1.where, s32[1]{0:T(128)} %bitcast.8.half, f32[1024,2048]{1,0:T(8,128)S(1)} %bitcast.14, f32[2048,256]{1,0:T(8,128)S(1)} %copy-done.4), custom_call_target="tpu_custom_call" | custom-call | flops 4294967296 | bytes 8388608 | tf_op jit(solution)/shard_map/coef/pallas_call | solution.py:101
  12.1 2.9 %collective-permute-start.1 = (f32[512,128]{1,0:T(8,128)S(1)}, f32[512,128]{1,0:T(8,128)S(1)}, u32[]{:S(2)}, u32[]{:S(2)}) collective-permute-start(f32[512,128]{1,0:T(8,128)S(1)} %add.216), channel_id=1, source_target_pairs={{0,2},{1,3},{2,0},{3,1},{4,6},{5,7},{6,4},{7,5},{8,10},{9,11},{10,... | collective-permute-start | bytes 786440 | tf_op jit(solution)/shard_map/ppermute | solution.py:321
  15.4 6.7 %collective-permute-done.1 = f32[512,128]{1,0:T(8,128)S(1)} collective-permute-done((f32[512,128]{1,0:T(8,128)S(1)}, f32[512,128]{1,0:T(8,128)S(1)}, u32[]{:S(2)}, u32[]{:S(2)}) %collective-permute-start.1) | collective-permute-done | bytes 262176 | tf_op jit(solution)/shard_map/ppermute | solution.py:321
  22.3 5.0 %collective-permute-done.35 = f32[512,128]{1,0:T(8,128)S(1)} collective-permute-done((f32[512,128]{1,0:T(8,128)S(1)}, f32[512,128]{1,0:T(8,128)S(1)}, u32[]{:S(2)}, u32[]{:S(2)}) %collective-permute-start.35) | collective-permute-done | bytes 262176 | tf_op jit(solution)/shard_map/ppermute | solution.py:321
  27.6 3.4 %copy-done = f32[4,2048,256]{2,1,0:T(8,128)S(1)} copy-done((f32[4,2048,256]{2,1,0:T(8,128)S(1)}, f32[4,2048,256]{2,1,0:T(8,128)}, u32[]{:S(2)}) %copy-start) | copy-done | bytes 8388632
  30.9 5.1 %panel.4 = (f32[256,128]{1,0:T(8,128)S(1)}, f32[256,128]{1,0:T(8,128)S(1)}, f32[256,128]{1,0:T(8,128)S(1)}, f32[256,128]{1,0:T(8,128)S(1)}, f32[256,128]{1,0:T(8...) custom-call(s32[8]{0:T(128)S(1)} %stack.53.where, s32[1]{0:T(128)} %bitcast.8.half, ...), custom_call_target="tpu_custom_call" | custom-call | flops 2147483648 | bytes 8388608 | tf_op jit(solution)/shard_map/panel/pallas_call | solution.py:162
  36.1 1.8 collective-permute-start.5
  37.9 5.1 %panel.6 = (f32[256,128]{1,0:T(8,128)S(1)}, f32[256,128]{1,0:T(8,128)S(1)}, f32[256,128]{1,0:T(8,128)S(1)}, f32[256,128]{1,0:T(8,128)S(1)}, f32[256,128]{1,0:T(8...) custom-call(s32[8]{0:T(128)S(1)} %stack.53.where, s32[1]{0:T(128)} %bitcast.8.half, ...), custom_call_target="tpu_custom_call" | custom-call | flops 2147483648 | bytes 8388608 | tf_op jit(solution)/shard_map/panel/pallas_call | solution.py:162
  43.4 1.8 collective-permute-start.39
  45.4 1.9 collective-permute-start.7
  47.3 2.2 collective-permute-done.37
  49.7 2.6 %collective-permute-done.39 = f32[256,128]{1,0:T(8,128)S(1)} collective-permute-done((f32[256,128]{1,0:T(8,128)S(1)}, f32[256,128]{1,0:T(8,128)S(1)}, u32[]{:S(2)}, u32[]{:S(2)}) %collective-permute-start.39) | collective-permute-done | bytes 131104 | tf_op jit(solution)/shard_map/ppermute | solution.py:315
  52.3 1.7 collective-permute-start.41
  57.1 2.0 collective-permute-done.41
  59.1 6.4 %collective-permute-done.6 = f32[256,128]{1,0:T(8,128)S(1)} collective-permute-done((f32[256,128]{1,0:T(8,128)S(1)}, f32[256,128]{1,0:T(8,128)S(1)}, u32[]{:S(2)}, u32[]{:S(2)}) %collective-permute-start.6) | collective-permute-done | bytes 131104 | tf_op jit(solution)/shard_map/ppermute | solution.py:315
  68.8 4.8 %collective-permute-done.42 = f32[256,128]{1,0:T(8,128)S(1)} collective-permute-done((f32[256,128]{1,0:T(8,128)S(1)}, f32[256,128]{1,0:T(8,128)S(1)}, u32[]{:S(2)}, u32[]{:S(2)}) %collective-permute-start.42) | collective-permute-done | bytes 131104 | tf_op jit(solution)/shard_map/ppermute | solution.py:318
  75.8 4.9 %collective-permute-done.43 = f32[256,128]{1,0:T(8,128)S(1)} collective-permute-done((f32[256,128]{1,0:T(8,128)S(1)}, f32[256,128]{1,0:T(8,128)S(1)}, u32[]{:S(2)}, u32[]{:S(2)}) %collective-permute-start.43) | collective-permute-done | bytes 131104 | tf_op jit(solution)/shard_map/ppermute | solution.py:318
  80.8 2.6 %collective-permute-done.11.refs_2_ = f32[256,128]{1,0:T(8,128)S(1)} collective-permute-done((f32[256,128]{1,0:T(8,128)S(1)}, f32[256,128]{1,0:T(8,128)S(1)}, u32[]{:S(2)}, u32[]{:S(2)}) %collective-permute-start.11) | collective-permute-done | bytes 131104 | tf_op jit(solution)/shard_map/ppermute | solution.py:318
  83.4 4.1 %collective-permute-done.45.refs_2_.refs_10_ = f32[256,128]{1,0:T(8,128)S(1)} collective-permute-done((f32[256,128]{1,0:T(8,128)S(1)}, f32[256,128]{1,0:T(8,128)S(1)}, u32[]{:S(2)}, u32[]{:S(2)}) %collective-permute-start.45) | collective-permute-done | bytes 131104 | tf_op jit(solution)/shard_map/ppermute | solution.py:318
  87.5 4.0 %collective-permute-done.13.refs_4_ = f32[256,128]{1,0:T(8,128)S(1)} collective-permute-done((f32[256,128]{1,0:T(8,128)S(1)}, f32[256,128]{1,0:T(8,128)S(1)}, u32[]{:S(2)}, u32[]{:S(2)}) %collective-permute-start.13) | collective-permute-done | bytes 131104 | tf_op jit(solution)/shard_map/ppermute | solution.py:318
  95.3 3.0 %collective-permute-done.15.refs_6_ = f32[256,128]{1,0:T(8,128)S(1)} collective-permute-done((f32[256,128]{1,0:T(8,128)S(1)}, f32[256,128]{1,0:T(8,128)S(1)}, u32[]{:S(2)}, u32[]{:S(2)}) %collective-permute-start.15) | collective-permute-done | bytes 131104 | tf_op jit(solution)/shard_map/ppermute | solution.py:318
  104.1 2.3 collective-permute-done.16.refs_7_
  106.3 3.4 %copy-done.2 = f32[4,256,2048]{2,1,0:T(8,128)S(1)} copy-done((f32[4,256,2048]{2,1,0:T(8,128)S(1)}, f32[4,256,2048]{2,1,0:T(8,128)}, u32[]{:S(2)}) %copy-start.2) | copy-done | bytes 8388632
  109.7 4.7 %coef.4 = (f32[520,128]{1,0:T(8,128)S(1)}, f32[520,128]{1,0:T(8,128)S(1)}) custom-call(s32[8]{0:T(128)S(1)} %stack.50.where, s32[1]{0:T(128)} %bitcast.8.half, f32[1024,2048]{1,0:T(8,128)S(1)} %bitcast.15, f32[256,128]{1,0:T(8,128)S(1)} %add_add_fusion.11.refs_0_, f32[256,128]{1,0:T(8,128)S(1)} %collective-permute-done.10.refs_1_, ...), custom_call_target="tpu_custom_call" | custom-call | flops 2147483648 | bytes 8388608 | tf_op jit(solution)/shard_map/coef/pallas_call | solution.py:101
  114.6 4.7 %coef.5 = (f32[520,128]{1,0:T(8,128)S(1)}, f32[520,128]{1,0:T(8,128)S(1)}) custom-call(s32[8]{0:T(128)S(1)} %stack.50.where, s32[1]{0:T(128)} %bitcast.8.half, f32[1024,2048]{1,0:T(8,128)S(1)} %bitcast.16, f32[256,128]{1,0:T(8,128)S(1)} %add_add_fusion.5.refs_0_.refs_8_, f32[256,128]{1,0:T(8,128)S(1)} %collective-permute-done.44.refs_1_.refs_9_, ...), custom_call_target="tpu_custom_call" | custom-call | flops 2147483648 | bytes 8388608 | tf_op jit(solution)/shard_map/coef/pallas_call | solution.py:101
  122.6 6.6 %collective-permute-done.18 = f32[520,128]{1,0:T(8,128)S(1)} collective-permute-done((f32[520,128]{1,0:T(8,128)S(1)}, f32[520,128]{1,0:T(8,128)S(1)}, u32[]{:S(2)}, u32[]{:S(2)}) %collective-permute-start.18) | collective-permute-done | bytes 266272 | tf_op jit(solution)/shard_map/ppermute | solution.py:321
  129.3 4.7 %collective-permute-done.52 = f32[520,128]{1,0:T(8,128)S(1)} collective-permute-done((f32[520,128]{1,0:T(8,128)S(1)}, f32[520,128]{1,0:T(8,128)S(1)}, u32[]{:S(2)}, u32[]{:S(2)}) %collective-permute-start.52) | collective-permute-done | bytes 266272 | tf_op jit(solution)/shard_map/ppermute | solution.py:321
  134.1 5.2 %panel.5 = (f32[256,128]{1,0:T(8,128)S(1)}, f32[256,128]{1,0:T(8,128)S(1)}, f32[256,128]{1,0:T(8,128)S(1)}, f32[256,128]{1,0:T(8,128)S(1)}, f32[256,128]{1,0:T(8...) custom-call(s32[8]{0:T(128)S(1)} %stack.53.where, ...), custom_call_target="tpu_custom_call" | custom-call | flops 2147483648 | bytes 8388608 | tf_op jit(solution)/shard_map/panel/pallas_call | solution.py:162
  141.4 5.2 %panel.7 = (f32[256,128]{1,0:T(8,128)S(1)}, f32[256,128]{1,0:T(8,128)S(1)}, f32[256,128]{1,0:T(8,128)S(1)}, f32[256,128]{1,0:T(8,128)S(1)}, f32[256,128]{1,0:T(8...) custom-call(s32[8]{0:T(128)S(1)} %stack.53.where, ...), custom_call_target="tpu_custom_call" | custom-call | flops 2147483648 | bytes 8388608 | tf_op jit(solution)/shard_map/panel/pallas_call | solution.py:162
  150.8 2.2 collective-permute-done.54
  153.5 2.3 collective-permute-done.56
  156.5 6.1 %collective-permute-done.58 = f32[256,128]{1,0:T(8,128)S(1)} collective-permute-done((f32[256,128]{1,0:T(8,128)S(1)}, f32[256,128]{1,0:T(8,128)S(1)}, u32[]{:S(2)}, u32[]{:S(2)}) %collective-permute-start.58) | collective-permute-done | bytes 131104 | tf_op jit(solution)/shard_map/ppermute | solution.py:318
  163.7 5.8 %collective-permute-done.25 = f32[256,128]{1,0:T(8,128)S(1)} collective-permute-done((f32[256,128]{1,0:T(8,128)S(1)}, f32[256,128]{1,0:T(8,128)S(1)}, u32[]{:S(2)}, u32[]{:S(2)}) %collective-permute-start.25) | collective-permute-done | bytes 131104 | tf_op jit(solution)/shard_map/ppermute | solution.py:318
  169.5 2.2 collective-permute-done.59
  171.8 4.5 %collective-permute-done.26 = f32[256,128]{1,0:T(8,128)S(1)} collective-permute-done((f32[256,128]{1,0:T(8,128)S(1)}, f32[256,128]{1,0:T(8,128)S(1)}, u32[]{:S(2)}, u32[]{:S(2)}) %collective-permute-start.26) | collective-permute-done | bytes 131104 | tf_op jit(solution)/shard_map/ppermute | solution.py:318
  176.4 3.5 %collective-permute-done.60 = f32[256,128]{1,0:T(8,128)S(1)} collective-permute-done((f32[256,128]{1,0:T(8,128)S(1)}, f32[256,128]{1,0:T(8,128)S(1)}, u32[]{:S(2)}, u32[]{:S(2)}) %collective-permute-start.60) | collective-permute-done | bytes 131104 | tf_op jit(solution)/shard_map/ppermute | solution.py:318
  180.0 3.1 %collective-permute-done.28.refs_2_ = f32[256,128]{1,0:T(8,128)S(1)} collective-permute-done((f32[256,128]{1,0:T(8,128)S(1)}, f32[256,128]{1,0:T(8,128)S(1)}, u32[]{:S(2)}, u32[]{:S(2)}) %collective-permute-start.28) | collective-permute-done | bytes 131104 | tf_op jit(solution)/shard_map/ppermute | solution.py:318
  183.1 4.6 %collective-permute-done.62.refs_10_ = f32[256,128]{1,0:T(8,128)S(1)} collective-permute-done((f32[256,128]{1,0:T(8,128)S(1)}, f32[256,128]{1,0:T(8,128)S(1)}, u32[]{:S(2)}, u32[]{:S(2)}) %collective-permute-start.62) | collective-permute-done | bytes 131104 | tf_op jit(solution)/shard_map/ppermute | solution.py:318
  191.0 3.8 %collective-permute-done.64.refs_12_ = f32[256,128]{1,0:T(8,128)S(1)} collective-permute-done((f32[256,128]{1,0:T(8,128)S(1)}, f32[256,128]{1,0:T(8,128)S(1)}, u32[]{:S(2)}, u32[]{:S(2)}) %collective-permute-start.64) | collective-permute-done | bytes 131104 | tf_op jit(solution)/shard_map/ppermute | solution.py:318
  197.5 2.2 collective-permute-done.29.refs_3_
  202.4 1.7 gram.3
  208.4 1.7 gram.2
  213.2 3.5 %collective-permute-done.72 = f32[128,256]{1,0:T(8,128)S(1)} collective-permute-done((f32[128,256]{1,0:T(8,128)S(1)}, f32[128,256]{1,0:T(8,128)S(1)}, u32[]{:S(2)}, u32[]{:S(2)}) %collective-permute-start.72) | collective-permute-done | bytes 131104 | tf_op jit(solution)/shard_map/ppermute | solution.py:321
  216.8 2.3 %collective-permute-done.69 = f32[128,256]{1,0:T(8,128)S(1)} collective-permute-done((f32[128,256]{1,0:T(8,128)S(1)}, f32[128,256]{1,0:T(8,128)S(1)}, u32[]{:S(2)}, u32[]{:S(2)}) %collective-permute-start.69) | collective-permute-done | bytes 131104 | tf_op jit(solution)/shard_map/ppermute | solution.py:321
  219.2 2.9 %mixing.2.before = f32[256,256]{1,0:T(8,128)S(1)} custom-call(s32[1]{0:T(128)} %bitcast.8.half, f32[128,256]{1,0:T(8,128)S(1)} %add.255.mine, f32[128,256]{1,0:T(8,128)S(1)} %collective-permute-done.73.partner), custom_call_target="tpu_custom_call" | custom-call | flops 1509949440 | bytes 786432 | tf_op jit(solution)/shard_map/mixing/pallas_call | solution.py:260
  222.1 3.8 %mixing.3 = f32[256,256]{1,0:T(8,128)S(1)} custom-call(s32[1]{0:T(128)} %bitcast.8.half, f32[128,256]{1,0:T(8,128)S(1)} %add.253.mine, f32[128,256]{1,0:T(8,128)S(1)} %collective-permute-done.70.partner, f32[256,256]{1,0:T(8,128)S(1)} %mixing.2.before, f32[8,128]{1,0:T(8,128)S(1)} %get-tuple-element.127.refs_0_, f32[8,128]{1,0:T(8,128)S(1)} %get-tuple-element.128.refs_1_), custom_call_target="tpu_custom_call" | custom-call | flops 1509949440 | bytes 786432 | tf_op jit(solution)/shard_map/mixing/pallas_call | solution.py:260
  225.9 3.0 %apply.1 = f32[2048,256]{1,0:T(8,128)} custom-call(s32[8]{0:T(128)S(1)} %stack.50.where, f32[256,256]{1,0:T(8,128)S(1)} %mixing.3, f32[256,128]{1,0:T(8,128)S(1)} %add_add_fusion.8.refs_0_, f32[256,128]{1,0:T(8,128)S(1)} %collective-permute-done.27.refs_1_, f32[256,128]{1,0:T(8,128)S(1)} %collective-permute-done.28.refs_2_, ...), custom_call_target="tpu_custom_call" | custom-call | flops 805306368 | bytes 4194304 | tf_op jit(solution)/shard_map/apply/pallas_call | solution.py:287
  (157 shorter events, 51.7 us)
Async XLA Ops:
  12.1 10.0 %collective-permute-start.1 = (f32[512,128]{1,0:T(8,128)S(1)}, f32[512,128]{1,0:T(8,128)S(1)}, u32[]{:S(2)}, u32[]{:S(2)}) collective-permute-start(f32[512,128]{1,0:T(8,128)S(1)} %add.216), channel_id=1, source_target_pairs={{0,2},{1,3},{2,0},{3,1},{4,6},{5,7},{6,4},{7,5},{8,10},{9,11},{10,... | collective-permute-start | bytes 786440 | tf_op jit(solution)/shard_map/ppermute | solution.py:321
  15.1 12.2 %collective-permute-start.35 = (f32[512,128]{1,0:T(8,128)S(1)}, f32[512,128]{1,0:T(8,128)S(1)}, u32[]{:S(2)}, u32[]{:S(2)}) collective-permute-start(f32[512,128]{1,0:T(8,128)S(1)} %add.234), channel_id=1, source_target_pairs={{0,2},{1,3},{2,0},{3,1},{4,6},{5,7},{6,4},{7,5},{8,10},{9,11},{10,... | collective-permute-start | bytes 786440 | tf_op jit(solution)/shard_map/ppermute | solution.py:321
  27.3 10.6 %collective-permute-start.36 = (f32[512,128]{1,0:T(8,128)S(1)}, f32[512,128]{1,0:T(8,128)S(1)}, u32[]{:S(2)}, u32[]{:S(2)}) collective-permute-start(f32[512,128]{1,0:T(8,128)S(1)} %add.235.mine_ref), channel_id=1, source_target_pairs={{0,1},{1,0},{2,3},{3,2},{4,5},{5,4},{6,7},{7,6},{8,9},{9,8},{10,11... | collective-permute-start | bytes 786440 | tf_op jit(solution)/shard_map/ppermute | solution.py:321
  36.1 9.3 %collective-permute-start.5 = (f32[256,128]{1,0:T(8,128)S(1)}, f32[256,128]{1,0:T(8,128)S(1)}, u32[]{:S(2)}, u32[]{:S(2)}) collective-permute-start(f32[256,128]{1,0:T(8,128)S(1)} %get-tuple-element.74), channel_id=1, source_target_pairs={{0,4},{4,0},{8,12},{12,8},{16,20},{20,16},{24,28},{28,24},{1,5},{5... | collective-permute-start | bytes 393224 | tf_op jit(solution)/shard_map/ppermute | solution.py:315
  43.4 8.9 %collective-permute-start.39 = (f32[256,128]{1,0:T(8,128)S(1)}, f32[256,128]{1,0:T(8,128)S(1)}, u32[]{:S(2)}, u32[]{:S(2)}) collective-permute-start(f32[256,128]{1,0:T(8,128)S(1)} %get-tuple-element.102), channel_id=1, source_target_pairs={{0,4},{4,0},{8,12},{12,8},{16,20},{20,16},{24,28},{28,24},{1,5},{5... | collective-permute-start | bytes 393224 | tf_op jit(solution)/shard_map/ppermute | solution.py:315
  45.2 9.9 %collective-permute-start.3 = (f32[256,128]{1,0:T(8,128)S(1)}, f32[256,128]{1,0:T(8,128)S(1)}, u32[]{:S(2)}, u32[]{:S(2)}) collective-permute-start(f32[256,128]{1,0:T(8,128)S(1)} %get-tuple-element.70), channel_id=1, source_target_pairs={{0,4},{4,0},{8,12},{12,8},{16,20},{20,16},{24,28},{28,24},{1,5},{5... | collective-permute-start | bytes 393224 | tf_op jit(solution)/shard_map/ppermute | solution.py:315
  45.4 10.5 %collective-permute-start.7 = (f32[256,128]{1,0:T(8,128)S(1)}, f32[256,128]{1,0:T(8,128)S(1)}, u32[]{:S(2)}, u32[]{:S(2)}) collective-permute-start(f32[256,128]{1,0:T(8,128)S(1)} %add.221), channel_id=1, source_target_pairs={{0,8},{4,12},{8,16},{12,20},{16,24},{20,28},{24,0},{28,4},{1,9},{5... | collective-permute-start | bytes 393224 | tf_op jit(solution)/shard_map/ppermute | solution.py:318
  49.5 26.4 %collective-permute-start.38 = (f32[256,128]{1,0:T(8,128)S(1)}, f32[256,128]{1,0:T(8,128)S(1)}, u32[]{:S(2)}, u32[]{:S(2)}) collective-permute-start(f32[256,128]{1,0:T(8,128)S(1)} %get-tuple-element.99), channel_id=1, source_target_pairs={{0,4},{4,0},{8,12},{12,8},{16,20},{20,16},{24,28},{28,24},{1,5},{5... | collective-permute-start | bytes 393224 | tf_op jit(solution)/shard_map/ppermute | solution.py:315
  53.9 14.8 %collective-permute-start.40 = (f32[256,128]{1,0:T(8,128)S(1)}, f32[256,128]{1,0:T(8,128)S(1)}, u32[]{:S(2)}, u32[]{:S(2)}) collective-permute-start(f32[256,128]{1,0:T(8,128)S(1)} %get-tuple-element.103), channel_id=1, source_target_pairs={{0,4},{4,0},{8,12},{12,8},{16,20},{20,16},{24,28},{28,24},{1,5},{5... | collective-permute-start | bytes 393224 | tf_op jit(solution)/shard_map/ppermute | solution.py:315
  55.1 18.6 %collective-permute-start.4 = (f32[256,128]{1,0:T(8,128)S(1)}, f32[256,128]{1,0:T(8,128)S(1)}, u32[]{:S(2)}, u32[]{:S(2)}) collective-permute-start(f32[256,128]{1,0:T(8,128)S(1)} %get-tuple-element.71), channel_id=1, source_target_pairs={{0,4},{4,0},{8,12},{12,8},{16,20},{20,16},{24,28},{28,24},{1,5},{5... | collective-permute-start | bytes 393224 | tf_op jit(solution)/shard_map/ppermute | solution.py:315
  56.0 9.6 %collective-permute-start.6 = (f32[256,128]{1,0:T(8,128)S(1)}, f32[256,128]{1,0:T(8,128)S(1)}, u32[]{:S(2)}, u32[]{:S(2)}) collective-permute-start(f32[256,128]{1,0:T(8,128)S(1)} %get-tuple-element.75), channel_id=1, source_target_pairs={{0,4},{4,0},{8,12},{12,8},{16,20},{20,16},{24,28},{28,24},{1,5},{5... | collective-permute-start | bytes 393224 | tf_op jit(solution)/shard_map/ppermute | solution.py:315
  59.1 8.0 %collective-permute-start.8 = (f32[256,128]{1,0:T(8,128)S(1)}, f32[256,128]{1,0:T(8,128)S(1)}, u32[]{:S(2)}, u32[]{:S(2)}) collective-permute-start(f32[256,128]{1,0:T(8,128)S(1)} %add_add_fusion.9), channel_id=1, source_target_pairs={{0,8},{4,12},{8,16},{12,20},{16,24},{20,28},{24,0},{28,4},{1,9},{5... | collective-permute-start | bytes 393224 | tf_op jit(solution)/shard_map/ppermute | solution.py:318
  65.5 8.0 %collective-permute-start.42 = (f32[256,128]{1,0:T(8,128)S(1)}, f32[256,128]{1,0:T(8,128)S(1)}, u32[]{:S(2)}, u32[]{:S(2)}) collective-permute-start(f32[256,128]{1,0:T(8,128)S(1)} %add_add_fusion.3), channel_id=1, source_target_pairs={{0,8},{4,12},{8,16},{12,20},{16,24},{20,28},{24,0},{28,4},{1,9},{5... | collective-permute-start | bytes 393224 | tf_op jit(solution)/shard_map/ppermute | solution.py:318
  67.2 7.8 %collective-permute-start.9 = (f32[256,128]{1,0:T(8,128)S(1)}, f32[256,128]{1,0:T(8,128)S(1)}, u32[]{:S(2)}, u32[]{:S(2)}) collective-permute-start(f32[256,128]{1,0:T(8,128)S(1)} %add_add_fusion.10), channel_id=1, source_target_pairs={{0,8},{4,12},{8,16},{12,20},{16,24},{20,28},{24,0},{28,4},{1,9},{5... | collective-permute-start | bytes 393224 | tf_op jit(solution)/shard_map/ppermute | solution.py:318
  73.6 7.1 %collective-permute-start.43 = (f32[256,128]{1,0:T(8,128)S(1)}, f32[256,128]{1,0:T(8,128)S(1)}, u32[]{:S(2)}, u32[]{:S(2)}) collective-permute-start(f32[256,128]{1,0:T(8,128)S(1)} %add_add_fusion.4), channel_id=1, source_target_pairs={{0,8},{4,12},{8,16},{12,20},{16,24},{20,28},{24,0},{28,4},{1,9},{5... | collective-permute-start | bytes 393224 | tf_op jit(solution)/shard_map/ppermute | solution.py:318
  75.0 8.4 %collective-permute-start.11 = (f32[256,128]{1,0:T(8,128)S(1)}, f32[256,128]{1,0:T(8,128)S(1)}, u32[]{:S(2)}, u32[]{:S(2)}) collective-permute-start(f32[256,128]{1,0:T(8,128)S(1)} %add_add_fusion.11.refs_0_), channel_id=1, source_target_pairs={{0,8},{4,12},{8,16},{12,20},{16,24},{20,28},{24,0},{28,4},{1,9},{5... | collective-permute-start | bytes 393224 | tf_op jit(solution)/shard_map/ppermute | solution.py:318
  83.4 8.1 %collective-permute-start.13 = (f32[256,128]{1,0:T(8,128)S(1)}, f32[256,128]{1,0:T(8,128)S(1)}, u32[]{:S(2)}, u32[]{:S(2)}) collective-permute-start(f32[256,128]{1,0:T(8,128)S(1)} %collective-permute-done.11.refs_2_), channel_id=1, source_target_pairs={{0,8},{4,12},{8,16},{12,20},{16,24},{20,28},{24,0},{28,4},{1,9},{5... | collective-permute-start | bytes 393224 | tf_op jit(solution)/shard_map/ppermute | solution.py:318
  91.6 7.4 %collective-permute-start.10 = (f32[256,128]{1,0:T(8,128)S(1)}, f32[256,128]{1,0:T(8,128)S(1)}, u32[]{:S(2)}, u32[]{:S(2)}) collective-permute-start(f32[256,128]{1,0:T(8,128)S(1)} %add_add_fusion.11.refs_0_), channel_id=1, source_target_pairs={{0,4},{4,0},{8,12},{12,8},{16,20},{20,16},{24,28},{28,24},{1,5},{5... | collective-permute-start | bytes 393224 | tf_op jit(solution)/shard_map/ppermute | solution.py:315
  92.1 8.6 %collective-permute-start.12 = (f32[256,128]{1,0:T(8,128)S(1)}, f32[256,128]{1,0:T(8,128)S(1)}, u32[]{:S(2)}, u32[]{:S(2)}) collective-permute-start(f32[256,128]{1,0:T(8,128)S(1)} %collective-permute-done.11.refs_2_), channel_id=1, source_target_pairs={{0,4},{4,0},{8,12},{12,8},{16,20},{20,16},{24,28},{28,24},{1,5},{5... | collective-permute-start | bytes 393224 | tf_op jit(solution)/shard_map/ppermute | solution.py:315
  94.3 9.2 %collective-permute-start.14 = (f32[256,128]{1,0:T(8,128)S(1)}, f32[256,128]{1,0:T(8,128)S(1)}, u32[]{:S(2)}, u32[]{:S(2)}) collective-permute-start(f32[256,128]{1,0:T(8,128)S(1)} %collective-permute-done.13.refs_4_), channel_id=1, source_target_pairs={{0,4},{4,0},{8,12},{12,8},{16,20},{20,16},{24,28},{28,24},{1,5},{5... | collective-permute-start | bytes 393224 | tf_op jit(solution)/shard_map/ppermute | solution.py:315
  98.3 8.0 %collective-permute-start.16 = (f32[256,128]{1,0:T(8,128)S(1)}, f32[256,128]{1,0:T(8,128)S(1)}, u32[]{:S(2)}, u32[]{:S(2)}) collective-permute-start(f32[256,128]{1,0:T(8,128)S(1)} %collective-permute-done.15.refs_6_), channel_id=1, source_target_pairs={{0,4},{4,0},{8,12},{12,8},{16,20},{20,16},{24,28},{28,24},{1,5},{5... | collective-permute-start | bytes 393224 | tf_op jit(solution)/shard_map/ppermute | solution.py:315
  99.0 15.5 %collective-permute-start.44 = (f32[256,128]{1,0:T(8,128)S(1)}, f32[256,128]{1,0:T(8,128)S(1)}, u32[]{:S(2)}, u32[]{:S(2)}) collective-permute-start(f32[256,128]{1,0:T(8,128)S(1)} %add_add_fusion.5.refs_0_.refs_8_), channel_id=1, source_target_pairs={{0,4},{4,0},{8,12},{12,8},{16,20},{20,16},{24,28},{28,24},{1,5},{5... | collective-permute-start | bytes 393224 | tf_op jit(solution)/shard_map/ppermute | solution.py:315
  100.7 13.8 %collective-permute-start.46 = (f32[256,128]{1,0:T(8,128)S(1)}, f32[256,128]{1,0:T(8,128)S(1)}, u32[]{:S(2)}, u32[]{:S(2)}) collective-permute-start(f32[256,128]{1,0:T(8,128)S(1)} %collective-permute-done.45.refs_2_.refs_10_), channel_id=1, source_target_pairs={{0,4},{4,0},{8,12},{12,8},{16,20},{20,16},{24,28},{28,24},{1,5},{5... | collective-permute-start | bytes 393224 | tf_op jit(solution)/shard_map/ppermute | solution.py:315
  101.2 13.3 %collective-permute-start.48 = (f32[256,128]{1,0:T(8,128)S(1)}, f32[256,128]{1,0:T(8,128)S(1)}, u32[]{:S(2)}, u32[]{:S(2)}) collective-permute-start(f32[256,128]{1,0:T(8,128)S(1)} %collective-permute-done.47.refs_4_.refs_12_), channel_id=1, source_target_pairs={{0,4},{4,0},{8,12},{12,8},{16,20},{20,16},{24,28},{28,24},{1,5},{5... | collective-permute-start | bytes 393224 | tf_op jit(solution)/shard_map/ppermute | solution.py:315
  103.5 11.0 %collective-permute-start.50 = (f32[256,128]{1,0:T(8,128)S(1)}, f32[256,128]{1,0:T(8,128)S(1)}, u32[]{:S(2)}, u32[]{:S(2)}) collective-permute-start(f32[256,128]{1,0:T(8,128)S(1)} %collective-permute-done.49.refs_6_.refs_14_), channel_id=1, source_target_pairs={{0,4},{4,0},{8,12},{12,8},{16,20},{20,16},{24,28},{28,24},{1,5},{5... | collective-permute-start | bytes 393224 | tf_op jit(solution)/shard_map/ppermute | solution.py:315
  119.9 9.3 %collective-permute-start.18 = (f32[520,128]{1,0:T(8,128)S(1)}, f32[520,128]{1,0:T(8,128)S(1)}, u32[]{:S(2)}, u32[]{:S(2)}) collective-permute-start(f32[520,128]{1,0:T(8,128)S(1)} %add.225), channel_id=1, source_target_pairs={{0,2},{1,3},{2,0},{3,1},{4,6},{5,7},{6,4},{7,5},{8,10},{9,11},{10,... | collective-permute-start | bytes 798728 | tf_op jit(solution)/shard_map/ppermute | solution.py:321
  121.4 12.5 %collective-permute-start.52 = (f32[520,128]{1,0:T(8,128)S(1)}, f32[520,128]{1,0:T(8,128)S(1)}, u32[]{:S(2)}, u32[]{:S(2)}) collective-permute-start(f32[520,128]{1,0:T(8,128)S(1)} %add.243), channel_id=1, source_target_pairs={{0,2},{1,3},{2,0},{3,1},{4,6},{5,7},{6,4},{7,5},{8,10},{9,11},{10,... | collective-permute-start | bytes 798728 | tf_op jit(solution)/shard_map/ppermute | solution.py:321
  134.0 7.4 %collective-permute-start.53 = (f32[520,128]{1,0:T(8,128)S(1)}, f32[520,128]{1,0:T(8,128)S(1)}, u32[]{:S(2)}, u32[]{:S(2)}) collective-permute-start(f32[520,128]{1,0:T(8,128)S(1)} %add.244.mine_ref), channel_id=1, source_target_pairs={{0,1},{1,0},{2,3},{3,2},{4,5},{5,4},{6,7},{7,6},{8,9},{9,8},{10,11... | collective-permute-start | bytes 798728 | tf_op jit(solution)/shard_map/ppermute | solution.py:321
  139.3 9.4 %collective-permute-start.20 = (f32[256,128]{1,0:T(8,128)S(1)}, f32[256,128]{1,0:T(8,128)S(1)}, u32[]{:S(2)}, u32[]{:S(2)}) collective-permute-start(f32[256,128]{1,0:T(8,128)S(1)} %get-tuple-element.84), channel_id=1, source_target_pairs={{0,4},{4,0},{8,12},{12,8},{16,20},{20,16},{24,28},{28,24},{1,5},{5... | collective-permute-start | bytes 393224 | tf_op jit(solution)/shard_map/ppermute | solution.py:315
  139.9 8.7 %collective-permute-start.22 = (f32[256,128]{1,0:T(8,128)S(1)}, f32[256,128]{1,0:T(8,128)S(1)}, u32[]{:S(2)}, u32[]{:S(2)}) collective-permute-start(f32[256,128]{1,0:T(8,128)S(1)} %get-tuple-element.88), channel_id=1, source_target_pairs={{0,4},{4,0},{8,12},{12,8},{16,20},{20,16},{24,28},{28,24},{1,5},{5... | collective-permute-start | bytes 393224 | tf_op jit(solution)/shard_map/ppermute | solution.py:315
  147.2 8.6 %collective-permute-start.56 = (f32[256,128]{1,0:T(8,128)S(1)}, f32[256,128]{1,0:T(8,128)S(1)}, u32[]{:S(2)}, u32[]{:S(2)}) collective-permute-start(f32[256,128]{1,0:T(8,128)S(1)} %get-tuple-element.116), channel_id=1, source_target_pairs={{0,4},{4,0},{8,12},{12,8},{16,20},{20,16},{24,28},{28,24},{1,5},{5... | collective-permute-start | bytes 393224 | tf_op jit(solution)/shard_map/ppermute | solution.py:315
  148.7 7.2 %collective-permute-start.24 = (f32[256,128]{1,0:T(8,128)S(1)}, f32[256,128]{1,0:T(8,128)S(1)}, u32[]{:S(2)}, u32[]{:S(2)}) collective-permute-start(f32[256,128]{1,0:T(8,128)S(1)} %add.230), channel_id=1, source_target_pairs={{0,8},{4,12},{8,16},{12,20},{16,24},{20,28},{24,0},{28,4},{1,9},{5... | collective-permute-start | bytes 393224 | tf_op jit(solution)/shard_map/ppermute | solution.py:318
  148.7 23.1 %collective-permute-start.21 = (f32[256,128]{1,0:T(8,128)S(1)}, f32[256,128]{1,0:T(8,128)S(1)}, u32[]{:S(2)}, u32[]{:S(2)}) collective-permute-start(f32[256,128]{1,0:T(8,128)S(1)} %get-tuple-element.85), channel_id=1, source_target_pairs={{0,4},{4,0},{8,12},{12,8},{16,20},{20,16},{24,28},{28,24},{1,5},{5... | collective-permute-start | bytes 393224 | tf_op jit(solution)/shard_map/ppermute | solution.py:315
  149.4 13.4 %collective-permute-start.23 = (f32[256,128]{1,0:T(8,128)S(1)}, f32[256,128]{1,0:T(8,128)S(1)}, u32[]{:S(2)}, u32[]{:S(2)}) collective-permute-start(f32[256,128]{1,0:T(8,128)S(1)} %get-tuple-element.89), channel_id=1, source_target_pairs={{0,4},{4,0},{8,12},{12,8},{16,20},{20,16},{24,28},{28,24},{1,5},{5... | collective-permute-start | bytes 393224 | tf_op jit(solution)/shard_map/ppermute | solution.py:315
  153.0 23.4 %collective-permute-start.55 = (f32[256,128]{1,0:T(8,128)S(1)}, f32[256,128]{1,0:T(8,128)S(1)}, u32[]{:S(2)}, u32[]{:S(2)}) collective-permute-start(f32[256,128]{1,0:T(8,128)S(1)} %get-tuple-element.113), channel_id=1, source_target_pairs={{0,4},{4,0},{8,12},{12,8},{16,20},{20,16},{24,28},{28,24},{1,5},{5... | collective-permute-start | bytes 393224 | tf_op jit(solution)/shard_map/ppermute | solution.py:315
  155.9 13.6 %collective-permute-start.57 = (f32[256,128]{1,0:T(8,128)S(1)}, f32[256,128]{1,0:T(8,128)S(1)}, u32[]{:S(2)}, u32[]{:S(2)}) collective-permute-start(f32[256,128]{1,0:T(8,128)S(1)} %get-tuple-element.117), channel_id=1, source_target_pairs={{0,4},{4,0},{8,12},{12,8},{16,20},{20,16},{24,28},{28,24},{1,5},{5... | collective-permute-start | bytes 393224 | tf_op jit(solution)/shard_map/ppermute | solution.py:315
  162.7 9.0 %collective-permute-start.59 = (f32[256,128]{1,0:T(8,128)S(1)}, f32[256,128]{1,0:T(8,128)S(1)}, u32[]{:S(2)}, u32[]{:S(2)}) collective-permute-start(f32[256,128]{1,0:T(8,128)S(1)} %add_add_fusion), channel_id=1, source_target_pairs={{0,8},{4,12},{8,16},{12,20},{16,24},{20,28},{24,0},{28,4},{1,9},{5... | collective-permute-start | bytes 393224 | tf_op jit(solution)/shard_map/ppermute | solution.py:318
  171.8 8.2 %collective-permute-start.60 = (f32[256,128]{1,0:T(8,128)S(1)}, f32[256,128]{1,0:T(8,128)S(1)}, u32[]{:S(2)}, u32[]{:S(2)}) collective-permute-start(f32[256,128]{1,0:T(8,128)S(1)} %add_add_fusion.1), channel_id=1, source_target_pairs={{0,8},{4,12},{8,16},{12,20},{16,24},{20,28},{24,0},{28,4},{1,9},{5... | collective-permute-start | bytes 393224 | tf_op jit(solution)/shard_map/ppermute | solution.py:318
  179.9 7.8 %collective-permute-start.62 = (f32[256,128]{1,0:T(8,128)S(1)}, f32[256,128]{1,0:T(8,128)S(1)}, u32[]{:S(2)}, u32[]{:S(2)}) collective-permute-start(f32[256,128]{1,0:T(8,128)S(1)} %add_add_fusion.2.refs_8_), channel_id=1, source_target_pairs={{0,8},{4,12},{8,16},{12,20},{16,24},{20,28},{24,0},{28,4},{1,9},{5... | collective-permute-start | bytes 393224 | tf_op jit(solution)/shard_map/ppermute | solution.py:318
  183.1 7.8 %collective-permute-start.30 = (f32[256,128]{1,0:T(8,128)S(1)}, f32[256,128]{1,0:T(8,128)S(1)}, u32[]{:S(2)}, u32[]{:S(2)}) collective-permute-start(f32[256,128]{1,0:T(8,128)S(1)} %collective-permute-done.28.refs_2_), channel_id=1, source_target_pairs={{0,8},{4,12},{8,16},{12,20},{16,24},{20,28},{24,0},{28,4},{1,9},{5... | collective-permute-start | bytes 393224 | tf_op jit(solution)/shard_map/ppermute | solution.py:318
  187.8 7.0 %collective-permute-start.27 = (f32[256,128]{1,0:T(8,128)S(1)}, f32[256,128]{1,0:T(8,128)S(1)}, u32[]{:S(2)}, u32[]{:S(2)}) collective-permute-start(f32[256,128]{1,0:T(8,128)S(1)} %add_add_fusion.8.refs_0_), channel_id=1, source_target_pairs={{0,4},{4,0},{8,12},{12,8},{16,20},{20,16},{24,28},{28,24},{1,5},{5... | collective-permute-start | bytes 393224 | tf_op jit(solution)/shard_map/ppermute | solution.py:315
  188.3 8.6 %collective-permute-start.61 = (f32[256,128]{1,0:T(8,128)S(1)}, f32[256,128]{1,0:T(8,128)S(1)}, u32[]{:S(2)}, u32[]{:S(2)}) collective-permute-start(f32[256,128]{1,0:T(8,128)S(1)} %add_add_fusion.2.refs_8_), channel_id=1, source_target_pairs={{0,4},{4,0},{8,12},{12,8},{16,20},{20,16},{24,28},{28,24},{1,5},{5... | collective-permute-start | bytes 393224 | tf_op jit(solution)/shard_map/ppermute | solution.py:315
  189.8 10.0 %collective-permute-start.29 = (f32[256,128]{1,0:T(8,128)S(1)}, f32[256,128]{1,0:T(8,128)S(1)}, u32[]{:S(2)}, u32[]{:S(2)}) collective-permute-start(f32[256,128]{1,0:T(8,128)S(1)} %collective-permute-done.28.refs_2_), channel_id=1, source_target_pairs={{0,4},{4,0},{8,12},{12,8},{16,20},{20,16},{24,28},{28,24},{1,5},{5... | collective-permute-start | bytes 393224 | tf_op jit(solution)/shard_map/ppermute | solution.py:315
  191.0 9.4 %collective-permute-start.32 = (f32[256,128]{1,0:T(8,128)S(1)}, f32[256,128]{1,0:T(8,128)S(1)}, u32[]{:S(2)}, u32[]{:S(2)}) collective-permute-start(f32[256,128]{1,0:T(8,128)S(1)} %collective-permute-done.30.refs_4_), channel_id=1, source_target_pairs={{0,8},{4,12},{8,16},{12,20},{16,24},{20,28},{24,0},{28,4},{1,9},{5... | collective-permute-start | bytes 393224 | tf_op jit(solution)/shard_map/ppermute | solution.py:318
  194.8 7.0 %collective-permute-start.66 = (f32[256,128]{1,0:T(8,128)S(1)}, f32[256,128]{1,0:T(8,128)S(1)}, u32[]{:S(2)}, u32[]{:S(2)}) collective-permute-start(f32[256,128]{1,0:T(8,128)S(1)} %collective-permute-done.64.refs_12_), channel_id=1, source_target_pairs={{0,8},{4,12},{8,16},{12,20},{16,24},{20,28},{24,0},{28,4},{1,9},{5... | collective-permute-start | bytes 393224 | tf_op jit(solution)/shard_map/ppermute | solution.py:318
  194.8 9.3 %collective-permute-start.63 = (f32[256,128]{1,0:T(8,128)S(1)}, f32[256,128]{1,0:T(8,128)S(1)}, u32[]{:S(2)}, u32[]{:S(2)}) collective-permute-start(f32[256,128]{1,0:T(8,128)S(1)} %collective-permute-done.62.refs_10_), channel_id=1, source_target_pairs={{0,4},{4,0},{8,12},{12,8},{16,20},{20,16},{24,28},{28,24},{1,5},{5... | collective-permute-start | bytes 393224 | tf_op jit(solution)/shard_map/ppermute | solution.py:315
  197.0 7.3 %collective-permute-start.31 = (f32[256,128]{1,0:T(8,128)S(1)}, f32[256,128]{1,0:T(8,128)S(1)}, u32[]{:S(2)}, u32[]{:S(2)}) collective-permute-start(f32[256,128]{1,0:T(8,128)S(1)} %collective-permute-done.30.refs_4_), channel_id=1, source_target_pairs={{0,4},{4,0},{8,12},{12,8},{16,20},{20,16},{24,28},{28,24},{1,5},{5... | collective-permute-start | bytes 393224 | tf_op jit(solution)/shard_map/ppermute | solution.py:315
  211.9 7.2 %collective-permute-start.69 = (f32[128,256]{1,0:T(8,128)S(1)}, f32[128,256]{1,0:T(8,128)S(1)}, u32[]{:S(2)}, u32[]{:S(2)}) collective-permute-start(f32[128,256]{1,0:T(8,128)S(1)} %add.252), channel_id=1, source_target_pairs={{0,2},{1,3},{2,0},{3,1},{4,6},{5,7},{6,4},{7,5},{8,10},{9,11},{10,... | collective-permute-start | bytes 393224 | tf_op jit(solution)/shard_map/ppermute | solution.py:321
  (33 other events, 222.0 us)

commit v3 on v2

v3 whole, which is shorter than its diff:
```python
import functools
import math

import jax
import jax.numpy as jnp
from jax import lax
from jax.experimental import pallas as pl
from jax.experimental.pallas import tpu as pltpu
from jax.sharding import PartitionSpec as P

ITERS = 2
NS_STEPS = 5
GROUPS = 2
EXTRA = 8
SLICES = 4
LARGE = 16
RING_SCATTER = True
RING_GATHER = True
CHAIN = 2
SCATTER_CHAIN = 2
ORDER_FEAT = 1
ORDER_SCATTER = 0
ORDER_GATHER = 0
JOIN = 1
WHOLE = pl.BlockSpec(memory_space=pltpu.VMEM)
SCALARS = pl.BlockSpec(memory_space=pltpu.SMEM)
F32 = jnp.float32
BF16 = jnp.bfloat16


def split(value):
    high = value.astype(BF16)
    return high, (value - high.astype(F32)).astype(BF16)


def dot(left, right):
    return jnp.dot(left, right, preferred_element_type=F32)


def product(left, right):
    left_high, left_low = split(left)
    right_high, right_low = split(right)
    return dot(left_high, right_high) + (dot(left_high, right_low) + dot(left_low, right_high))


def wide_product(left, pair, width):
    high, low = split(left)
    both = dot(high, pair)
    return both[:, :width] + (both[:, width:] + dot(low, pair[:, :width]))


def params(mib):
    return pltpu.CompilerParams(vmem_limit_bytes=mib * 2**20)


def cost(flops, moved):
    return pl.CostEstimate(flops=int(flops), bytes_accessed=int(moved), transcendentals=0)


def accumulate(a_ref, pair, total, columns):
    depth = a_ref.shape[1]
    wide = depth // SLICES
    for k in range(SLICES):
        at = pl.ds(k * wide, wide)
        term = wide_product(a_ref[:, at], pair[at, :], columns)
        total[...] = total[...] + term if k else term


def hand_out(total, half, outputs):
    tall = total.shape[0] // 2
    for out, at in zip(outputs, [(1 - half[0]) * tall, half[0] * tall]):
        out[:tall, :] = total[pl.ds(pl.multiple_of(at, tall), tall), :]


def first_coef_kernel(group, half, probes, a_ref, *refs):
    outputs, (pair, total) = refs[-4:-2], refs[-2:]
    columns = total.shape[1]
    high, low = split(probes[:, group * columns : (group + 1) * columns])
    pair[:, :columns] = high
    pair[:, columns:] = low
    accumulate(a_ref, pair, total, columns)
    hand_out(total, half, outputs)


def first_coef(a_rows, probes, group, half, also):
    total, depth = a_rows.shape
    columns = probes.shape[1] // GROUPS
    return pl.pallas_call(
        functools.partial(first_coef_kernel, group),
        in_specs=[SCALARS] + [WHOLE] * (2 + len(also)),
        out_specs=[WHOLE] * 2,
        out_shape=[jax.ShapeDtypeStruct((total // 2, columns), F32)] * 2,
        scratch_shapes=[
            pltpu.VMEM((depth, 2 * columns), BF16),
            pltpu.VMEM((total, columns), F32),
        ],
        compiler_params=params(LARGE),
        cost_estimate=cost(8 * total * depth * columns, 4 * total * depth),
        name="first_coef",
    )(half, probes, a_rows, *also)


def coef_kernel(blocks, where, half, a_ref, *refs):
    inputs, outputs, (pair, total, sums) = refs[:blocks], refs[blocks:-3], refs[-3:]
    rows, columns = inputs[0].shape
    for k in range(blocks):
        value = inputs[k][...]
        high, low = split(value)
        at = pl.ds(pl.multiple_of(where[k] * rows, rows), rows)
        pair[at, :columns] = high
        pair[at, columns:] = low
        sums[pl.ds(where[k], 1), :] = jnp.sum(value * value, axis=0, keepdims=True)
    square = jnp.sum(sums[...], axis=0, keepdims=True)
    square = jnp.sum(square, axis=1, keepdims=True)
    for out in outputs:
        out[out.shape[0] - EXTRA :, :] = jnp.broadcast_to(square, (EXTRA, out.shape[1]))
    accumulate(a_ref, pair, total, columns)
    hand_out(total, half, outputs)


def coef_terms(a_rows, basis, where, half):
    total, depth = a_rows.shape
    columns = basis[0].shape[1]
    return pl.pallas_call(
        functools.partial(coef_kernel, len(basis)),
        in_specs=[SCALARS, SCALARS, WHOLE] + [WHOLE] * len(basis),
        out_specs=[WHOLE] * 2,
        out_shape=[jax.ShapeDtypeStruct((total // 2 + EXTRA, columns), F32)] * 2,
        scratch_shapes=[
            pltpu.VMEM((depth, 2 * columns), BF16),
            pltpu.VMEM((total, columns), F32),
            pltpu.VMEM((len(basis), columns), F32),
        ],
        compiler_params=params(LARGE),
        cost_estimate=cost(8 * total * depth * columns, 4 * total * depth),
        name="coef",
    )(where, half, a_rows, *basis)


def panel_kernel(sizes, squares, where, half, ranks, b_ref, mine_ref, partner_ref, *refs):
    total = refs[-1]
    clients, rows, slots = b_ref.shape
    columns = total.shape[1]
    scale = jnp.ones((1, columns), F32)
    if squares:
        square = mine_ref[mine_ref.shape[0] - EXTRA : mine_ref.shape[0] - EXTRA + 1, :]
        scale = jnp.where(square > 0, lax.rsqrt(square), 1.0)
        refs[len(sizes)][...] = jnp.broadcast_to(scale, refs[len(sizes)].shape)
    first = half[0] == 0
    for c in range(clients):
        at = pl.ds((c % (clients // 2)) * slots, slots)
        mine, partner = mine_ref[at, :], partner_ref[at, :]
        value = jnp.where(first, mine, partner) if c < clients // 2 else jnp.where(first, partner, mine)
        slot = lax.broadcasted_iota(jnp.int32, value.shape, 0)
        value = jnp.where(slot < ranks[c], value * scale, 0.0)
        term = wide_product(b_ref[c], jnp.concatenate(split(value), axis=1), columns)
        total[...] = total[...] + term if c else term
    tall = rows // sum(sizes)
    k = 0
    for out, size in zip(refs, sizes):
        for i in range(size):
            out[i * tall : (i + 1) * tall, :] = total[pl.ds(pl.multiple_of(where[k] * tall, tall), tall), :]
            k += 1


def panel_terms(b_factors, mine, partner, where, half, ranks, sizes, squares):
    clients, rows, slots = b_factors.shape
    columns = mine.shape[1]
    tall = rows // sum(sizes)
    outs = [jax.ShapeDtypeStruct((size * tall, columns), F32) for size in sizes]
    if squares:
        outs = outs + [jax.ShapeDtypeStruct((EXTRA, columns), F32)]
    return pl.pallas_call(
        functools.partial(panel_kernel, sizes, squares),
        in_specs=[SCALARS] * 3 + [WHOLE] * 3,
        out_specs=[WHOLE] * len(outs),
        out_shape=outs,
        scratch_shapes=[
            pltpu.VMEM((rows, columns), F32),
        ],
        compiler_params=params(LARGE),
        cost_estimate=cost(8 * clients * slots * rows * columns, 4 * clients * slots * rows),
        name="panel",
    )(where, half, ranks, b_factors, mine, partner)


def gram_kernel(blocks, where, half, *refs):
    inputs, (other, mine), (highs, lows) = refs[: GROUPS * blocks], refs[-4:-2], refs[-2:]
    rows, columns = inputs[0].shape
    for g in range(GROUPS):
        for k in range(blocks):
            high, low = split(inputs[g * blocks + k][...])
            at = pl.ds(pl.multiple_of(where[k] * rows, rows), rows)
            highs[at, g * columns : (g + 1) * columns] = high
            lows[at, g * columns : (g + 1) * columns] = low
    contract = (((0,), (0,)), ((), ()))
    high = highs[...]
    cross = lax.dot_general(high, lows[...], contract, preferred_element_type=F32)
    gram = lax.dot_general(high, high, contract, preferred_element_type=F32) + (cross + cross.T)
    tall = other.shape[0]
    first = half[0] == 0
    other[...] = jnp.where(first, gram[tall:], gram[:tall])
    mine[...] = jnp.where(first, gram[:tall], gram[tall:])


def gram_terms(panels, where, half):
    blocks = len(panels[0])
    rows, columns = panels[0][0].shape
    size = GROUPS * columns
    return pl.pallas_call(
        functools.partial(gram_kernel, blocks),
        in_specs=[SCALARS, SCALARS] + [WHOLE] * (GROUPS * blocks),
        out_specs=[WHOLE] * 2,
        out_shape=[jax.ShapeDtypeStruct((size // 2, size), F32)] * 2,
        scratch_shapes=[pltpu.VMEM((blocks * rows, size), BF16)] * 2,
        compiler_params=params(LARGE),
        cost_estimate=cost(4 * blocks * rows * size * size, 4 * blocks * rows * size),
        name="gram",
    )(where, half, *[block for panel in panels for block in panel])


def iterate(gram):
    size = gram.shape[0]
    row = lax.broadcasted_iota(jnp.int32, gram.shape, 0)
    column = lax.broadcasted_iota(jnp.int32, gram.shape, 1)
    eye = jnp.where(row == column, 1.0, 0.0).astype(F32)
    trace = jnp.sum(jnp.sum(gram * eye, axis=0, keepdims=True), axis=1, keepdims=True)
    scale = lax.rsqrt(trace)
    inner = gram * scale * scale
    mixing = None
    for turn in range(NS_STEPS):
        factor = 1.5 * eye - 0.5 * inner
        mixing = product(mixing, factor) if turn else factor * scale
        if turn < NS_STEPS - 1:
            inner = product(product(inner, factor), factor)
    return mixing


def joined(half, mine, partner):
    first = half[0] == 0
    low = jnp.where(first, mine[...], partner[...])
    high = jnp.where(first, partner[...], mine[...])
    return jnp.concatenate([low, high], axis=0)


def first_kernel(half, mine, partner, out):
    out[...] = iterate(joined(half, mine, partner))


def next_kernel(factor, half, mine, partner, before, *refs):
    scales, out = refs[:-1], refs[-1]
    columns = scales[0].shape[1]
    mixing = jnp.concatenate(
        [before[g * columns : (g + 1) * columns, :] / scales[g][0:1, 0:1] for g in range(GROUPS)], axis=0
    )
    gram = joined(half, mine, partner)
    out[...] = product(mixing, iterate(product(mixing.T, product(gram, mixing)))) * factor


def mixing_of(half, mine, partner, before=None, scales=(), factor=1.0):
    size = mine.shape[1]
    operands = (half, mine, partner) + (() if before is None else (before,) + tuple(scales))
    return pl.pallas_call(
        first_kernel if before is None else functools.partial(next_kernel, factor),
        in_specs=[SCALARS] + [WHOLE] * (len(operands) - 1),
        out_specs=WHOLE,
        out_shape=jax.ShapeDtypeStruct((size, size), F32),
        compiler_params=params(LARGE),
        cost_estimate=cost(90 * size**3, 12 * size * size),
        name="mixing",
    )(*operands)


def apply_kernel(blocks, where, mixing, *refs):
    inputs, (out,) = refs[: GROUPS * blocks], refs[GROUPS * blocks :]
    rows, columns = inputs[0].shape
    high, low = split(mixing[...])
    for k in range(blocks):
        value = jnp.concatenate([inputs[g * blocks + k][...] for g in range(GROUPS)], axis=1)
        value_high, value_low = split(value)
        at = pl.ds(pl.multiple_of(where[k] * rows, rows), rows)
        out[at, :] = dot(value_high, high) + (dot(value_high, low) + dot(value_low, high))


def apply_mixing(panels, where, mixing):
    blocks = len(panels[0])
    rows, columns = panels[0][0].shape
    size = GROUPS * columns
    return pl.pallas_call(
        functools.partial(apply_kernel, blocks),
        in_specs=[SCALARS] + [WHOLE] * (1 + GROUPS * blocks),
        out_specs=WHOLE,
        out_shape=jax.ShapeDtypeStruct((blocks * rows, size), F32),
        compiler_params=params(LARGE),
        cost_estimate=cost(6 * blocks * rows * size * size, 8 * blocks * rows * size),
        name="apply",
    )(where, mixing, *[block for panel in panels for block in panel])


class Grid:
    def __init__(self, mesh, go):
        self.go = go
        self.cohorts = mesh.shape["cohort"]
        self.feats = mesh.shape["feat"]
        self.places = self.cohorts // 2
        cohort = lax.axis_index("cohort")
        place, side = cohort // 2, cohort % 2
        self.half = (lax.axis_index("feat") % 2).astype(jnp.int32).reshape(1)
        shifts = sorted(range(1, self.places), key=lambda d: (-min(d, self.places - d), d)) + [0]
        self.out_shifts = list(range(-1, -self.places, -1)) + [0] if RING_SCATTER else shifts
        self.in_shifts = list(range(0, -self.places, -1)) if RING_GATHER else [-d for d in shifts[::-1]]

        def block(shift, side):
            return lax.rem(place + shift + self.places, self.places) * 2 + side

        self.sendings = [self.out_shifts[i : i + JOIN] for i in range(0, self.places, JOIN)]
        self.sizes = [len(s) for s in self.sendings] + [1] * self.places
        self.scatter_order = jnp.stack(
            [block(d, 1 - side) for d in self.out_shifts] + [block(d, side) for d in self.out_shifts]
        ).astype(jnp.int32)
        self.gather_order = jnp.stack([block(d, s) for d in self.in_shifts for s in (side, 1 - side)]).astype(jnp.int32)

    def across(self, block):
        return lax.ppermute(block, "cohort", [(i, i ^ 1) for i in range(self.cohorts)])

    def along(self, block, shift):
        return lax.ppermute(block, "cohort", [(i, (i + 2 * shift) % self.cohorts) for i in range(self.cohorts)])

    def feat_swap(self, block, bit):
        return lax.ppermute(block, "feat", [(i, i ^ bit) for i in range(self.feats)])

    def feat_sum(self, other, mine, after=None):
        total = mine + self.feat_swap(other, 1)
        if after is not None:
            total = self.follow(total, after)
        bit = 2
        while bit < self.feats:
            total = total + self.feat_swap(total, bit)
            bit *= 2
        return total, self.feat_swap(total, 1)

    def follow(self, block, earlier):
        return jnp.where(self.go, block, earlier[: block.shape[0], : block.shape[1]])

    def scatter_sum(self, terms, after=None):
        keep = terms[len(self.sendings) :]
        rows = keep[0].shape[0]
        total, arrivals = None, []
        for i, sending in enumerate(self.sendings):
            send = terms[i]
            if SCATTER_CHAIN and i >= SCATTER_CHAIN:
                send = self.follow(send, arrivals[i - SCATTER_CHAIN])
            elif after is not None:
                send = self.follow(send, after)
            arrived = self.across(send)
            arrivals.append(arrived)
            for j, shift in enumerate(sending):
                here = arrived[j * rows : (j + 1) * rows] + keep[JOIN * i + j]
                if RING_SCATTER:
                    total = here if total is None else here + self.along(total, 1)
                else:
                    here = self.along(here, shift) if shift else here
                    total = here if total is None else total + here
        return total, arrivals

    def gather(self, block, early=None, after=None):
        blocks = []
        if after is not None:
            block = self.follow(block, after)
        own = block
        for step, shift in enumerate(self.in_shifts):
            if step and RING_GATHER:
                if CHAIN and step >= CHAIN:
                    block = self.follow(block, blocks[2 * (step - CHAIN) + 1])
                block = self.along(block, 1)
            elif step:
                block = self.along(own, -shift)
            if early is not None and step == self.places - 1:
                block = self.follow(block, early)
            blocks += [block, self.across(block)]
        return blocks


def solution(mesh):
    def on_device(b_factors, a_factors, ranks, probes):
        grid = Grid(mesh, ranks[0] > 0)
        clients, rows, slots = b_factors.shape
        a_rows = a_factors.reshape(clients * slots, rows)
        mixing, panels = None, None
        for turn in range(ITERS):
            squares = turn > 0
            if turn == 0:
                halves = [first_coef(a_rows, probes, g, grid.half, [b_factors] if g else []) for g in range(GROUPS)]
            else:
                halves = [coef_terms(a_rows, panel, grid.gather_order, grid.half) for panel in panels]
            totals, scales, arrivals, mine = [], [], None, None
            for g in range(GROUPS):
                mine, partner = grid.feat_sum(*halves[g], mine if ORDER_FEAT else None)
                terms = panel_terms(
                    b_factors, mine, partner, grid.scatter_order, grid.half, ranks, grid.sizes, squares
                )
                scales += terms[len(grid.sizes) :]
                after = arrivals[ORDER_SCATTER] if g and ORDER_SCATTER else None
                total, arrivals = grid.scatter_sum(terms[: len(grid.sizes)], after)
                totals.append(total)
            panels = []
            for g in range(GROUPS):
                after = panels[-1][ORDER_GATHER] if g and ORDER_GATHER else None
                panels.append(grid.gather(totals[g], mixing if g else None, after))
            gram = grid.feat_sum(*gram_terms(panels, grid.gather_order, grid.half))
            if turn == 0:
                mixing = mixing_of(grid.half, *gram)
            else:
                last = turn == ITERS - 1
                factor = math.sqrt(rows * grid.feats) if last else 1.0
                mixing = mixing_of(grid.half, *gram, mixing, scales, factor)
        return apply_mixing(panels, grid.gather_order, mixing)

    in_specs = (P("cohort", "feat", None), P("cohort", None, "feat"), P("cohort"), P("feat", None))
    return jax.shard_map(on_device, mesh=mesh, in_specs=in_specs, out_specs=P("feat", None), check_vma=False)
```

time: 229 us -> 210 us (0.917)
  waiting for transfers between devices: 119 us -> 99.4 us
  Pallas kernels: 48.6 us -> 37 us
  starting transfers between devices: 48 us -> 59.1 us
    ppermute x32, waiting for transfers between devices: 27.6 us -> 13.5 us  [across(): lax.ppermute(block, 'cohort', [(i, i ^ 1) for i in range(self.cohorts)])]
    pallas_call x10 -> x11, Pallas kernels: 41.9 us -> 30.3 us  [the longest x4 12.3 us: panel_terms(): pl.pallas_call(functools.partial(panel_kernel, sizes, squares), in_specs=...]
    ppermute x32, starting transfers between devices: 28.4 us -> 36.7 us  [across(): lax.ppermute(block, 'cohort', [(i, i ^ 1) for i in range(self.cohorts)])]
    ppermute x24, waiting for transfers between devices: 61.6 us -> 53.5 us  [along(): lax.ppermute(block, 'cohort', [(i, (i + 2 * shift) % self.cohorts) for i...]
    ppermute x18, waiting for transfers between devices: 29.9 us -> 32.4 us  [feat_swap(): lax.ppermute(block, 'feat', [(i, i ^ bit) for i in range(self.feats)])]
    unnamed x14 -> x16, local copies, waits for them, and re-layouts: 11.7 us -> 12.2 us
  transfers between devices with their start and end apart: 74 -> 74, of which waited for: 39 -> 40; matrix products, arithmetic and copies ran while one was open for 0% -> 0% of each run, Pallas kernels for 16% -> 12%
where the time goes in v3:
time: 210 us; the launch traced here: 209 us
  waiting for transfers between devices  99.4 us (47%)
  starting transfers between devices  59.1 us (28%)
  Pallas kernels  37 us (18%)
  local copies, waits for them, and re-layouts  12.3 us (6%)
    ppermute x24, waiting for transfers between devices, along(): lax.ppermute(block, 'cohort', [(i, (i + 2 * shift) % self.cohorts) for i...  53.5 us
    ppermute x32, starting transfers between devices, across(): lax.ppermute(block, 'cohort', [(i, i ^ 1) for i in range(self.cohorts)])  36.7 us
    ppermute x18, waiting for transfers between devices, feat_swap(): lax.ppermute(block, 'feat', [(i, i ^ bit) for i in range(self.feats)])  32.4 us
    ppermute x32, waiting for transfers between devices, across(): lax.ppermute(block, 'cohort', [(i, i ^ 1) for i in range(self.cohorts)])  13.5 us
    pallas_call x4, Pallas kernels, panel_terms(): pl.pallas_call(functools.partial(panel_kernel, sizes, squares), in_specs=...  12.3 us
    unnamed x16, local copies, waits for them, and re-layouts  12.2 us
    ppermute x18, starting transfers between devices, feat_swap(): lax.ppermute(block, 'feat', [(i, i ^ bit) for i in range(self.feats)])  11.9 us
    ppermute x24, starting transfers between devices, along(): lax.ppermute(block, 'cohort', [(i, (i + 2 * shift) % self.cohorts) for i...  10.5 us
  transfers between devices with their start and end apart: 74, of which 40 were waited for; matrix products, arithmetic and copies ran while one was open for 0% of the time, Pallas kernels for 12%

profile of v3, /device:TPU:0, one launch (start us, length us, event | category | flops | bytes accessed | tf_op | source)
XLA Modules:
  0.0 209.5 jit_solution(17322496709082260370)
XLA Ops:
  0.0 3.5 %copy-done.2 = f32[4,256,2048]{2,1,0:T(8,128)S(1)} copy-done((f32[4,256,2048]{2,1,0:T(8,128)S(1)}, f32[4,256,2048]{2,1,0:T(8,128)}, u32[]{:S(2)}) %copy-start.2) | copy-done | bytes 8388632
  3.5 1.8 copy-done.4
  5.4 2.6 %first_coef.2 = (f32[512,128]{1,0:T(8,128)S(1)}, f32[512,128]{1,0:T(8,128)S(1)}) custom-call(s32[1]{0:T(128)} %bitcast.8.half, f32[2048,256]{1,0:T(8,128)S(1)} %copy-done.4, f32[1024,2048]{1,0:T(8,128)S(1)} %bitcast.14), custom_call_target="tpu_custom_call" | custom-call | flops 2147483648 | bytes 8388608 | tf_op jit(solution)/shard_map/first_coef/pallas_call | solution.py:88
  8.5 2.6 %first_coef.3 = (f32[512,128]{1,0:T(8,128)S(1)}, f32[512,128]{1,0:T(8,128)S(1)}) custom-call(s32[1]{0:T(128)} %bitcast.8.half, f32[2048,256]{1,0:T(8,128)S(1)} %copy-done.4, f32[1024,2048]{1,0:T(8,128)S(1)} %bitcast.15, f32[4,2048,256]{2,1,0:T(8,128)S(1)} %copy-done), custom_call_target="tpu_custom_call" | custom-call | flops 2147483648 | bytes 8388608 | tf_op jit(solution)/shard_map/first_coef/pallas_call | solution.py:88
  11.3 3.0 %collective-permute-start.1 = (f32[512,128]{1,0:T(8,128)S(1)}, f32[512,128]{1,0:T(8,128)S(1)}, u32[]{:S(2)}, u32[]{:S(2)}) collective-permute-start(f32[512,128]{1,0:T(8,128)S(1)} %add.216), channel_id=1, source_target_pairs={{0,2},{1,3},{2,0},{3,1},{4,6},{5,7},{6,4},{7,5},{8,10},{9,11},{10,... | collective-permute-start | bytes 786440 | tf_op jit(solution)/shard_map/ppermute | solution.py:330
  14.3 6.4 %collective-permute-done.1 = f32[512,128]{1,0:T(8,128)S(1)} collective-permute-done((f32[512,128]{1,0:T(8,128)S(1)}, f32[512,128]{1,0:T(8,128)S(1)}, u32[]{:S(2)}, u32[]{:S(2)}) %collective-permute-start.1) | collective-permute-done | bytes 262176 | tf_op jit(solution)/shard_map/ppermute | solution.py:330
  20.8 1.8 collective-permute-start.35
  22.7 6.0 %collective-permute-done.35 = f32[512,128]{1,0:T(8,128)S(1)} collective-permute-done((f32[512,128]{1,0:T(8,128)S(1)}, f32[512,128]{1,0:T(8,128)S(1)}, u32[]{:S(2)}, u32[]{:S(2)}) %collective-permute-start.35) | collective-permute-done | bytes 262176 | tf_op jit(solution)/shard_map/ppermute | solution.py:330
  28.9 3.4 %copy-done.1 = f32[4,2048,256]{2,1,0:T(8,128)S(1)} copy-done((f32[4,2048,256]{2,1,0:T(8,128)S(1)}, f32[4,2048,256]{2,1,0:T(8,128)}, u32[]{:S(2)}) %copy-start.1) | copy-done | bytes 8388632
  32.3 3.0 %panel.4 = (f32[256,128]{1,0:T(8,128)S(1)}, f32[256,128]{1,0:T(8,128)S(1)}, f32[256,128]{1,0:T(8,128)S(1)}, f32[256,128]{1,0:T(8,128)S(1)}, f32[256,128]{1,0:T(8...) custom-call(s32[8]{0:T(128)S(1)} %stack.47.where, s32[1]{0:T(128)} %bitcast.8.half, ...), custom_call_target="tpu_custom_call" | custom-call | flops 2147483648 | bytes 8388608 | tf_op jit(solution)/shard_map/panel/pallas_call | solution.py:173
  37.4 3.0 %panel.6 = (f32[256,128]{1,0:T(8,128)S(1)}, f32[256,128]{1,0:T(8,128)S(1)}, f32[256,128]{1,0:T(8,128)S(1)}, f32[256,128]{1,0:T(8,128)S(1)}, f32[256,128]{1,0:T(8...) custom-call(s32[8]{0:T(128)S(1)} %stack.47.where, s32[1]{0:T(128)} %bitcast.8.half, ...), custom_call_target="tpu_custom_call" | custom-call | flops 2147483648 | bytes 8388608 | tf_op jit(solution)/shard_map/panel/pallas_call | solution.py:173
  42.0 2.5 %collective-permute-done.5 = f32[256,128]{1,0:T(8,128)S(1)} collective-permute-done((f32[256,128]{1,0:T(8,128)S(1)}, f32[256,128]{1,0:T(8,128)S(1)}, u32[]{:S(2)}, u32[]{:S(2)}) %collective-permute-start.5) | collective-permute-done | bytes 131104 | tf_op jit(solution)/shard_map/ppermute | solution.py:324
  46.0 1.6 collective-permute-start.7
  48.2 1.6 collective-permute-start.41
  49.8 4.0 %collective-permute-done.7 = f32[256,128]{1,0:T(8,128)S(1)} collective-permute-done((f32[256,128]{1,0:T(8,128)S(1)}, f32[256,128]{1,0:T(8,128)S(1)}, u32[]{:S(2)}, u32[]{:S(2)}) %collective-permute-start.7) | collective-permute-done | bytes 131104 | tf_op jit(solution)/shard_map/ppermute | solution.py:327
  57.4 3.8 %collective-permute-done.8 = f32[256,128]{1,0:T(8,128)S(1)} collective-permute-done((f32[256,128]{1,0:T(8,128)S(1)}, f32[256,128]{1,0:T(8,128)S(1)}, u32[]{:S(2)}, u32[]{:S(2)}) %collective-permute-start.8) | collective-permute-done | bytes 131104 | tf_op jit(solution)/shard_map/ppermute | solution.py:327
  64.3 3.8 %collective-permute-done.9 = f32[256,128]{1,0:T(8,128)S(1)} collective-permute-done((f32[256,128]{1,0:T(8,128)S(1)}, f32[256,128]{1,0:T(8,128)S(1)}, u32[]{:S(2)}, u32[]{:S(2)}) %collective-permute-start.9) | collective-permute-done | bytes 131104 | tf_op jit(solution)/shard_map/ppermute | solution.py:327
  69.7 2.7 %collective-permute-done.43 = f32[256,128]{1,0:T(8,128)S(1)} collective-permute-done((f32[256,128]{1,0:T(8,128)S(1)}, f32[256,128]{1,0:T(8,128)S(1)}, u32[]{:S(2)}, u32[]{:S(2)}) %collective-permute-start.43) | collective-permute-done | bytes 131104 | tf_op jit(solution)/shard_map/ppermute | solution.py:327
  76.6 3.3 %collective-permute-done.45.refs_2_.refs_10_ = f32[256,128]{1,0:T(8,128)S(1)} collective-permute-done((f32[256,128]{1,0:T(8,128)S(1)}, f32[256,128]{1,0:T(8,128)S(1)}, u32[]{:S(2)}, u32[]{:S(2)}) %collective-permute-start.45) | collective-permute-done | bytes 131104 | tf_op jit(solution)/shard_map/ppermute | solution.py:327
  81.5 2.0 collective-permute-done.13.refs_4_
  85.0 1.7 collective-permute-done.47.refs_4_.refs_12_
  88.5 1.7 collective-permute-done.15.refs_6_
  95.2 3.4 %copy-done.3 = f32[4,256,2048]{2,1,0:T(8,128)S(1)} copy-done((f32[4,256,2048]{2,1,0:T(8,128)S(1)}, f32[4,256,2048]{2,1,0:T(8,128)}, u32[]{:S(2)}) %copy-start.3) | copy-done | bytes 8388632
  98.6 3.2 %coef.2 = (f32[520,128]{1,0:T(8,128)S(1)}, f32[520,128]{1,0:T(8,128)S(1)}) custom-call(s32[8]{0:T(128)S(1)} %stack.46.where, s32[1]{0:T(128)} %bitcast.8.half, f32[1024,2048]{1,0:T(8,128)S(1)} %bitcast.16, f32[256,128]{1,0:T(8,128)S(1)} %add_add_fusion.11.refs_0_, f32[256,128]{1,0:T(8,128)S(1)} %collective-permute-done.10.refs_1_, ...), custom_call_target="tpu_custom_call" | custom-call | flops 2147483648 | bytes 8388608 | tf_op jit(solution)/shard_map/coef/pallas_call | solution.py:124
  101.9 3.2 %coef.3 = (f32[520,128]{1,0:T(8,128)S(1)}, f32[520,128]{1,0:T(8,128)S(1)}) custom-call(s32[8]{0:T(128)S(1)} %stack.46.where, s32[1]{0:T(128)} %bitcast.8.half, f32[1024,2048]{1,0:T(8,128)S(1)} %bitcast.17, f32[256,128]{1,0:T(8,128)S(1)} %add_add_fusion.5.refs_0_.refs_8_, f32[256,128]{1,0:T(8,128)S(1)} %collective-permute-done.44.refs_1_.refs_9_, ...), custom_call_target="tpu_custom_call" | custom-call | flops 2147483648 | bytes 8388608 | tf_op jit(solution)/shard_map/coef/pallas_call | solution.py:124
  107.2 6.9 %collective-permute-done.18 = f32[520,128]{1,0:T(8,128)S(1)} collective-permute-done((f32[520,128]{1,0:T(8,128)S(1)}, f32[520,128]{1,0:T(8,128)S(1)}, u32[]{:S(2)}, u32[]{:S(2)}) %collective-permute-start.18) | collective-permute-done | bytes 266272 | tf_op jit(solution)/shard_map/ppermute | solution.py:330
  115.7 1.7 gram.2
  119.7 2.1 collective-permute-done.52
  121.9 3.0 %collective-permute-done.68 = f32[128,256]{1,0:T(8,128)S(1)} collective-permute-done((f32[128,256]{1,0:T(8,128)S(1)}, f32[128,256]{1,0:T(8,128)S(1)}, u32[]{:S(2)}, u32[]{:S(2)}) %collective-permute-start.68) | collective-permute-done | bytes 131104 | tf_op jit(solution)/shard_map/ppermute | solution.py:330
  125.0 3.0 %panel.5 = (f32[256,128]{1,0:T(8,128)S(1)}, f32[256,128]{1,0:T(8,128)S(1)}, f32[256,128]{1,0:T(8,128)S(1)}, f32[256,128]{1,0:T(8,128)S(1)}, f32[256,128]{1,0:T(8...) custom-call(s32[8]{0:T(128)S(1)} %stack.47.where, ...), custom_call_target="tpu_custom_call" | custom-call | flops 2147483648 | bytes 8388608 | tf_op jit(solution)/shard_map/panel/pallas_call | solution.py:173
  130.1 3.3 %panel.7 = (f32[256,128]{1,0:T(8,128)S(1)}, f32[256,128]{1,0:T(8,128)S(1)}, f32[256,128]{1,0:T(8,128)S(1)}, f32[256,128]{1,0:T(8,128)S(1)}, f32[256,128]{1,0:T(8...) custom-call(s32[8]{0:T(128)S(1)} %stack.47.where, ...), custom_call_target="tpu_custom_call" | custom-call | flops 2147483648 | bytes 8388608 | tf_op jit(solution)/shard_map/panel/pallas_call | solution.py:173
  134.5 2.7 %collective-permute-done.22 = f32[256,128]{1,0:T(8,128)S(1)} collective-permute-done((f32[256,128]{1,0:T(8,128)S(1)}, f32[256,128]{1,0:T(8,128)S(1)}, u32[]{:S(2)}, u32[]{:S(2)}) %collective-permute-start.22) | collective-permute-done | bytes 131104 | tf_op jit(solution)/shard_map/ppermute | solution.py:324
  142.2 3.4 %collective-permute-done.24 = f32[256,128]{1,0:T(8,128)S(1)} collective-permute-done((f32[256,128]{1,0:T(8,128)S(1)}, f32[256,128]{1,0:T(8,128)S(1)}, u32[]{:S(2)}, u32[]{:S(2)}) %collective-permute-start.24) | collective-permute-done | bytes 131104 | tf_op jit(solution)/shard_map/ppermute | solution.py:327
  148.9 1.8 collective-permute-start.59
  150.7 3.7 %collective-permute-done.25 = f32[256,128]{1,0:T(8,128)S(1)} collective-permute-done((f32[256,128]{1,0:T(8,128)S(1)}, f32[256,128]{1,0:T(8,128)S(1)}, u32[]{:S(2)}, u32[]{:S(2)}) %collective-permute-start.25) | collective-permute-done | bytes 131104 | tf_op jit(solution)/shard_map/ppermute | solution.py:327
  155.6 1.6 collective-permute-done.59
  157.2 4.0 %collective-permute-done.26 = f32[256,128]{1,0:T(8,128)S(1)} collective-permute-done((f32[256,128]{1,0:T(8,128)S(1)}, f32[256,128]{1,0:T(8,128)S(1)}, u32[]{:S(2)}, u32[]{:S(2)}) %collective-permute-start.26) | collective-permute-done | bytes 131104 | tf_op jit(solution)/shard_map/ppermute | solution.py:327
  162.4 2.4 %collective-permute-done.60 = f32[256,128]{1,0:T(8,128)S(1)} collective-permute-done((f32[256,128]{1,0:T(8,128)S(1)}, f32[256,128]{1,0:T(8,128)S(1)}, u32[]{:S(2)}, u32[]{:S(2)}) %collective-permute-start.60) | collective-permute-done | bytes 131104 | tf_op jit(solution)/shard_map/ppermute | solution.py:327
  166.0 2.1 %collective-permute-done.28.refs_2_ = f32[256,128]{1,0:T(8,128)S(1)} collective-permute-done((f32[256,128]{1,0:T(8,128)S(1)}, f32[256,128]{1,0:T(8,128)S(1)}, u32[]{:S(2)}, u32[]{:S(2)}) %collective-permute-start.28) | collective-permute-done | bytes 131104 | tf_op jit(solution)/shard_map/ppermute | solution.py:327
  169.3 3.7 %collective-permute-done.62.refs_10_ = f32[256,128]{1,0:T(8,128)S(1)} collective-permute-done((f32[256,128]{1,0:T(8,128)S(1)}, f32[256,128]{1,0:T(8,128)S(1)}, u32[]{:S(2)}, u32[]{:S(2)}) %collective-permute-start.62) | collective-permute-done | bytes 131104 | tf_op jit(solution)/shard_map/ppermute | solution.py:327
  174.1 2.0 collective-permute-done.30.refs_4_
  176.2 1.9 collective-permute-done.63.refs_11_
  178.1 2.2 %collective-permute-done.64.refs_12_ = f32[256,128]{1,0:T(8,128)S(1)} collective-permute-done((f32[256,128]{1,0:T(8,128)S(1)}, f32[256,128]{1,0:T(8,128)S(1)}, u32[]{:S(2)}, u32[]{:S(2)}) %collective-permute-start.64) | collective-permute-done | bytes 131104 | tf_op jit(solution)/shard_map/ppermute | solution.py:327
  180.3 2.9 %mixing.2.before = f32[256,256]{1,0:T(8,128)S(1)} custom-call(s32[1]{0:T(128)} %bitcast.8.half, f32[128,256]{1,0:T(8,128)S(1)} %add.253.mine, f32[128,256]{1,0:T(8,128)S(1)} %collective-permute-done.69.partner), custom_call_target="tpu_custom_call" | custom-call | flops 1509949440 | bytes 786432 | tf_op jit(solution)/shard_map/mixing/pallas_call | solution.py:263
  192.5 1.7 gram.3
  196.9 4.4 %collective-permute-done.72 = f32[128,256]{1,0:T(8,128)S(1)} collective-permute-done((f32[128,256]{1,0:T(8,128)S(1)}, f32[128,256]{1,0:T(8,128)S(1)}, u32[]{:S(2)}, u32[]{:S(2)}) %collective-permute-start.72) | collective-permute-done | bytes 131104 | tf_op jit(solution)/shard_map/ppermute | solution.py:330
  202.7 3.8 %mixing.3 = f32[256,256]{1,0:T(8,128)S(1)} custom-call(s32[1]{0:T(128)} %bitcast.8.half, f32[128,256]{1,0:T(8,128)S(1)} %add.255.mine, f32[128,256]{1,0:T(8,128)S(1)} %collective-permute-done.73.partner, f32[256,256]{1,0:T(8,128)S(1)} %mixing.2.before, f32[8,128]{1,0:T(8,128)S(1)} %get-tuple-element.95.refs_0_, f32[8,128]{1,0:T(8,128)S(1)} %get-tuple-element.96.refs_1_), custom_call_target="tpu_custom_call" | custom-call | flops 1509949440 | bytes 786432 | tf_op jit(solution)/shard_map/mixing/pallas_call | solution.py:263
  206.5 3.0 %apply.1 = f32[2048,256]{1,0:T(8,128)} custom-call(s32[8]{0:T(128)S(1)} %stack.46.where, f32[256,256]{1,0:T(8,128)S(1)} %mixing.3, f32[256,128]{1,0:T(8,128)S(1)} %add_add_fusion.8.refs_0_, f32[256,128]{1,0:T(8,128)S(1)} %collective-permute-done.27.refs_1_, f32[256,128]{1,0:T(8,128)S(1)} %collective-permute-done.28.refs_2_, ...), custom_call_target="tpu_custom_call" | custom-call | flops 805306368 | bytes 4194304 | tf_op jit(solution)/shard_map/apply/pallas_call | solution.py:289
  (167 shorter events, 66.0 us)
Async XLA Ops:
  11.3 9.5 %collective-permute-start.1 = (f32[512,128]{1,0:T(8,128)S(1)}, f32[512,128]{1,0:T(8,128)S(1)}, u32[]{:S(2)}, u32[]{:S(2)}) collective-permute-start(f32[512,128]{1,0:T(8,128)S(1)} %add.216), channel_id=1, source_target_pairs={{0,2},{1,3},{2,0},{3,1},{4,6},{5,7},{6,4},{7,5},{8,10},{9,11},{10,... | collective-permute-start | bytes 786440 | tf_op jit(solution)/shard_map/ppermute | solution.py:330
  20.8 7.8 %collective-permute-start.35 = (f32[512,128]{1,0:T(8,128)S(1)}, f32[512,128]{1,0:T(8,128)S(1)}, u32[]{:S(2)}, u32[]{:S(2)}) collective-permute-start(f32[512,128]{1,0:T(8,128)S(1)} %get-tuple-element.99), channel_id=1, source_target_pairs={{0,2},{1,3},{2,0},{3,1},{4,6},{5,7},{6,4},{7,5},{8,10},{9,11},{10,... | collective-permute-start | bytes 786440 | tf_op jit(solution)/shard_map/ppermute | solution.py:330
  28.6 8.7 %collective-permute-start.36 = (f32[512,128]{1,0:T(8,128)S(1)}, f32[512,128]{1,0:T(8,128)S(1)}, u32[]{:S(2)}, u32[]{:S(2)}) collective-permute-start(f32[512,128]{1,0:T(8,128)S(1)} %add.235.mine_ref), channel_id=1, source_target_pairs={{0,1},{1,0},{2,3},{3,2},{4,5},{5,4},{6,7},{7,6},{8,9},{9,8},{10,11... | collective-permute-start | bytes 786440 | tf_op jit(solution)/shard_map/ppermute | solution.py:330
  35.3 14.5 %collective-permute-start.3 = (f32[256,128]{1,0:T(8,128)S(1)}, f32[256,128]{1,0:T(8,128)S(1)}, u32[]{:S(2)}, u32[]{:S(2)}) collective-permute-start(f32[256,128]{1,0:T(8,128)S(1)} %get-tuple-element.54), channel_id=1, source_target_pairs={{0,4},{4,0},{8,12},{12,8},{16,20},{20,16},{24,28},{28,24},{1,5},{5... | collective-permute-start | bytes 393224 | tf_op jit(solution)/shard_map/ppermute | solution.py:324
  36.8 7.6 %collective-permute-start.5 = (f32[256,128]{1,0:T(8,128)S(1)}, f32[256,128]{1,0:T(8,128)S(1)}, u32[]{:S(2)}, u32[]{:S(2)}) collective-permute-start(f32[256,128]{1,0:T(8,128)S(1)} %get-tuple-element.57), channel_id=1, source_target_pairs={{0,4},{4,0},{8,12},{12,8},{16,20},{20,16},{24,28},{28,24},{1,5},{5... | collective-permute-start | bytes 393224 | tf_op jit(solution)/shard_map/ppermute | solution.py:324
  40.4 7.7 %collective-permute-start.39 = (f32[256,128]{1,0:T(8,128)S(1)}, f32[256,128]{1,0:T(8,128)S(1)}, u32[]{:S(2)}, u32[]{:S(2)}) collective-permute-start(f32[256,128]{1,0:T(8,128)S(1)} %get-tuple-element.77), channel_id=1, source_target_pairs={{0,4},{4,0},{8,12},{12,8},{16,20},{20,16},{24,28},{28,24},{1,5},{5... | collective-permute-start | bytes 393224 | tf_op jit(solution)/shard_map/ppermute | solution.py:324
  44.5 12.9 %collective-permute-start.6 = (f32[256,128]{1,0:T(8,128)S(1)}, f32[256,128]{1,0:T(8,128)S(1)}, u32[]{:S(2)}, u32[]{:S(2)}) collective-permute-start(f32[256,128]{1,0:T(8,128)S(1)} %get-tuple-element.111), channel_id=1, source_target_pairs={{0,4},{4,0},{8,12},{12,8},{16,20},{20,16},{24,28},{28,24},{1,5},{5... | collective-permute-start | bytes 393224 | tf_op jit(solution)/shard_map/ppermute | solution.py:324
  46.0 7.7 %collective-permute-start.7 = (f32[256,128]{1,0:T(8,128)S(1)}, f32[256,128]{1,0:T(8,128)S(1)}, u32[]{:S(2)}, u32[]{:S(2)}) collective-permute-start(f32[256,128]{1,0:T(8,128)S(1)} %get-tuple-element.112), channel_id=1, source_target_pairs={{0,8},{4,12},{8,16},{12,20},{16,24},{20,28},{24,0},{28,4},{1,9},{5... | collective-permute-start | bytes 393224 | tf_op jit(solution)/shard_map/ppermute | solution.py:327
  48.2 7.8 %collective-permute-start.41 = (f32[256,128]{1,0:T(8,128)S(1)}, f32[256,128]{1,0:T(8,128)S(1)}, u32[]{:S(2)}, u32[]{:S(2)}) collective-permute-start(f32[256,128]{1,0:T(8,128)S(1)} %get-tuple-element.116), channel_id=1, source_target_pairs={{0,8},{4,12},{8,16},{12,20},{16,24},{20,28},{24,0},{28,4},{1,9},{5... | collective-permute-start | bytes 393224 | tf_op jit(solution)/shard_map/ppermute | solution.py:327
  53.8 10.5 %collective-permute-start.4 = (f32[256,128]{1,0:T(8,128)S(1)}, f32[256,128]{1,0:T(8,128)S(1)}, u32[]{:S(2)}, u32[]{:S(2)}) collective-permute-start(f32[256,128]{1,0:T(8,128)S(1)} %get-tuple-element.109), channel_id=1, source_target_pairs={{0,4},{4,0},{8,12},{12,8},{16,20},{20,16},{24,28},{28,24},{1,5},{5... | collective-permute-start | bytes 393224 | tf_op jit(solution)/shard_map/ppermute | solution.py:324
  54.4 6.8 %collective-permute-start.8 = (f32[256,128]{1,0:T(8,128)S(1)}, f32[256,128]{1,0:T(8,128)S(1)}, u32[]{:S(2)}, u32[]{:S(2)}) collective-permute-start(f32[256,128]{1,0:T(8,128)S(1)} %get-tuple-element.110), channel_id=1, source_target_pairs={{0,8},{4,12},{8,16},{12,20},{16,24},{20,28},{24,0},{28,4},{1,9},{5... | collective-permute-start | bytes 393224 | tf_op jit(solution)/shard_map/ppermute | solution.py:327
  54.4 8.5 %collective-permute-start.40 = (f32[256,128]{1,0:T(8,128)S(1)}, f32[256,128]{1,0:T(8,128)S(1)}, u32[]{:S(2)}, u32[]{:S(2)}) collective-permute-start(f32[256,128]{1,0:T(8,128)S(1)} %get-tuple-element.115), channel_id=1, source_target_pairs={{0,4},{4,0},{8,12},{12,8},{16,20},{20,16},{24,28},{28,24},{1,5},{5... | collective-permute-start | bytes 393224 | tf_op jit(solution)/shard_map/ppermute | solution.py:324
  56.0 8.2 %collective-permute-start.42 = (f32[256,128]{1,0:T(8,128)S(1)}, f32[256,128]{1,0:T(8,128)S(1)}, u32[]{:S(2)}, u32[]{:S(2)}) collective-permute-start(f32[256,128]{1,0:T(8,128)S(1)} %get-tuple-element.114), channel_id=1, source_target_pairs={{0,8},{4,12},{8,16},{12,20},{16,24},{20,28},{24,0},{28,4},{1,9},{5... | collective-permute-start | bytes 393224 | tf_op jit(solution)/shard_map/ppermute | solution.py:327
  61.3 6.8 %collective-permute-start.9 = (f32[256,128]{1,0:T(8,128)S(1)}, f32[256,128]{1,0:T(8,128)S(1)}, u32[]{:S(2)}, u32[]{:S(2)}) collective-permute-start(f32[256,128]{1,0:T(8,128)S(1)} %add_add_fusion.10), channel_id=1, source_target_pairs={{0,8},{4,12},{8,16},{12,20},{16,24},{20,28},{24,0},{28,4},{1,9},{5... | collective-permute-start | bytes 393224 | tf_op jit(solution)/shard_map/ppermute | solution.py:327
  61.3 8.4 %collective-permute-start.38 = (f32[256,128]{1,0:T(8,128)S(1)}, f32[256,128]{1,0:T(8,128)S(1)}, u32[]{:S(2)}, u32[]{:S(2)}) collective-permute-start(f32[256,128]{1,0:T(8,128)S(1)} %get-tuple-element.113), channel_id=1, source_target_pairs={{0,4},{4,0},{8,12},{12,8},{16,20},{20,16},{24,28},{28,24},{1,5},{5... | collective-permute-start | bytes 393224 | tf_op jit(solution)/shard_map/ppermute | solution.py:324
  64.2 8.2 %collective-permute-start.43 = (f32[256,128]{1,0:T(8,128)S(1)}, f32[256,128]{1,0:T(8,128)S(1)}, u32[]{:S(2)}, u32[]{:S(2)}) collective-permute-start(f32[256,128]{1,0:T(8,128)S(1)} %add_add_fusion.4), channel_id=1, source_target_pairs={{0,8},{4,12},{8,16},{12,20},{16,24},{20,28},{24,0},{28,4},{1,9},{5... | collective-permute-start | bytes 393224 | tf_op jit(solution)/shard_map/ppermute | solution.py:327
  68.1 7.3 %collective-permute-start.11 = (f32[256,128]{1,0:T(8,128)S(1)}, f32[256,128]{1,0:T(8,128)S(1)}, u32[]{:S(2)}, u32[]{:S(2)}) collective-permute-start(f32[256,128]{1,0:T(8,128)S(1)} %add_add_fusion.11.refs_0_), channel_id=1, source_target_pairs={{0,8},{4,12},{8,16},{12,20},{16,24},{20,28},{24,0},{28,4},{1,9},{5... | collective-permute-start | bytes 393224 | tf_op jit(solution)/shard_map/ppermute | solution.py:327
  68.2 7.3 %collective-permute-start.10 = (f32[256,128]{1,0:T(8,128)S(1)}, f32[256,128]{1,0:T(8,128)S(1)}, u32[]{:S(2)}, u32[]{:S(2)}) collective-permute-start(f32[256,128]{1,0:T(8,128)S(1)} %add_add_fusion.11.refs_0_), channel_id=1, source_target_pairs={{0,4},{4,0},{8,12},{12,8},{16,20},{20,16},{24,28},{28,24},{1,5},{5... | collective-permute-start | bytes 393224 | tf_op jit(solution)/shard_map/ppermute | solution.py:324
  72.5 7.4 %collective-permute-start.45 = (f32[256,128]{1,0:T(8,128)S(1)}, f32[256,128]{1,0:T(8,128)S(1)}, u32[]{:S(2)}, u32[]{:S(2)}) collective-permute-start(f32[256,128]{1,0:T(8,128)S(1)} %add_add_fusion.5.refs_0_.refs_8_), channel_id=1, source_target_pairs={{0,8},{4,12},{8,16},{12,20},{16,24},{20,28},{24,0},{28,4},{1,9},{5... | collective-permute-start | bytes 393224 | tf_op jit(solution)/shard_map/ppermute | solution.py:327
  72.5 7.3 %collective-permute-start.44 = (f32[256,128]{1,0:T(8,128)S(1)}, f32[256,128]{1,0:T(8,128)S(1)}, u32[]{:S(2)}, u32[]{:S(2)}) collective-permute-start(f32[256,128]{1,0:T(8,128)S(1)} %add_add_fusion.5.refs_0_.refs_8_), channel_id=1, source_target_pairs={{0,4},{4,0},{8,12},{12,8},{16,20},{20,16},{24,28},{28,24},{1,5},{5... | collective-permute-start | bytes 393224 | tf_op jit(solution)/shard_map/ppermute | solution.py:324
  75.5 8.0 %collective-permute-start.13 = (f32[256,128]{1,0:T(8,128)S(1)}, f32[256,128]{1,0:T(8,128)S(1)}, u32[]{:S(2)}, u32[]{:S(2)}) collective-permute-start(f32[256,128]{1,0:T(8,128)S(1)} %broadcast_select_fusion.13), channel_id=1, source_target_pairs={{0,8},{4,12},{8,16},{12,20},{16,24},{20,28},{24,0},{28,4},{1,9},{5... | collective-permute-start | bytes 393224 | tf_op jit(solution)/shard_map/ppermute | solution.py:327
  79.9 6.8 %collective-permute-start.47 = (f32[256,128]{1,0:T(8,128)S(1)}, f32[256,128]{1,0:T(8,128)S(1)}, u32[]{:S(2)}, u32[]{:S(2)}) collective-permute-start(f32[256,128]{1,0:T(8,128)S(1)} %broadcast_select_fusion.5), channel_id=1, source_target_pairs={{0,8},{4,12},{8,16},{12,20},{16,24},{20,28},{24,0},{28,4},{1,9},{5... | collective-permute-start | bytes 393224 | tf_op jit(solution)/shard_map/ppermute | solution.py:327
  83.5 6.8 %collective-permute-start.15 = (f32[256,128]{1,0:T(8,128)S(1)}, f32[256,128]{1,0:T(8,128)S(1)}, u32[]{:S(2)}, u32[]{:S(2)}) collective-permute-start(f32[256,128]{1,0:T(8,128)S(1)} %broadcast_select_fusion.12), channel_id=1, source_target_pairs={{0,8},{4,12},{8,16},{12,20},{16,24},{20,28},{24,0},{28,4},{1,9},{5... | collective-permute-start | bytes 393224 | tf_op jit(solution)/shard_map/ppermute | solution.py:327
  86.7 7.0 %collective-permute-start.49 = (f32[256,128]{1,0:T(8,128)S(1)}, f32[256,128]{1,0:T(8,128)S(1)}, u32[]{:S(2)}, u32[]{:S(2)}) collective-permute-start(f32[256,128]{1,0:T(8,128)S(1)} %broadcast_select_fusion.4), channel_id=1, source_target_pairs={{0,8},{4,12},{8,16},{12,20},{16,24},{20,28},{24,0},{28,4},{1,9},{5... | collective-permute-start | bytes 393224 | tf_op jit(solution)/shard_map/ppermute | solution.py:327
  87.2 8.0 %collective-permute-start.14 = (f32[256,128]{1,0:T(8,128)S(1)}, f32[256,128]{1,0:T(8,128)S(1)}, u32[]{:S(2)}, u32[]{:S(2)}) collective-permute-start(f32[256,128]{1,0:T(8,128)S(1)} %collective-permute-done.13.refs_4_), channel_id=1, source_target_pairs={{0,4},{4,0},{8,12},{12,8},{16,20},{20,16},{24,28},{28,24},{1,5},{5... | collective-permute-start | bytes 393224 | tf_op jit(solution)/shard_map/ppermute | solution.py:324
  91.3 10.6 %collective-permute-start.48 = (f32[256,128]{1,0:T(8,128)S(1)}, f32[256,128]{1,0:T(8,128)S(1)}, u32[]{:S(2)}, u32[]{:S(2)}) collective-permute-start(f32[256,128]{1,0:T(8,128)S(1)} %collective-permute-done.47.refs_4_.refs_12_), channel_id=1, source_target_pairs={{0,4},{4,0},{8,12},{12,8},{16,20},{20,16},{24,28},{28,24},{1,5},{5... | collective-permute-start | bytes 393224 | tf_op jit(solution)/shard_map/ppermute | solution.py:324
  93.7 8.2 %collective-permute-start.50 = (f32[256,128]{1,0:T(8,128)S(1)}, f32[256,128]{1,0:T(8,128)S(1)}, u32[]{:S(2)}, u32[]{:S(2)}) collective-permute-start(f32[256,128]{1,0:T(8,128)S(1)} %collective-permute-done.49.refs_6_.refs_14_), channel_id=1, source_target_pairs={{0,4},{4,0},{8,12},{12,8},{16,20},{20,16},{24,28},{28,24},{1,5},{5... | collective-permute-start | bytes 393224 | tf_op jit(solution)/shard_map/ppermute | solution.py:324
  105.7 8.4 %collective-permute-start.18 = (f32[520,128]{1,0:T(8,128)S(1)}, f32[520,128]{1,0:T(8,128)S(1)}, u32[]{:S(2)}, u32[]{:S(2)}) collective-permute-start(f32[520,128]{1,0:T(8,128)S(1)} %add.225), channel_id=1, source_target_pairs={{0,2},{1,3},{2,0},{3,1},{4,6},{5,7},{6,4},{7,5},{8,10},{9,11},{10,... | collective-permute-start | bytes 798728 | tf_op jit(solution)/shard_map/ppermute | solution.py:330
  114.2 7.6 %collective-permute-start.52 = (f32[520,128]{1,0:T(8,128)S(1)}, f32[520,128]{1,0:T(8,128)S(1)}, u32[]{:S(2)}, u32[]{:S(2)}) collective-permute-start(f32[520,128]{1,0:T(8,128)S(1)} %get-tuple-element.97), channel_id=1, source_target_pairs={{0,2},{1,3},{2,0},{3,1},{4,6},{5,7},{6,4},{7,5},{8,10},{9,11},{10,... | collective-permute-start | bytes 798728 | tf_op jit(solution)/shard_map/ppermute | solution.py:330
  115.7 9.3 %collective-permute-start.19 = (f32[520,128]{1,0:T(8,128)S(1)}, f32[520,128]{1,0:T(8,128)S(1)}, u32[]{:S(2)}, u32[]{:S(2)}) collective-permute-start(f32[520,128]{1,0:T(8,128)S(1)} %get-tuple-element.98.mine_ref), channel_id=1, source_target_pairs={{0,1},{1,0},{2,3},{3,2},{4,5},{5,4},{6,7},{7,6},{8,9},{9,8},{10,11... | collective-permute-start | bytes 798728 | tf_op jit(solution)/shard_map/ppermute | solution.py:330
  121.8 8.3 %collective-permute-start.53 = (f32[520,128]{1,0:T(8,128)S(1)}, f32[520,128]{1,0:T(8,128)S(1)}, u32[]{:S(2)}, u32[]{:S(2)}) collective-permute-start(f32[520,128]{1,0:T(8,128)S(1)} %add.244.mine_ref), channel_id=1, source_target_pairs={{0,1},{1,0},{2,3},{3,2},{4,5},{5,4},{6,7},{7,6},{8,9},{9,8},{10,11... | collective-permute-start | bytes 798728 | tf_op jit(solution)/shard_map/ppermute | solution.py:330
  124.9 55.4 %collective-permute-start.69 = (f32[128,256]{1,0:T(8,128)S(1)}, f32[128,256]{1,0:T(8,128)S(1)}, u32[]{:S(2)}, u32[]{:S(2)}) collective-permute-start(f32[128,256]{1,0:T(8,128)S(1)} %add.253.mine), channel_id=1, source_target_pairs={{0,1},{1,0},{2,3},{3,2},{4,5},{5,4},{6,7},{7,6},{8,9},{9,8},{10,11... | collective-permute-start | bytes 393224 | tf_op jit(solution)/shard_map/ppermute | solution.py:330
  128.0 13.0 %collective-permute-start.20 = (f32[256,128]{1,0:T(8,128)S(1)}, f32[256,128]{1,0:T(8,128)S(1)}, u32[]{:S(2)}, u32[]{:S(2)}) collective-permute-start(f32[256,128]{1,0:T(8,128)S(1)} %get-tuple-element.64), channel_id=1, source_target_pairs={{0,4},{4,0},{8,12},{12,8},{16,20},{20,16},{24,28},{28,24},{1,5},{5... | collective-permute-start | bytes 393224 | tf_op jit(solution)/shard_map/ppermute | solution.py:324
  129.1 8.1 %collective-permute-start.22 = (f32[256,128]{1,0:T(8,128)S(1)}, f32[256,128]{1,0:T(8,128)S(1)}, u32[]{:S(2)}, u32[]{:S(2)}) collective-permute-start(f32[256,128]{1,0:T(8,128)S(1)} %get-tuple-element.67), channel_id=1, source_target_pairs={{0,4},{4,0},{8,12},{12,8},{16,20},{20,16},{24,28},{28,24},{1,5},{5... | collective-permute-start | bytes 393224 | tf_op jit(solution)/shard_map/ppermute | solution.py:324
  137.2 11.7 %collective-permute-start.23 = (f32[256,128]{1,0:T(8,128)S(1)}, f32[256,128]{1,0:T(8,128)S(1)}, u32[]{:S(2)}, u32[]{:S(2)}) collective-permute-start(f32[256,128]{1,0:T(8,128)S(1)} %get-tuple-element.107), channel_id=1, source_target_pairs={{0,4},{4,0},{8,12},{12,8},{16,20},{20,16},{24,28},{28,24},{1,5},{5... | collective-permute-start | bytes 393224 | tf_op jit(solution)/shard_map/ppermute | solution.py:324
  138.3 7.3 %collective-permute-start.24 = (f32[256,128]{1,0:T(8,128)S(1)}, f32[256,128]{1,0:T(8,128)S(1)}, u32[]{:S(2)}, u32[]{:S(2)}) collective-permute-start(f32[256,128]{1,0:T(8,128)S(1)} %get-tuple-element.108), channel_id=1, source_target_pairs={{0,8},{4,12},{8,16},{12,20},{16,24},{20,28},{24,0},{28,4},{1,9},{5... | collective-permute-start | bytes 393224 | tf_op jit(solution)/shard_map/ppermute | solution.py:327
  141.1 6.8 %collective-permute-start.58 = (f32[256,128]{1,0:T(8,128)S(1)}, f32[256,128]{1,0:T(8,128)S(1)}, u32[]{:S(2)}, u32[]{:S(2)}) collective-permute-start(f32[256,128]{1,0:T(8,128)S(1)} %get-tuple-element.104), channel_id=1, source_target_pairs={{0,8},{4,12},{8,16},{12,20},{16,24},{20,28},{24,0},{28,4},{1,9},{5... | collective-permute-start | bytes 393224 | tf_op jit(solution)/shard_map/ppermute | solution.py:327
  145.7 11.6 %collective-permute-start.21 = (f32[256,128]{1,0:T(8,128)S(1)}, f32[256,128]{1,0:T(8,128)S(1)}, u32[]{:S(2)}, u32[]{:S(2)}) collective-permute-start(f32[256,128]{1,0:T(8,128)S(1)} %get-tuple-element.105), channel_id=1, source_target_pairs={{0,4},{4,0},{8,12},{12,8},{16,20},{20,16},{24,28},{28,24},{1,5},{5... | collective-permute-start | bytes 393224 | tf_op jit(solution)/shard_map/ppermute | solution.py:324
  146.8 7.6 %collective-permute-start.25 = (f32[256,128]{1,0:T(8,128)S(1)}, f32[256,128]{1,0:T(8,128)S(1)}, u32[]{:S(2)}, u32[]{:S(2)}) collective-permute-start(f32[256,128]{1,0:T(8,128)S(1)} %get-tuple-element.106), channel_id=1, source_target_pairs={{0,8},{4,12},{8,16},{12,20},{16,24},{20,28},{24,0},{28,4},{1,9},{5... | collective-permute-start | bytes 393224 | tf_op jit(solution)/shard_map/ppermute | solution.py:327
  148.9 8.2 %collective-permute-start.59 = (f32[256,128]{1,0:T(8,128)S(1)}, f32[256,128]{1,0:T(8,128)S(1)}, u32[]{:S(2)}, u32[]{:S(2)}) collective-permute-start(f32[256,128]{1,0:T(8,128)S(1)} %get-tuple-element.102), channel_id=1, source_target_pairs={{0,8},{4,12},{8,16},{12,20},{16,24},{20,28},{24,0},{28,4},{1,9},{5... | collective-permute-start | bytes 393224 | tf_op jit(solution)/shard_map/ppermute | solution.py:327
  154.4 6.8 %collective-permute-start.26 = (f32[256,128]{1,0:T(8,128)S(1)}, f32[256,128]{1,0:T(8,128)S(1)}, u32[]{:S(2)}, u32[]{:S(2)}) collective-permute-start(f32[256,128]{1,0:T(8,128)S(1)} %add_add_fusion.7), channel_id=1, source_target_pairs={{0,8},{4,12},{8,16},{12,20},{16,24},{20,28},{24,0},{28,4},{1,9},{5... | collective-permute-start | bytes 393224 | tf_op jit(solution)/shard_map/ppermute | solution.py:327
  154.5 7.9 %collective-permute-start.55 = (f32[256,128]{1,0:T(8,128)S(1)}, f32[256,128]{1,0:T(8,128)S(1)}, u32[]{:S(2)}, u32[]{:S(2)}) collective-permute-start(f32[256,128]{1,0:T(8,128)S(1)} %get-tuple-element.101), channel_id=1, source_target_pairs={{0,4},{4,0},{8,12},{12,8},{16,20},{20,16},{24,28},{28,24},{1,5},{5... | collective-permute-start | bytes 393224 | tf_op jit(solution)/shard_map/ppermute | solution.py:324
  157.2 7.6 %collective-permute-start.60 = (f32[256,128]{1,0:T(8,128)S(1)}, f32[256,128]{1,0:T(8,128)S(1)}, u32[]{:S(2)}, u32[]{:S(2)}) collective-permute-start(f32[256,128]{1,0:T(8,128)S(1)} %add_add_fusion.1), channel_id=1, source_target_pairs={{0,8},{4,12},{8,16},{12,20},{16,24},{20,28},{24,0},{28,4},{1,9},{5... | collective-permute-start | bytes 393224 | tf_op jit(solution)/shard_map/ppermute | solution.py:327
  164.8 8.1 %collective-permute-start.62 = (f32[256,128]{1,0:T(8,128)S(1)}, f32[256,128]{1,0:T(8,128)S(1)}, u32[]{:S(2)}, u32[]{:S(2)}) collective-permute-start(f32[256,128]{1,0:T(8,128)S(1)} %add_add_fusion.2.refs_8_), channel_id=1, source_target_pairs={{0,8},{4,12},{8,16},{12,20},{16,24},{20,28},{24,0},{28,4},{1,9},{5... | collective-permute-start | bytes 393224 | tf_op jit(solution)/shard_map/ppermute | solution.py:327
  164.9 8.1 %collective-permute-start.61 = (f32[256,128]{1,0:T(8,128)S(1)}, f32[256,128]{1,0:T(8,128)S(1)}, u32[]{:S(2)}, u32[]{:S(2)}) collective-permute-start(f32[256,128]{1,0:T(8,128)S(1)} %add_add_fusion.2.refs_8_), channel_id=1, source_target_pairs={{0,4},{4,0},{8,12},{12,8},{16,20},{20,16},{24,28},{28,24},{1,5},{5... | collective-permute-start | bytes 393224 | tf_op jit(solution)/shard_map/ppermute | solution.py:324
  168.1 8.0 %collective-permute-start.30 = (f32[256,128]{1,0:T(8,128)S(1)}, f32[256,128]{1,0:T(8,128)S(1)}, u32[]{:S(2)}, u32[]{:S(2)}) collective-permute-start(f32[256,128]{1,0:T(8,128)S(1)} %broadcast_select_fusion.9), channel_id=1, source_target_pairs={{0,8},{4,12},{8,16},{12,20},{16,24},{20,28},{24,0},{28,4},{1,9},{5... | collective-permute-start | bytes 393224 | tf_op jit(solution)/shard_map/ppermute | solution.py:327
  173.0 7.3 %collective-permute-start.64 = (f32[256,128]{1,0:T(8,128)S(1)}, f32[256,128]{1,0:T(8,128)S(1)}, u32[]{:S(2)}, u32[]{:S(2)}) collective-permute-start(f32[256,128]{1,0:T(8,128)S(1)} %broadcast_select_fusion.1), channel_id=1, source_target_pairs={{0,8},{4,12},{8,16},{12,20},{16,24},{20,28},{24,0},{28,4},{1,9},{5... | collective-permute-start | bytes 393224 | tf_op jit(solution)/shard_map/ppermute | solution.py:327
  176.1 8.2 %collective-permute-start.32 = (f32[256,128]{1,0:T(8,128)S(1)}, f32[256,128]{1,0:T(8,128)S(1)}, u32[]{:S(2)}, u32[]{:S(2)}) collective-permute-start(f32[256,128]{1,0:T(8,128)S(1)} %broadcast_select_fusion.8), channel_id=1, source_target_pairs={{0,8},{4,12},{8,16},{12,20},{16,24},{20,28},{24,0},{28,4},{1,9},{5... | collective-permute-start | bytes 393224 | tf_op jit(solution)/shard_map/ppermute | solution.py:327
  (34 other events, 203.4 us)

commit v4 on v3

--- a/solution.py
+++ b/solution.py
@@ -14,14 +14,14 @@
 EXTRA = 8
 SLICES = 4
 LARGE = 16
-RING_SCATTER = True
-RING_GATHER = True
-CHAIN = 2
-SCATTER_CHAIN = 2
-ORDER_FEAT = 1
-ORDER_SCATTER = 0
-ORDER_GATHER = 0
-JOIN = 1
+HOLD = 1
+FIRST_OUT = 2
+NEXT_OUT = 2
+NEXT_IN = 2
+PANELS_FIRST = 0
+SWAP_GATE = 1
+IN_TURN = 1
+LATE_GRAM = 1
 WHOLE = pl.BlockSpec(memory_space=pltpu.VMEM)
 SCALARS = pl.BlockSpec(memory_space=pltpu.SMEM)
 F32 = jnp.float32
@@ -100,11 +100,14 @@
     )(half, probes, a_rows, *also)
 
 
-def coef_kernel(blocks, where, half, a_ref, *refs):
-    inputs, outputs, (pair, total, sums) = refs[:blocks], refs[blocks:-3], refs[-3:]
-    rows, columns = inputs[0].shape
-    for k in range(blocks):
-        value = inputs[k][...]
+def pieces(inputs, rows):
+    return [ref[i : i + rows, :] for ref in inputs for i in range(0, ref.shape[0], rows)]
+
+
+def coef_kernel(rows, where, half, a_ref, *refs):
+    inputs, outputs, (pair, total, sums) = refs[:-5], refs[-5:-3], refs[-3:]
+    columns = inputs[0].shape[1]
+    for k, value in enumerate(pieces(inputs, rows)):
         high, low = split(value)
         at = pl.ds(pl.multiple_of(where[k] * rows, rows), rows)
         pair[at, :columns] = high
@@ -122,14 +125,14 @@
     total, depth = a_rows.shape
     columns = basis[0].shape[1]
     return pl.pallas_call(
-        functools.partial(coef_kernel, len(basis)),
+        functools.partial(coef_kernel, depth // where.shape[0]),
         in_specs=[SCALARS, SCALARS, WHOLE] + [WHOLE] * len(basis),
         out_specs=[WHOLE] * 2,
         out_shape=[jax.ShapeDtypeStruct((total // 2 + EXTRA, columns), F32)] * 2,
         scratch_shapes=[
             pltpu.VMEM((depth, 2 * columns), BF16),
             pltpu.VMEM((total, columns), F32),
-            pltpu.VMEM((len(basis), columns), F32),
+            pltpu.VMEM((where.shape[0], columns), F32),
         ],
         compiler_params=params(LARGE),
         cost_estimate=cost(8 * total * depth * columns, 4 * total * depth),
@@ -184,12 +187,13 @@
     )(where, half, ranks, b_factors, mine, partner)
 
 
-def gram_kernel(blocks, where, half, *refs):
-    inputs, (other, mine), (highs, lows) = refs[: GROUPS * blocks], refs[-4:-2], refs[-2:]
-    rows, columns = inputs[0].shape
+def gram_kernel(rows, where, half, *refs):
+    inputs, (other, mine), (highs, lows) = refs[:-4], refs[-4:-2], refs[-2:]
+    columns = inputs[0].shape[1]
+    each = len(inputs) // GROUPS
     for g in range(GROUPS):
-        for k in range(blocks):
-            high, low = split(inputs[g * blocks + k][...])
+        for k, value in enumerate(pieces(inputs[g * each : (g + 1) * each], rows)):
+            high, low = split(value)
             at = pl.ds(pl.multiple_of(where[k] * rows, rows), rows)
             highs[at, g * columns : (g + 1) * columns] = high
             lows[at, g * columns : (g + 1) * columns] = low
@@ -204,12 +208,12 @@
 
 
 def gram_terms(panels, where, half):
-    blocks = len(panels[0])
+    blocks = where.shape[0]
     rows, columns = panels[0][0].shape
     size = GROUPS * columns
     return pl.pallas_call(
-        functools.partial(gram_kernel, blocks),
-        in_specs=[SCALARS, SCALARS] + [WHOLE] * (GROUPS * blocks),
+        functools.partial(gram_kernel, rows),
+        in_specs=[SCALARS, SCALARS] + [WHOLE] * sum(len(panel) for panel in panels),
         out_specs=[WHOLE] * 2,
         out_shape=[jax.ShapeDtypeStruct((size // 2, size), F32)] * 2,
         scratch_shapes=[pltpu.VMEM((blocks * rows, size), BF16)] * 2,
@@ -271,26 +275,33 @@
     )(*operands)
 
 
-def apply_kernel(blocks, where, mixing, *refs):
-    inputs, (out,) = refs[: GROUPS * blocks], refs[GROUPS * blocks :]
-    rows, columns = inputs[0].shape
+def apply_kernel(rows, where, mixing, *refs):
+    inputs, (out, held, sems) = refs[:-3], refs[-3:]
+    each = len(inputs) // GROUPS
     high, low = split(mixing[...])
-    for k in range(blocks):
-        value = jnp.concatenate([inputs[g * blocks + k][...] for g in range(GROUPS)], axis=1)
+    copies = []
+    values = [pieces(inputs[g * each : (g + 1) * each], rows) for g in range(GROUPS)]
+    for k, value in enumerate(zip(*values)):
+        value = jnp.concatenate(value, axis=1)
         value_high, value_low = split(value)
+        held[k] = dot(value_high, high) + (dot(value_high, low) + dot(value_low, high))
         at = pl.ds(pl.multiple_of(where[k] * rows, rows), rows)
-        out[at, :] = dot(value_high, high) + (dot(value_high, low) + dot(value_low, high))
+        copies.append(pltpu.make_async_copy(held.at[k], out.at[at], sems.at[k]))
+        copies[k].start()
+    for copy in copies:
+        copy.wait()
 
 
 def apply_mixing(panels, where, mixing):
-    blocks = len(panels[0])
+    blocks = where.shape[0]
     rows, columns = panels[0][0].shape
     size = GROUPS * columns
     return pl.pallas_call(
-        functools.partial(apply_kernel, blocks),
-        in_specs=[SCALARS] + [WHOLE] * (1 + GROUPS * blocks),
-        out_specs=WHOLE,
+        functools.partial(apply_kernel, rows),
+        in_specs=[SCALARS] + [WHOLE] * (1 + sum(len(panel) for panel in panels)),
+        out_specs=pl.BlockSpec(memory_space=pl.ANY),
         out_shape=jax.ShapeDtypeStruct((blocks * rows, size), F32),
+        scratch_shapes=[pltpu.VMEM((blocks, rows, size), F32), pltpu.SemaphoreType.DMA((blocks,))],
         compiler_params=params(LARGE),
         cost_estimate=cost(6 * blocks * rows * size * size, 8 * blocks * rows * size),
         name="apply",
@@ -306,30 +317,32 @@
         cohort = lax.axis_index("cohort")
         place, side = cohort // 2, cohort % 2
         self.half = (lax.axis_index("feat") % 2).astype(jnp.int32).reshape(1)
-        shifts = sorted(range(1, self.places), key=lambda d: (-min(d, self.places - d), d)) + [0]
-        self.out_shifts = list(range(-1, -self.places, -1)) + [0] if RING_SCATTER else shifts
-        self.in_shifts = list(range(0, -self.places, -1)) if RING_GATHER else [-d for d in shifts[::-1]]
-
         def block(shift, side):
             return lax.rem(place + shift + self.places, self.places) * 2 + side
 
-        self.sendings = [self.out_shifts[i : i + JOIN] for i in range(0, self.places, JOIN)]
-        self.sizes = [len(s) for s in self.sendings] + [1] * self.places
-        self.scatter_order = jnp.stack(
-            [block(d, 1 - side) for d in self.out_shifts] + [block(d, side) for d in self.out_shifts]
-        ).astype(jnp.int32)
-        self.gather_order = jnp.stack([block(d, s) for d in self.in_shifts for s in (side, 1 - side)]).astype(jnp.int32)
+        ahead = self.places // 2
+        self.shifts = sorted(range(ahead + 1 - self.places, ahead + 1), key=lambda d: (abs(d), -d))
+        outward, inward = self.shifts[::-1], [-d for d in self.shifts]
+        self.scatter_order = jnp.stack([block(d, s) for s in (1 - side, side) for d in outward]).astype(jnp.int32)
+        self.gather_order = jnp.stack([block(d, s) for s in (side, 1 - side) for d in inward]).astype(jnp.int32)
+        places = range(self.places)
+        cuts = [0] + list(places)[FIRST_OUT :: NEXT_OUT] + [self.places]
+        self.outs = [b - a for a, b in zip(cuts, cuts[1:])]
+        self.sizes = self.outs + [1] * self.places
+        cuts = [0] + list(places)[1::NEXT_IN] + [self.places]
+        self.ins = list(zip(cuts, cuts[1:]))
 
     def across(self, block):
         return lax.ppermute(block, "cohort", [(i, i ^ 1) for i in range(self.cohorts)])
 
-    def along(self, block, shift):
-        return lax.ppermute(block, "cohort", [(i, (i + 2 * shift) % self.cohorts) for i in range(self.cohorts)])
+    def along(self, block, way):
+        step = 2 if way > 0 else self.cohorts - 2
+        return lax.ppermute(block, "cohort", [(i, (i + step) % self.cohorts) for i in range(self.cohorts)])
 
     def feat_swap(self, block, bit):
         return lax.ppermute(block, "feat", [(i, i ^ bit) for i in range(self.feats)])
 
-    def feat_sum(self, other, mine, after=None):
+    def feat_sum(self, other, mine, after=None, before_last=None):
         total = mine + self.feat_swap(other, 1)
         if after is not None:
             total = self.follow(total, after)
@@ -337,48 +350,56 @@
         while bit < self.feats:
             total = total + self.feat_swap(total, bit)
             bit *= 2
-        return total, self.feat_swap(total, 1)
+        return total, self.feat_swap(total if before_last is None else self.follow(total, before_last), 1)
 
     def follow(self, block, earlier):
-        return jnp.where(self.go, block, earlier[: block.shape[0], : block.shape[1]])
-
-    def scatter_sum(self, terms, after=None):
-        keep = terms[len(self.sendings) :]
+        rows, columns = (min(a, b) for a, b in zip(block.shape, earlier.shape))
+        if rows < block.shape[0]:
+            return jnp.concatenate([jnp.where(self.go, block[:rows], earlier[:rows, :columns]), block[rows:]], 0)
+        return jnp.where(self.go, block, earlier[:rows, :columns])
+
+    def scatter_sum(self, terms, early=None, turn=None):
+        keep = terms[len(self.outs) :]
         rows = keep[0].shape[0]
-        total, arrivals = None, []
-        for i, sending in enumerate(self.sendings):
+        carried, step = {}, 0
+        for i, size in enumerate(self.outs):
             send = terms[i]
-            if SCATTER_CHAIN and i >= SCATTER_CHAIN:
-                send = self.follow(send, arrivals[i - SCATTER_CHAIN])
-            elif after is not None:
-                send = self.follow(send, after)
+            if i and early is not None:
+                send = self.follow(send, early)
+            if not i and turn is not None:
+                send = self.follow(send, turn)
             arrived = self.across(send)
-            arrivals.append(arrived)
-            for j, shift in enumerate(sending):
-                here = arrived[j * rows : (j + 1) * rows] + keep[JOIN * i + j]
-                if RING_SCATTER:
-                    total = here if total is None else here + self.along(total, 1)
-                else:
-                    here = self.along(here, shift) if shift else here
-                    total = here if total is None else total + here
-        return total, arrivals
-
-    def gather(self, block, early=None, after=None):
-        blocks = []
-        if after is not None:
-            block = self.follow(block, after)
-        own = block
-        for step, shift in enumerate(self.in_shifts):
-            if step and RING_GATHER:
-                if CHAIN and step >= CHAIN:
-                    block = self.follow(block, blocks[2 * (step - CHAIN) + 1])
-                block = self.along(block, 1)
-            elif step:
-                block = self.along(own, -shift)
-            if early is not None and step == self.places - 1:
-                block = self.follow(block, early)
-            blocks += [block, self.across(block)]
-        return blocks
+            if not i:
+                arrival = arrived
+            for j in range(size):
+                shift = self.shifts[self.places - 1 - step]
+                total = arrived[j * rows : (j + 1) * rows] + keep[step]
+                step += 1
+                way = (shift > 0) - (shift < 0)
+                for carry in [carried.get(way)] if way else carried.values():
+                    total = total if carry is None else total + carry
+                if way:
+                    carried[way] = self.along(total, way)
+        return total, arrival
+
+    def gather(self, block, early=None):
+        carried = {0: block, 1: block, -1: block}
+        near, far = [], []
+        for first, end in self.ins:
+            group = []
+            for step in range(first, end):
+                way = (self.shifts[step] > 0) - (self.shifts[step] < 0)
+                if way:
+                    if HOLD and step >= 3:
+                        carried[way] = self.follow(carried[way], far[(step - 3) // NEXT_IN])
+                    carried[way] = self.along(carried[way], way)
+                group.append(carried[way])
+            group = jnp.concatenate(group, 0) if len(group) > 1 else group[0]
+            near.append(group)
+            if early is not None and end == self.places:
+                group = self.follow(group, early)
+            far.append(self.across(group))
+        return near + far
 
 
 def solution(mesh):
@@ -386,6 +407,11 @@
         grid = Grid(mesh, ranks[0] > 0)
         clients, rows, slots = b_factors.shape
         a_rows = a_factors.reshape(clients * slots, rows)
+
+        def mixing_after(mixing, panels, scales, factor):
+            gram = grid.feat_sum(*gram_terms(panels, grid.gather_order, grid.half))
+            return mixing_of(grid.half, *gram, mixing, scales if mixing is not None else (), factor)
+
         mixing, panels = None, None
         for turn in range(ITERS):
             squares = turn > 0
@@ -393,27 +419,28 @@
                 halves = [first_coef(a_rows, probes, g, grid.half, [b_factors] if g else []) for g in range(GROUPS)]
             else:
                 halves = [coef_terms(a_rows, panel, grid.gather_order, grid.half) for panel in panels]
-            totals, scales, arrivals, mine = [], [], None, None
+            terms, mine = [], None
             for g in range(GROUPS):
-                mine, partner = grid.feat_sum(*halves[g], mine if ORDER_FEAT else None)
-                terms = panel_terms(
-                    b_factors, mine, partner, grid.scatter_order, grid.half, ranks, grid.sizes, squares
+                before_last = terms[-1][0] if g and SWAP_GATE else None
+                mine, partner = grid.feat_sum(*halves[g], mine, before_last)
+                terms.append(
+                    panel_terms(b_factors, mine, partner, grid.scatter_order, grid.half, ranks, grid.sizes, squares)
                 )
-                scales += terms[len(grid.sizes) :]
-                after = arrivals[ORDER_SCATTER] if g and ORDER_SCATTER else None
-                total, arrivals = grid.scatter_sum(terms[: len(grid.sizes)], after)
+            scales = [array for term in terms for array in term[len(grid.sizes) :]]
+            terms = [term[: len(grid.sizes)] for term in terms]
+            totals, arrival = [], None
+            for g, term in enumerate(terms):
+                early = terms[-1][-1] if g < GROUPS - 1 and PANELS_FIRST else None
+                total, arrival = grid.scatter_sum(term, early, arrival if IN_TURN else None)
                 totals.append(total)
-            panels = []
-            for g in range(GROUPS):
-                after = panels[-1][ORDER_GATHER] if g and ORDER_GATHER else None
-                panels.append(grid.gather(totals[g], mixing if g else None, after))
-            gram = grid.feat_sum(*gram_terms(panels, grid.gather_order, grid.half))
-            if turn == 0:
-                mixing = mixing_of(grid.half, *gram)
-            else:
-                last = turn == ITERS - 1
-                factor = math.sqrt(rows * grid.feats) if last else 1.0
-                mixing = mixing_of(grid.half, *gram, mixing, scales, factor)
+            if turn:
+                first = panels[0]
+                if LATE_GRAM:
+                    first = [grid.follow(first[0], totals[0])] + first[1:]
+                mixing = mixing_after(mixing, [first] + panels[1:], before_scales, 1.0)
+            panels = [grid.gather(total, mixing if g else None) for g, total in enumerate(totals)]
+            before_scales = scales
+        mixing = mixing_after(mixing, panels, scales, math.sqrt(rows * grid.feats))
         return apply_mixing(panels, grid.gather_order, mixing)
 
     in_specs = (P("cohort", "feat", None), P("cohort", None, "feat"), P("cohort"), P("feat", None))

time: 210 us -> 195 us (0.929)
  waiting for transfers between devices: 99.4 us -> 70.4 us
  starting transfers between devices: 59.1 us -> 73.8 us
    ppermute x24, waiting for transfers between devices: 53.5 us -> 25.9 us  [along(): lax.ppermute(block, 'cohort', [(i, (i + step) % self.cohorts) for i in ra...]
    ppermute x24, starting transfers between devices: 10.5 us -> 33.7 us  [along(): lax.ppermute(block, 'cohort', [(i, (i + step) % self.cohorts) for i in ra...]
    ppermute x18, waiting for transfers between devices: 32.4 us -> 22.6 us  [feat_swap(): lax.ppermute(block, 'feat', [(i, i ^ bit) for i in range(self.feats)])]
    ppermute x32 -> x20, starting transfers between devices: 36.7 us -> 27.6 us  [across(): lax.ppermute(block, 'cohort', [(i, i ^ 1) for i in range(self.cohorts)])]
    ppermute x32 -> x20, waiting for transfers between devices: 13.5 us -> 21.9 us  [across(): lax.ppermute(block, 'cohort', [(i, i ^ 1) for i in range(self.cohorts)])]
  transfers between devices with their start and end apart: 74 -> 62, of which waited for: 40 -> 29; matrix products, arithmetic and copies ran while one was open for 0% -> 0% of each run, Pallas kernels for 12% -> 13%
where the time goes in v4:
time: 195 us; the launch traced here: 194 us
  starting transfers between devices  73.8 us (38%)
  waiting for transfers between devices  70.4 us (36%)
  Pallas kernels  36.3 us (19%)
  local copies, waits for them, and re-layouts  12.4 us (6%)
    ppermute x24, starting transfers between devices, along(): lax.ppermute(block, 'cohort', [(i, (i + step) % self.cohorts) for i in ra...  33.7 us
    ppermute x20, starting transfers between devices, across(): lax.ppermute(block, 'cohort', [(i, i ^ 1) for i in range(self.cohorts)])  27.6 us
    ppermute x24, waiting for transfers between devices, along(): lax.ppermute(block, 'cohort', [(i, (i + step) % self.cohorts) for i in ra...  25.9 us
    ppermute x18, waiting for transfers between devices, feat_swap(): lax.ppermute(block, 'feat', [(i, i ^ bit) for i in range(self.feats)])  22.6 us
    ppermute x20, waiting for transfers between devices, across(): lax.ppermute(block, 'cohort', [(i, i ^ 1) for i in range(self.cohorts)])  21.9 us
    ppermute x18, starting transfers between devices, feat_swap(): lax.ppermute(block, 'feat', [(i, i ^ bit) for i in range(self.feats)])  12.5 us
    unnamed x16, local copies, waits for them, and re-layouts  12.2 us
    pallas_call x4, Pallas kernels, panel_terms(): pl.pallas_call(functools.partial(panel_kernel, sizes, squares), in_specs=...  12.1 us
  transfers between devices with their start and end apart: 62, of which 29 were waited for; matrix products, arithmetic and copies ran while one was open for 0% of the time, Pallas kernels for 13%

profile of v4, /device:TPU:0, one launch (start us, length us, event | category | flops | bytes accessed | tf_op | source)
XLA Modules:
  0.0 194.5 jit_solution(6267478532853645406)
XLA Ops:
  0.0 3.5 %copy-done.2 = f32[4,256,2048]{2,1,0:T(8,128)S(1)} copy-done((f32[4,256,2048]{2,1,0:T(8,128)S(1)}, f32[4,256,2048]{2,1,0:T(8,128)}, u32[]{:S(2)}) %copy-start.2) | copy-done | bytes 8388632
  3.5 1.8 copy-done.4
  5.4 2.6 %first_coef.2 = (f32[512,128]{1,0:T(8,128)S(1)}, f32[512,128]{1,0:T(8,128)S(1)}) custom-call(s32[1]{0:T(128)} %bitcast.8.half, f32[2048,256]{1,0:T(8,128)S(1)} %copy-done.4, f32[1024,2048]{1,0:T(8,128)S(1)} %bitcast.16), custom_call_target="tpu_custom_call" | custom-call | flops 2147483648 | bytes 8388608 | tf_op jit(solution)/shard_map/first_coef/pallas_call | solution.py:88
  8.5 2.6 %first_coef.3 = (f32[512,128]{1,0:T(8,128)S(1)}, f32[512,128]{1,0:T(8,128)S(1)}) custom-call(s32[1]{0:T(128)} %bitcast.8.half, f32[2048,256]{1,0:T(8,128)S(1)} %copy-done.4, f32[1024,2048]{1,0:T(8,128)S(1)} %bitcast.17, f32[4,2048,256]{2,1,0:T(8,128)S(1)} %copy-done), custom_call_target="tpu_custom_call" | custom-call | flops 2147483648 | bytes 8388608 | tf_op jit(solution)/shard_map/first_coef/pallas_call | solution.py:88
  11.3 3.0 %collective-permute-start.1 = (f32[512,128]{1,0:T(8,128)S(1)}, f32[512,128]{1,0:T(8,128)S(1)}, u32[]{:S(2)}, u32[]{:S(2)}) collective-permute-start(f32[512,128]{1,0:T(8,128)S(1)} %add.227), channel_id=1, source_target_pairs={{0,2},{1,3},{2,0},{3,1},{4,6},{5,7},{6,4},{7,5},{8,10},{9,11},{10,... | collective-permute-start | bytes 786440 | tf_op jit(solution)/shard_map/ppermute | solution.py:343
  14.3 6.4 %collective-permute-done.1 = f32[512,128]{1,0:T(8,128)S(1)} collective-permute-done((f32[512,128]{1,0:T(8,128)S(1)}, f32[512,128]{1,0:T(8,128)S(1)}, u32[]{:S(2)}, u32[]{:S(2)}) %collective-permute-start.1) | collective-permute-done | bytes 262176 | tf_op jit(solution)/shard_map/ppermute | solution.py:343
  22.8 3.4 %copy-done.1 = f32[4,2048,256]{2,1,0:T(8,128)S(1)} copy-done((f32[4,2048,256]{2,1,0:T(8,128)S(1)}, f32[4,2048,256]{2,1,0:T(8,128)}, u32[]{:S(2)}) %copy-start.1) | copy-done | bytes 8388632
  26.2 3.0 %panel.4 = (f32[512,128]{1,0:T(8,128)S(1)}, f32[512,128]{1,0:T(8,128)S(1)}, f32[256,128]{1,0:T(8,128)S(1)}, f32[256,128]{1,0:T(8,128)S(1)}, f32[256,128]{1,0:T(8,128)S(1)}, /*index=5*/f32[256,128]{1,0:T(8,128)S(1)}) custom-call(s32[8]{0:T(128)S(1)} %stack.53.where, s32[1]{0:T(128)} %bitcast.8.half, s32[4]{0:T(128)S(1)} %copy-done.5, ...), custom_call_target="tpu_custom_call" | custom-call | flops 2147483648 | bytes 8388608 | tf_op jit(solution)/shard_map/panel/pallas_call | solution.py:176
  29.8 1.8 collective-permute-start.4
  31.6 3.0 %panel.6 = (f32[512,128]{1,0:T(8,128)S(1)}, f32[512,128]{1,0:T(8,128)S(1)}, f32[256,128]{1,0:T(8,128)S(1)}, f32[256,128]{1,0:T(8,128)S(1)}, f32[256,128]{1,0:T(8,128)S(1)}, /*index=5*/f32[256,128]{1,0:T(8,128)S(1)}) custom-call(s32[8]{0:T(128)S(1)} %stack.53.where, s32[1]{0:T(128)} %bitcast.8.half, s32[4]{0:T(128)S(1)} %copy-done.5, ...), custom_call_target="tpu_custom_call" | custom-call | flops 2147483648 | bytes 8388608 | tf_op jit(solution)/shard_map/panel/pallas_call | solution.py:176
  34.7 3.9 %collective-permute-done.4 = f32[512,128]{1,0:T(8,128)S(1)} collective-permute-done((f32[512,128]{1,0:T(8,128)S(1)}, f32[512,128]{1,0:T(8,128)S(1)}, u32[]{:S(2)}, u32[]{:S(2)}) %collective-permute-start.4) | collective-permute-done | bytes 262176 | tf_op jit(solution)/shard_map/ppermute | solution.py:336
  38.5 1.8 collective-permute-start.32
  40.7 1.9 collective-permute-start.5
  42.5 2.1 %collective-permute-start.7 = (f32[256,128]{1,0:T(8,128)S(1)}, f32[256,128]{1,0:T(8,128)S(1)}, u32[]{:S(2)}, u32[]{:S(2)}) collective-permute-start(f32[256,128]{1,0:T(8,128)S(1)} %get-tuple-element.96), channel_id=1, source_target_pairs={{0,24},{4,28},{8,0},{12,4},{16,8},{20,12},{24,16},{28,20},{1,25},{... | collective-permute-start | bytes 393224 | tf_op jit(solution)/shard_map/ppermute | solution.py:340
  47.9 1.9 collective-permute-start.33
  49.7 3.7 %collective-permute-done.3 = f32[512,128]{1,0:T(8,128)S(1)} collective-permute-done((f32[512,128]{1,0:T(8,128)S(1)}, f32[512,128]{1,0:T(8,128)S(1)}, u32[]{:S(2)}, u32[]{:S(2)}) %collective-permute-start.3) | collective-permute-done | bytes 262176 | tf_op jit(solution)/shard_map/ppermute | solution.py:336
  53.5 1.9 collective-permute-start.6
  55.4 2.1 %collective-permute-start.35 = (f32[256,128]{1,0:T(8,128)S(1)}, f32[256,128]{1,0:T(8,128)S(1)}, u32[]{:S(2)}, u32[]{:S(2)}) collective-permute-start(f32[256,128]{1,0:T(8,128)S(1)} %get-tuple-element.94), channel_id=1, source_target_pairs={{0,24},{4,28},{8,0},{12,4},{16,8},{20,12},{24,16},{28,20},{1,25},{... | collective-permute-start | bytes 393224 | tf_op jit(solution)/shard_map/ppermute | solution.py:340
  57.8 1.9 collective-permute-start.34
  60.5 1.8 collective-permute-start.10
  69.1 2.4 %collective-permute-done.8 = f32[256,128]{1,0:T(8,128)S(1)} collective-permute-done((f32[256,128]{1,0:T(8,128)S(1)}, f32[256,128]{1,0:T(8,128)S(1)}, u32[]{:S(2)}, u32[]{:S(2)}) %collective-permute-start.8) | collective-permute-done | bytes 131104 | tf_op jit(solution)/shard_map/ppermute | solution.py:340
  73.9 3.4 %collective-permute-start.37 = (f32[256,128]{1,0:T(8,128)S(1)}, f32[256,128]{1,0:T(8,128)S(1)}, u32[]{:S(2)}, u32[]{:S(2)}) collective-permute-start(f32[256,128]{1,0:T(8,128)S(1)} %fusion.5.refs_0_.refs_6_), channel_id=1, source_target_pairs={{0,24},{4,28},{8,0},{12,4},{16,8},{20,12},{24,16},{28,20},{1,25},{... | collective-permute-start | bytes 393224 | tf_op jit(solution)/shard_map/ppermute | solution.py:340
  79.0 2.3 %collective-permute-start.13 = (f32[256,128]{1,0:T(8,128)S(1)}, f32[256,128]{1,0:T(8,128)S(1)}, u32[]{:S(2)}, u32[]{:S(2)}) collective-permute-start(f32[256,128]{1,0:T(8,128)S(1)} %collective-permute-done.11.refs_2_), channel_id=1, source_target_pairs={{0,4},{4,0},{8,12},{12,8},{16,20},{20,16},{24,28},{28,24},{1,5},{5... | collective-permute-start | bytes 393224 | tf_op jit(solution)/shard_map/ppermute | solution.py:336
  85.6 3.4 %copy-done.3 = f32[4,256,2048]{2,1,0:T(8,128)S(1)} copy-done((f32[4,256,2048]{2,1,0:T(8,128)S(1)}, f32[4,256,2048]{2,1,0:T(8,128)}, u32[]{:S(2)}) %copy-start.3) | copy-done | bytes 8388632
  89.0 3.2 %coef.2 = (f32[520,128]{1,0:T(8,128)S(1)}, f32[520,128]{1,0:T(8,128)S(1)}) custom-call(s32[8]{0:T(128)S(1)} %stack.50.where, s32[1]{0:T(128)} %bitcast.8.half, f32[1024,2048]{1,0:T(8,128)S(1)} %bitcast.18, f32[256,128]{1,0:T(8,128)S(1)} %fusion.11.refs_0_, f32[512,128]{1,0:T(8,128)S(1)} %constant_dynamic-update-slice_fusion.refs_1_, ...), custom_call_target="tpu_custom_call" | custom-call | flops 2147483648 | bytes 8388608 | tf_op jit(solution)/shard_map/coef/pallas_call | solution.py:127
  92.3 3.2 %coef.3 = (f32[520,128]{1,0:T(8,128)S(1)}, f32[520,128]{1,0:T(8,128)S(1)}) custom-call(s32[8]{0:T(128)S(1)} %stack.50.where, s32[1]{0:T(128)} %bitcast.8.half, f32[1024,2048]{1,0:T(8,128)S(1)} %bitcast.19, f32[256,128]{1,0:T(8,128)S(1)} %fusion.5.refs_0_.refs_6_, f32[512,128]{1,0:T(8,128)S(1)} %constant_dynamic-update-slice_fusion.4.refs_1_.refs_7_, ...), custom_call_target="tpu_custom_call" | custom-call | flops 2147483648 | bytes 8388608 | tf_op jit(solution)/shard_map/coef/pallas_call | solution.py:127
  97.6 6.8 %collective-permute-done.15 = f32[520,128]{1,0:T(8,128)S(1)} collective-permute-done((f32[520,128]{1,0:T(8,128)S(1)}, f32[520,128]{1,0:T(8,128)S(1)}, u32[]{:S(2)}, u32[]{:S(2)}) %collective-permute-start.15) | collective-permute-done | bytes 266272 | tf_op jit(solution)/shard_map/ppermute | solution.py:343
  106.2 3.0 %panel.5 = (f32[512,128]{1,0:T(8,128)S(1)}, f32[512,128]{1,0:T(8,128)S(1)}, f32[256,128]{1,0:T(8,128)S(1)}, f32[256,128]{1,0:T(8,128)S(1)}, f32[256,128]{1,0:T(8...) custom-call(s32[8]{0:T(128)S(1)} %stack.53.where, s32[1]{0:T(128)} %bitcast.8.half, s32[4]{0:T(128)S(1)} %copy-done.5, ...), custom_call_target="tpu_custom_call" | custom-call | flops 2147483648 | bytes 8388608 | tf_op jit(solution)/shard_map/panel/pallas_call | solution.py:176
  109.2 2.2 %collective-permute-start.18 = (f32[512,128]{1,0:T(8,128)S(1)}, f32[512,128]{1,0:T(8,128)S(1)}, u32[]{:S(2)}, u32[]{:S(2)}) collective-permute-start(f32[512,128]{1,0:T(8,128)S(1)} %get-tuple-element.56), channel_id=1, source_target_pairs={{0,4},{4,0},{8,12},{12,8},{16,20},{20,16},{24,28},{28,24},{1,5},{5... | collective-permute-start | bytes 786440 | tf_op jit(solution)/shard_map/ppermute | solution.py:336
  111.4 2.0 %collective-permute-done.43 = f32[520,128]{1,0:T(8,128)S(1)} collective-permute-done((f32[520,128]{1,0:T(8,128)S(1)}, f32[520,128]{1,0:T(8,128)S(1)}, u32[]{:S(2)}, u32[]{:S(2)}) %collective-permute-start.43) | collective-permute-done | bytes 266272 | tf_op jit(solution)/shard_map/ppermute | solution.py:343
  113.6 2.2 %collective-permute-start.17 = (f32[512,128]{1,0:T(8,128)S(1)}, f32[512,128]{1,0:T(8,128)S(1)}, u32[]{:S(2)}, u32[]{:S(2)}) collective-permute-start(f32[512,128]{1,0:T(8,128)S(1)} %get-tuple-element.53), channel_id=1, source_target_pairs={{0,4},{4,0},{8,12},{12,8},{16,20},{20,16},{24,28},{28,24},{1,5},{5... | collective-permute-start | bytes 786440 | tf_op jit(solution)/shard_map/ppermute | solution.py:336
  115.9 2.7 %collective-permute-done.18 = f32[512,128]{1,0:T(8,128)S(1)} collective-permute-done((f32[512,128]{1,0:T(8,128)S(1)}, f32[512,128]{1,0:T(8,128)S(1)}, u32[]{:S(2)}, u32[]{:S(2)}) %collective-permute-start.18) | collective-permute-done | bytes 262176 | tf_op jit(solution)/shard_map/ppermute | solution.py:336
  118.6 3.8 %collective-permute-start.21 = (f32[256,128]{1,0:T(8,128)S(1)}, f32[256,128]{1,0:T(8,128)S(1)}, u32[]{:S(2)}, u32[]{:S(2)}) collective-permute-start(f32[256,128]{1,0:T(8,128)S(1)} %get-tuple-element.92), channel_id=1, source_target_pairs={{0,24},{4,28},{8,0},{12,4},{16,8},{20,12},{24,16},{28,20},{1,25},{... | collective-permute-start | bytes 393224 | tf_op jit(solution)/shard_map/ppermute | solution.py:340
  122.4 3.0 %panel.7 = (f32[512,128]{1,0:T(8,128)S(1)}, f32[512,128]{1,0:T(8,128)S(1)}, f32[256,128]{1,0:T(8,128)S(1)}, f32[256,128]{1,0:T(8,128)S(1)}, f32[256,128]{1,0:T(8...) custom-call(s32[8]{0:T(128)S(1)} %stack.53.where, s32[1]{0:T(128)} %bitcast.8.half, s32[4]{0:T(128)S(1)} %copy-done.5, ...), custom_call_target="tpu_custom_call" | custom-call | flops 2147483648 | bytes 8388608 | tf_op jit(solution)/shard_map/panel/pallas_call | solution.py:176
  125.5 2.1 %collective-permute-start.45 = (f32[512,128]{1,0:T(8,128)S(1)}, f32[512,128]{1,0:T(8,128)S(1)}, u32[]{:S(2)}, u32[]{:S(2)}) collective-permute-start(f32[512,128]{1,0:T(8,128)S(1)} %get-tuple-element.69), channel_id=1, source_target_pairs={{0,4},{4,0},{8,12},{12,8},{16,20},{20,16},{24,28},{28,24},{1,5},{5... | collective-permute-start | bytes 786440 | tf_op jit(solution)/shard_map/ppermute | solution.py:336
  128.1 6.4 %collective-permute-done.20 = f32[256,128]{1,0:T(8,128)S(1)} collective-permute-done((f32[256,128]{1,0:T(8,128)S(1)}, f32[256,128]{1,0:T(8,128)S(1)}, u32[]{:S(2)}, u32[]{:S(2)}) %collective-permute-start.20) | collective-permute-done | bytes 131104 | tf_op jit(solution)/shard_map/ppermute | solution.py:340
  139.6 3.7 %collective-permute-start.23 = (f32[256,128]{1,0:T(8,128)S(1)}, f32[256,128]{1,0:T(8,128)S(1)}, u32[]{:S(2)}, u32[]{:S(2)}) collective-permute-start(f32[256,128]{1,0:T(8,128)S(1)} %get-tuple-element.82.refs_0_), channel_id=1, source_target_pairs={{0,24},{4,28},{8,0},{12,4},{16,8},{20,12},{24,16},{28,20},{1,25},{... | collective-permute-start | bytes 393224 | tf_op jit(solution)/shard_map/ppermute | solution.py:340
  143.4 3.9 %collective-permute-start.49 = (f32[256,128]{1,0:T(8,128)S(1)}, f32[256,128]{1,0:T(8,128)S(1)}, u32[]{:S(2)}, u32[]{:S(2)}) collective-permute-start(f32[256,128]{1,0:T(8,128)S(1)} %get-tuple-element.90), channel_id=1, source_target_pairs={{0,24},{4,28},{8,0},{12,4},{16,8},{20,12},{24,16},{28,20},{1,25},{... | collective-permute-start | bytes 393224 | tf_op jit(solution)/shard_map/ppermute | solution.py:340
  148.7 3.4 %collective-permute-done.22 = f32[256,128]{1,0:T(8,128)S(1)} collective-permute-done((f32[256,128]{1,0:T(8,128)S(1)}, f32[256,128]{1,0:T(8,128)S(1)}, u32[]{:S(2)}, u32[]{:S(2)}) %collective-permute-start.22) | collective-permute-done | bytes 131104 | tf_op jit(solution)/shard_map/ppermute | solution.py:340
  152.6 4.2 %collective-permute-done.48 = f32[256,128]{1,0:T(8,128)S(1)} collective-permute-done((f32[256,128]{1,0:T(8,128)S(1)}, f32[256,128]{1,0:T(8,128)S(1)}, u32[]{:S(2)}, u32[]{:S(2)}) %collective-permute-start.48) | collective-permute-done | bytes 131104 | tf_op jit(solution)/shard_map/ppermute | solution.py:340
  159.9 1.9 collective-permute-done.52.refs_9_
  161.9 1.9 collective-permute-start.51
  164.7 2.9 %mixing.2.before = f32[256,256]{1,0:T(8,128)S(1)} custom-call(s32[1]{0:T(128)} %bitcast.8.half, f32[128,256]{1,0:T(8,128)S(1)} %add.264.mine, f32[128,256]{1,0:T(8,128)S(1)} %collective-permute-done.57.partner), custom_call_target="tpu_custom_call" | custom-call | flops 1509949440 | bytes 786432 | tf_op jit(solution)/shard_map/mixing/pallas_call | solution.py:267
  169.0 2.4 %collective-permute-done.53.refs_8_ = f32[256,128]{1,0:T(8,128)S(1)} collective-permute-done((f32[256,128]{1,0:T(8,128)S(1)}, f32[256,128]{1,0:T(8,128)S(1)}, u32[]{:S(2)}, u32[]{:S(2)}) %collective-permute-start.53) | collective-permute-done | bytes 131104 | tf_op jit(solution)/shard_map/ppermute | solution.py:340
  172.7 5.0 %collective-permute-done.58.refs_11_ = f32[256,128]{1,0:T(8,128)S(1)} collective-permute-done((f32[256,128]{1,0:T(8,128)S(1)}, f32[256,128]{1,0:T(8,128)S(1)}, u32[]{:S(2)}, u32[]{:S(2)}) %collective-permute-start.58) | collective-permute-done | bytes 131104 | tf_op jit(solution)/shard_map/ppermute | solution.py:336
  182.4 4.2 %collective-permute-done.60 = f32[128,256]{1,0:T(8,128)S(1)} collective-permute-done((f32[128,256]{1,0:T(8,128)S(1)}, f32[128,256]{1,0:T(8,128)S(1)}, u32[]{:S(2)}, u32[]{:S(2)}) %collective-permute-start.60) | collective-permute-done | bytes 131104 | tf_op jit(solution)/shard_map/ppermute | solution.py:343
  188.0 3.8 %mixing.3 = f32[256,256]{1,0:T(8,128)S(1)} custom-call(s32[1]{0:T(128)} %bitcast.8.half, f32[128,256]{1,0:T(8,128)S(1)} %add.266.mine, f32[128,256]{1,0:T(8,128)S(1)} %collective-permute-done.61.partner, f32[256,256]{1,0:T(8,128)S(1)} %mixing.2.before, f32[8,128]{1,0:T(8,128)S(1)} %get-tuple-element.79.refs_0_, f32[8,128]{1,0:T(8,128)S(1)} %get-tuple-element.80.refs_1_), custom_call_target="tpu_custom_call" | custom-call | flops 1509949440 | bytes 786432 | tf_op jit(solution)/shard_map/mixing/pallas_call | solution.py:267
  191.8 2.5 %apply.1 = f32[2048,256]{1,0:T(8,128)} custom-call(s32[8]{0:T(128)S(1)} %stack.50.where, f32[256,256]{1,0:T(8,128)S(1)} %mixing.3, f32[256,128]{1,0:T(8,128)S(1)} %get-tuple-element.82.refs_0_, f32[512,128]{1,0:T(8,128)S(1)} %constant_dynamic-update-slice_fusion.2.refs_1_, f32[256,128]{1,0:T(8,128)S(1)} %collective-permute-done.25.refs_2_, ...), custom_call_target="tpu_custom_call" | custom-call | flops 805306368 | bytes 4194304 | tf_op jit(solution)/shard_map/apply/pallas_call | solution.py:299
  (144 shorter events, 47.6 us)
Async XLA Ops:
  11.3 9.5 %collective-permute-start.1 = (f32[512,128]{1,0:T(8,128)S(1)}, f32[512,128]{1,0:T(8,128)S(1)}, u32[]{:S(2)}, u32[]{:S(2)}) collective-permute-start(f32[512,128]{1,0:T(8,128)S(1)} %add.227), channel_id=1, source_target_pairs={{0,2},{1,3},{2,0},{3,1},{4,6},{5,7},{6,4},{7,5},{8,10},{9,11},{10,... | collective-permute-start | bytes 786440 | tf_op jit(solution)/shard_map/ppermute | solution.py:343
  20.9 8.7 %collective-permute-start.29 = (f32[512,128]{1,0:T(8,128)S(1)}, f32[512,128]{1,0:T(8,128)S(1)}, u32[]{:S(2)}, u32[]{:S(2)}) collective-permute-start(f32[512,128]{1,0:T(8,128)S(1)} %get-tuple-element.87), channel_id=1, source_target_pairs={{0,2},{1,3},{2,0},{3,1},{4,6},{5,7},{6,4},{7,5},{8,10},{9,11},{10,... | collective-permute-start | bytes 786440 | tf_op jit(solution)/shard_map/ppermute | solution.py:343
  29.8 8.7 %collective-permute-start.4 = (f32[512,128]{1,0:T(8,128)S(1)}, f32[512,128]{1,0:T(8,128)S(1)}, u32[]{:S(2)}, u32[]{:S(2)}) collective-permute-start(f32[512,128]{1,0:T(8,128)S(1)} %get-tuple-element.48), channel_id=1, source_target_pairs={{0,4},{4,0},{8,12},{12,8},{16,20},{20,16},{24,28},{28,24},{1,5},{5... | collective-permute-start | bytes 786440 | tf_op jit(solution)/shard_map/ppermute | solution.py:336
  38.5 9.3 %collective-permute-start.32 = (f32[512,128]{1,0:T(8,128)S(1)}, f32[512,128]{1,0:T(8,128)S(1)}, u32[]{:S(2)}, u32[]{:S(2)}) collective-permute-start(f32[512,128]{1,0:T(8,128)S(1)} %broadcast_select_fusion.1), channel_id=1, source_target_pairs={{0,4},{4,0},{8,12},{12,8},{16,20},{20,16},{24,28},{28,24},{1,5},{5... | collective-permute-start | bytes 786440 | tf_op jit(solution)/shard_map/ppermute | solution.py:336
  40.4 13.1 %collective-permute-start.3 = (f32[512,128]{1,0:T(8,128)S(1)}, f32[512,128]{1,0:T(8,128)S(1)}, u32[]{:S(2)}, u32[]{:S(2)}) collective-permute-start(f32[512,128]{1,0:T(8,128)S(1)} %get-tuple-element.45), channel_id=1, source_target_pairs={{0,4},{4,0},{8,12},{12,8},{16,20},{20,16},{24,28},{28,24},{1,5},{5... | collective-permute-start | bytes 786440 | tf_op jit(solution)/shard_map/ppermute | solution.py:336
  40.7 12.8 %collective-permute-start.5 = (f32[256,128]{1,0:T(8,128)S(1)}, f32[256,128]{1,0:T(8,128)S(1)}, u32[]{:S(2)}, u32[]{:S(2)}) collective-permute-start(f32[256,128]{1,0:T(8,128)S(1)} %get-tuple-element.95), channel_id=1, source_target_pairs={{0,8},{4,12},{8,16},{12,20},{16,24},{20,28},{24,0},{28,4},{1,9},{5... | collective-permute-start | bytes 393224 | tf_op jit(solution)/shard_map/ppermute | solution.py:340
  42.5 17.1 %collective-permute-start.7 = (f32[256,128]{1,0:T(8,128)S(1)}, f32[256,128]{1,0:T(8,128)S(1)}, u32[]{:S(2)}, u32[]{:S(2)}) collective-permute-start(f32[256,128]{1,0:T(8,128)S(1)} %get-tuple-element.96), channel_id=1, source_target_pairs={{0,24},{4,28},{8,0},{12,4},{16,8},{20,12},{24,16},{28,20},{1,25},{... | collective-permute-start | bytes 393224 | tf_op jit(solution)/shard_map/ppermute | solution.py:340
  44.6 13.1 %collective-permute-start.31 = (f32[512,128]{1,0:T(8,128)S(1)}, f32[512,128]{1,0:T(8,128)S(1)}, u32[]{:S(2)}, u32[]{:S(2)}) collective-permute-start(f32[512,128]{1,0:T(8,128)S(1)} %get-tuple-element.61), channel_id=1, source_target_pairs={{0,4},{4,0},{8,12},{12,8},{16,20},{20,16},{24,28},{28,24},{1,5},{5... | collective-permute-start | bytes 786440 | tf_op jit(solution)/shard_map/ppermute | solution.py:336
  47.9 9.9 %collective-permute-start.33 = (f32[256,128]{1,0:T(8,128)S(1)}, f32[256,128]{1,0:T(8,128)S(1)}, u32[]{:S(2)}, u32[]{:S(2)}) collective-permute-start(f32[256,128]{1,0:T(8,128)S(1)} %get-tuple-element.93), channel_id=1, source_target_pairs={{0,8},{4,12},{8,16},{12,20},{16,24},{20,28},{24,0},{28,4},{1,9},{5... | collective-permute-start | bytes 393224 | tf_op jit(solution)/shard_map/ppermute | solution.py:340
  53.5 6.9 %collective-permute-start.6 = (f32[256,128]{1,0:T(8,128)S(1)}, f32[256,128]{1,0:T(8,128)S(1)}, u32[]{:S(2)}, u32[]{:S(2)}) collective-permute-start(f32[256,128]{1,0:T(8,128)S(1)} %fusion.9), channel_id=1, source_target_pairs={{0,8},{4,12},{8,16},{12,20},{16,24},{20,28},{24,0},{28,4},{1,9},{5... | collective-permute-start | bytes 393224 | tf_op jit(solution)/shard_map/ppermute | solution.py:340
  55.4 9.0 %collective-permute-start.35 = (f32[256,128]{1,0:T(8,128)S(1)}, f32[256,128]{1,0:T(8,128)S(1)}, u32[]{:S(2)}, u32[]{:S(2)}) collective-permute-start(f32[256,128]{1,0:T(8,128)S(1)} %get-tuple-element.94), channel_id=1, source_target_pairs={{0,24},{4,28},{8,0},{12,4},{16,8},{20,12},{24,16},{28,20},{1,25},{... | collective-permute-start | bytes 393224 | tf_op jit(solution)/shard_map/ppermute | solution.py:340
  57.8 8.4 %collective-permute-start.34 = (f32[256,128]{1,0:T(8,128)S(1)}, f32[256,128]{1,0:T(8,128)S(1)}, u32[]{:S(2)}, u32[]{:S(2)}) collective-permute-start(f32[256,128]{1,0:T(8,128)S(1)} %fusion.3), channel_id=1, source_target_pairs={{0,8},{4,12},{8,16},{12,20},{16,24},{20,28},{24,0},{28,4},{1,9},{5... | collective-permute-start | bytes 393224 | tf_op jit(solution)/shard_map/ppermute | solution.py:340
  60.5 8.7 %collective-permute-start.10 = (f32[256,128]{1,0:T(8,128)S(1)}, f32[256,128]{1,0:T(8,128)S(1)}, u32[]{:S(2)}, u32[]{:S(2)}) collective-permute-start(f32[256,128]{1,0:T(8,128)S(1)} %fusion.11.refs_0_), channel_id=1, source_target_pairs={{0,4},{4,0},{8,12},{12,8},{16,20},{20,16},{24,28},{28,24},{1,5},{5... | collective-permute-start | bytes 393224 | tf_op jit(solution)/shard_map/ppermute | solution.py:336
  62.3 10.4 %collective-permute-start.9 = (f32[256,128]{1,0:T(8,128)S(1)}, f32[256,128]{1,0:T(8,128)S(1)}, u32[]{:S(2)}, u32[]{:S(2)}) collective-permute-start(f32[256,128]{1,0:T(8,128)S(1)} %fusion.11.refs_0_), channel_id=1, source_target_pairs={{0,24},{4,28},{8,0},{12,4},{16,8},{20,12},{24,16},{28,20},{1,25},{... | collective-permute-start | bytes 393224 | tf_op jit(solution)/shard_map/ppermute | solution.py:340
  64.0 7.6 %collective-permute-start.8 = (f32[256,128]{1,0:T(8,128)S(1)}, f32[256,128]{1,0:T(8,128)S(1)}, u32[]{:S(2)}, u32[]{:S(2)}) collective-permute-start(f32[256,128]{1,0:T(8,128)S(1)} %fusion.11.refs_0_), channel_id=1, source_target_pairs={{0,8},{4,12},{8,16},{12,20},{16,24},{20,28},{24,0},{28,4},{1,9},{5... | collective-permute-start | bytes 393224 | tf_op jit(solution)/shard_map/ppermute | solution.py:340
  66.2 11.2 %collective-permute-start.38 = (f32[256,128]{1,0:T(8,128)S(1)}, f32[256,128]{1,0:T(8,128)S(1)}, u32[]{:S(2)}, u32[]{:S(2)}) collective-permute-start(f32[256,128]{1,0:T(8,128)S(1)} %fusion.5.refs_0_.refs_6_), channel_id=1, source_target_pairs={{0,4},{4,0},{8,12},{12,8},{16,20},{20,16},{24,28},{28,24},{1,5},{5... | collective-permute-start | bytes 393224 | tf_op jit(solution)/shard_map/ppermute | solution.py:336
  67.8 9.5 %collective-permute-start.36 = (f32[256,128]{1,0:T(8,128)S(1)}, f32[256,128]{1,0:T(8,128)S(1)}, u32[]{:S(2)}, u32[]{:S(2)}) collective-permute-start(f32[256,128]{1,0:T(8,128)S(1)} %fusion.5.refs_0_.refs_6_), channel_id=1, source_target_pairs={{0,8},{4,12},{8,16},{12,20},{16,24},{20,28},{24,0},{28,4},{1,9},{5... | collective-permute-start | bytes 393224 | tf_op jit(solution)/shard_map/ppermute | solution.py:340
  71.6 7.5 %collective-permute-start.11 = (f32[256,128]{1,0:T(8,128)S(1)}, f32[256,128]{1,0:T(8,128)S(1)}, u32[]{:S(2)}, u32[]{:S(2)}) collective-permute-start(f32[256,128]{1,0:T(8,128)S(1)} %get-tuple-element.101), channel_id=1, source_target_pairs={{0,8},{4,12},{8,16},{12,20},{16,24},{20,28},{24,0},{28,4},{1,9},{5... | collective-permute-start | bytes 393224 | tf_op jit(solution)/shard_map/ppermute | solution.py:340
  72.7 12.9 %collective-permute-start.12 = (f32[512,128]{1,0:T(8,128)S(1)}, f32[512,128]{1,0:T(8,128)S(1)}, u32[]{:S(2)}, u32[]{:S(2)}) collective-permute-start(f32[512,128]{1,0:T(8,128)S(1)} %constant_dynamic-update-slice_fusion.refs_1_), channel_id=1, source_target_pairs={{0,4},{4,0},{8,12},{12,8},{16,20},{20,16},{24,28},{28,24},{1,5},{5... | collective-permute-start | bytes 786440 | tf_op jit(solution)/shard_map/ppermute | solution.py:336
  73.9 7.8 %collective-permute-start.37 = (f32[256,128]{1,0:T(8,128)S(1)}, f32[256,128]{1,0:T(8,128)S(1)}, u32[]{:S(2)}, u32[]{:S(2)}) collective-permute-start(f32[256,128]{1,0:T(8,128)S(1)} %fusion.5.refs_0_.refs_6_), channel_id=1, source_target_pairs={{0,24},{4,28},{8,0},{12,4},{16,8},{20,12},{24,16},{28,20},{1,25},{... | collective-permute-start | bytes 393224 | tf_op jit(solution)/shard_map/ppermute | solution.py:340
  77.4 6.8 %collective-permute-start.39 = (f32[256,128]{1,0:T(8,128)S(1)}, f32[256,128]{1,0:T(8,128)S(1)}, u32[]{:S(2)}, u32[]{:S(2)}) collective-permute-start(f32[256,128]{1,0:T(8,128)S(1)} %get-tuple-element.103), channel_id=1, source_target_pairs={{0,8},{4,12},{8,16},{12,20},{16,24},{20,28},{24,0},{28,4},{1,9},{5... | collective-permute-start | bytes 393224 | tf_op jit(solution)/shard_map/ppermute | solution.py:340
  79.0 6.6 %collective-permute-start.13 = (f32[256,128]{1,0:T(8,128)S(1)}, f32[256,128]{1,0:T(8,128)S(1)}, u32[]{:S(2)}, u32[]{:S(2)}) collective-permute-start(f32[256,128]{1,0:T(8,128)S(1)} %collective-permute-done.11.refs_2_), channel_id=1, source_target_pairs={{0,4},{4,0},{8,12},{12,8},{16,20},{20,16},{24,28},{28,24},{1,5},{5... | collective-permute-start | bytes 393224 | tf_op jit(solution)/shard_map/ppermute | solution.py:336
  81.7 10.6 %collective-permute-start.40 = (f32[512,128]{1,0:T(8,128)S(1)}, f32[512,128]{1,0:T(8,128)S(1)}, u32[]{:S(2)}, u32[]{:S(2)}) collective-permute-start(f32[512,128]{1,0:T(8,128)S(1)} %constant_dynamic-update-slice_fusion.4.refs_1_.refs_7_), channel_id=1, source_target_pairs={{0,4},{4,0},{8,12},{12,8},{16,20},{20,16},{24,28},{28,24},{1,5},{5... | collective-permute-start | bytes 786440 | tf_op jit(solution)/shard_map/ppermute | solution.py:336
  84.2 8.1 %collective-permute-start.41 = (f32[256,128]{1,0:T(8,128)S(1)}, f32[256,128]{1,0:T(8,128)S(1)}, u32[]{:S(2)}, u32[]{:S(2)}) collective-permute-start(f32[256,128]{1,0:T(8,128)S(1)} %collective-permute-done.39.refs_2_.refs_8_), channel_id=1, source_target_pairs={{0,4},{4,0},{8,12},{12,8},{16,20},{20,16},{24,28},{28,24},{1,5},{5... | collective-permute-start | bytes 393224 | tf_op jit(solution)/shard_map/ppermute | solution.py:336
  96.1 8.4 %collective-permute-start.15 = (f32[520,128]{1,0:T(8,128)S(1)}, f32[520,128]{1,0:T(8,128)S(1)}, u32[]{:S(2)}, u32[]{:S(2)}) collective-permute-start(f32[520,128]{1,0:T(8,128)S(1)} %add.236), channel_id=1, source_target_pairs={{0,2},{1,3},{2,0},{3,1},{4,6},{5,7},{6,4},{7,5},{8,10},{9,11},{10,... | collective-permute-start | bytes 798728 | tf_op jit(solution)/shard_map/ppermute | solution.py:343
  104.6 8.8 %collective-permute-start.43 = (f32[520,128]{1,0:T(8,128)S(1)}, f32[520,128]{1,0:T(8,128)S(1)}, u32[]{:S(2)}, u32[]{:S(2)}) collective-permute-start(f32[520,128]{1,0:T(8,128)S(1)} %get-tuple-element.83), channel_id=1, source_target_pairs={{0,2},{1,3},{2,0},{3,1},{4,6},{5,7},{6,4},{7,5},{8,10},{9,11},{10,... | collective-permute-start | bytes 798728 | tf_op jit(solution)/shard_map/ppermute | solution.py:343
  109.2 9.3 %collective-permute-start.18 = (f32[512,128]{1,0:T(8,128)S(1)}, f32[512,128]{1,0:T(8,128)S(1)}, u32[]{:S(2)}, u32[]{:S(2)}) collective-permute-start(f32[512,128]{1,0:T(8,128)S(1)} %get-tuple-element.56), channel_id=1, source_target_pairs={{0,4},{4,0},{8,12},{12,8},{16,20},{20,16},{24,28},{28,24},{1,5},{5... | collective-permute-start | bytes 786440 | tf_op jit(solution)/shard_map/ppermute | solution.py:336
  113.6 8.9 %collective-permute-start.44 = (f32[520,128]{1,0:T(8,128)S(1)}, f32[520,128]{1,0:T(8,128)S(1)}, u32[]{:S(2)}, u32[]{:S(2)}) collective-permute-start(f32[520,128]{1,0:T(8,128)S(1)} %pad_maximum_fusion), channel_id=1, source_target_pairs={{0,1},{1,0},{2,3},{3,2},{4,5},{5,4},{6,7},{7,6},{8,9},{9,8},{10,11... | collective-permute-start | bytes 798728 | tf_op jit(solution)/shard_map/ppermute | solution.py:343
  113.6 14.0 %collective-permute-start.17 = (f32[512,128]{1,0:T(8,128)S(1)}, f32[512,128]{1,0:T(8,128)S(1)}, u32[]{:S(2)}, u32[]{:S(2)}) collective-permute-start(f32[512,128]{1,0:T(8,128)S(1)} %get-tuple-element.53), channel_id=1, source_target_pairs={{0,4},{4,0},{8,12},{12,8},{16,20},{20,16},{24,28},{28,24},{1,5},{5... | collective-permute-start | bytes 786440 | tf_op jit(solution)/shard_map/ppermute | solution.py:336
  118.6 9.0 %collective-permute-start.19 = (f32[256,128]{1,0:T(8,128)S(1)}, f32[256,128]{1,0:T(8,128)S(1)}, u32[]{:S(2)}, u32[]{:S(2)}) collective-permute-start(f32[256,128]{1,0:T(8,128)S(1)} %get-tuple-element.91), channel_id=1, source_target_pairs={{0,8},{4,12},{8,16},{12,20},{16,24},{20,28},{24,0},{28,4},{1,9},{5... | collective-permute-start | bytes 393224 | tf_op jit(solution)/shard_map/ppermute | solution.py:340
  118.6 9.4 %collective-permute-start.21 = (f32[256,128]{1,0:T(8,128)S(1)}, f32[256,128]{1,0:T(8,128)S(1)}, u32[]{:S(2)}, u32[]{:S(2)}) collective-permute-start(f32[256,128]{1,0:T(8,128)S(1)} %get-tuple-element.92), channel_id=1, source_target_pairs={{0,24},{4,28},{8,0},{12,4},{16,8},{20,12},{24,16},{28,20},{1,25},{... | collective-permute-start | bytes 393224 | tf_op jit(solution)/shard_map/ppermute | solution.py:340
  125.5 17.9 %collective-permute-start.45 = (f32[512,128]{1,0:T(8,128)S(1)}, f32[512,128]{1,0:T(8,128)S(1)}, u32[]{:S(2)}, u32[]{:S(2)}) collective-permute-start(f32[512,128]{1,0:T(8,128)S(1)} %get-tuple-element.69), channel_id=1, source_target_pairs={{0,4},{4,0},{8,12},{12,8},{16,20},{20,16},{24,28},{28,24},{1,5},{5... | collective-permute-start | bytes 786440 | tf_op jit(solution)/shard_map/ppermute | solution.py:336
  127.6 6.8 %collective-permute-start.20 = (f32[256,128]{1,0:T(8,128)S(1)}, f32[256,128]{1,0:T(8,128)S(1)}, u32[]{:S(2)}, u32[]{:S(2)}) collective-permute-start(f32[256,128]{1,0:T(8,128)S(1)} %fusion.6), channel_id=1, source_target_pairs={{0,8},{4,12},{8,16},{12,20},{16,24},{20,28},{24,0},{28,4},{1,9},{5... | collective-permute-start | bytes 393224 | tf_op jit(solution)/shard_map/ppermute | solution.py:340
  127.7 10.3 %collective-permute-start.46 = (f32[512,128]{1,0:T(8,128)S(1)}, f32[512,128]{1,0:T(8,128)S(1)}, u32[]{:S(2)}, u32[]{:S(2)}) collective-permute-start(f32[512,128]{1,0:T(8,128)S(1)} %broadcast_select_fusion), channel_id=1, source_target_pairs={{0,4},{4,0},{8,12},{12,8},{16,20},{20,16},{24,28},{28,24},{1,5},{5... | collective-permute-start | bytes 786440 | tf_op jit(solution)/shard_map/ppermute | solution.py:336
  136.3 7.1 %collective-permute-start.55 = (f32[128,256]{1,0:T(8,128)S(1)}, f32[128,256]{1,0:T(8,128)S(1)}, u32[]{:S(2)}, u32[]{:S(2)}) collective-permute-start(f32[128,256]{1,0:T(8,128)S(1)} %get-tuple-element.76), channel_id=1, source_target_pairs={{0,1},{1,0},{2,3},{3,2},{4,5},{5,4},{6,7},{7,6},{8,9},{9,8},{10,11... | collective-permute-start | bytes 393224 | tf_op jit(solution)/shard_map/ppermute | solution.py:343
  138.0 9.2 %collective-permute-start.47 = (f32[256,128]{1,0:T(8,128)S(1)}, f32[256,128]{1,0:T(8,128)S(1)}, u32[]{:S(2)}, u32[]{:S(2)}) collective-permute-start(f32[256,128]{1,0:T(8,128)S(1)} %get-tuple-element.89), channel_id=1, source_target_pairs={{0,8},{4,12},{8,16},{12,20},{16,24},{20,28},{24,0},{28,4},{1,9},{5... | collective-permute-start | bytes 393224 | tf_op jit(solution)/shard_map/ppermute | solution.py:340
  138.1 10.5 %collective-permute-start.24 = (f32[256,128]{1,0:T(8,128)S(1)}, f32[256,128]{1,0:T(8,128)S(1)}, u32[]{:S(2)}, u32[]{:S(2)}) collective-permute-start(f32[256,128]{1,0:T(8,128)S(1)} %get-tuple-element.82.refs_0_), channel_id=1, source_target_pairs={{0,4},{4,0},{8,12},{12,8},{16,20},{20,16},{24,28},{28,24},{1,5},{5... | collective-permute-start | bytes 393224 | tf_op jit(solution)/shard_map/ppermute | solution.py:336
  139.6 18.1 %collective-permute-start.23 = (f32[256,128]{1,0:T(8,128)S(1)}, f32[256,128]{1,0:T(8,128)S(1)}, u32[]{:S(2)}, u32[]{:S(2)}) collective-permute-start(f32[256,128]{1,0:T(8,128)S(1)} %get-tuple-element.82.refs_0_), channel_id=1, source_target_pairs={{0,24},{4,28},{8,0},{12,4},{16,8},{20,12},{24,16},{28,20},{1,25},{... | collective-permute-start | bytes 393224 | tf_op jit(solution)/shard_map/ppermute | solution.py:340
  143.3 8.8 %collective-permute-start.22 = (f32[256,128]{1,0:T(8,128)S(1)}, f32[256,128]{1,0:T(8,128)S(1)}, u32[]{:S(2)}, u32[]{:S(2)}) collective-permute-start(f32[256,128]{1,0:T(8,128)S(1)} %get-tuple-element.82.refs_0_), channel_id=1, source_target_pairs={{0,8},{4,12},{8,16},{12,20},{16,24},{20,28},{24,0},{28,4},{1,9},{5... | collective-permute-start | bytes 393224 | tf_op jit(solution)/shard_map/ppermute | solution.py:340
  143.4 9.2 %collective-permute-start.49 = (f32[256,128]{1,0:T(8,128)S(1)}, f32[256,128]{1,0:T(8,128)S(1)}, u32[]{:S(2)}, u32[]{:S(2)}) collective-permute-start(f32[256,128]{1,0:T(8,128)S(1)} %get-tuple-element.90), channel_id=1, source_target_pairs={{0,24},{4,28},{8,0},{12,4},{16,8},{20,12},{24,16},{28,20},{1,25},{... | collective-permute-start | bytes 393224 | tf_op jit(solution)/shard_map/ppermute | solution.py:340
  147.3 11.8 %collective-permute-start.56 = (f32[128,256]{1,0:T(8,128)S(1)}, f32[128,256]{1,0:T(8,128)S(1)}, u32[]{:S(2)}, u32[]{:S(2)}) collective-permute-start(f32[128,256]{1,0:T(8,128)S(1)} %add.263), channel_id=1, source_target_pairs={{0,2},{1,3},{2,0},{3,1},{4,6},{5,7},{6,4},{7,5},{8,10},{9,11},{10,... | collective-permute-start | bytes 393224 | tf_op jit(solution)/shard_map/ppermute | solution.py:343
  148.7 8.1 %collective-permute-start.48 = (f32[256,128]{1,0:T(8,128)S(1)}, f32[256,128]{1,0:T(8,128)S(1)}, u32[]{:S(2)}, u32[]{:S(2)}) collective-permute-start(f32[256,128]{1,0:T(8,128)S(1)} %fusion), channel_id=1, source_target_pairs={{0,8},{4,12},{8,16},{12,20},{16,24},{20,28},{24,0},{28,4},{1,9},{5... | collective-permute-start | bytes 393224 | tf_op jit(solution)/shard_map/ppermute | solution.py:340
  152.1 7.2 %collective-permute-start.25 = (f32[256,128]{1,0:T(8,128)S(1)}, f32[256,128]{1,0:T(8,128)S(1)}, u32[]{:S(2)}, u32[]{:S(2)}) collective-permute-start(f32[256,128]{1,0:T(8,128)S(1)} %get-tuple-element.99), channel_id=1, source_target_pairs={{0,8},{4,12},{8,16},{12,20},{16,24},{20,28},{24,0},{28,4},{1,9},{5... | collective-permute-start | bytes 393224 | tf_op jit(solution)/shard_map/ppermute | solution.py:340
  157.7 6.9 %collective-permute-start.50 = (f32[256,128]{1,0:T(8,128)S(1)}, f32[256,128]{1,0:T(8,128)S(1)}, u32[]{:S(2)}, u32[]{:S(2)}) collective-permute-start(f32[256,128]{1,0:T(8,128)S(1)} %fusion.2.refs_6_), channel_id=1, source_target_pairs={{0,8},{4,12},{8,16},{12,20},{16,24},{20,28},{24,0},{28,4},{1,9},{5... | collective-permute-start | bytes 393224 | tf_op jit(solution)/shard_map/ppermute | solution.py:340
  157.7 15.1 %collective-permute-start.26 = (f32[512,128]{1,0:T(8,128)S(1)}, f32[512,128]{1,0:T(8,128)S(1)}, u32[]{:S(2)}, u32[]{:S(2)}) collective-permute-start(f32[512,128]{1,0:T(8,128)S(1)} %constant_dynamic-update-slice_fusion.2.refs_1_), channel_id=1, source_target_pairs={{0,4},{4,0},{8,12},{12,8},{16,20},{20,16},{24,28},{28,24},{1,5},{5... | collective-permute-start | bytes 786440 | tf_op jit(solution)/shard_map/ppermute | solution.py:336
  159.3 13.4 %collective-permute-start.27 = (f32[256,128]{1,0:T(8,128)S(1)}, f32[256,128]{1,0:T(8,128)S(1)}, u32[]{:S(2)}, u32[]{:S(2)}) collective-permute-start(f32[256,128]{1,0:T(8,128)S(1)} %collective-permute-done.25.refs_2_), channel_id=1, source_target_pairs={{0,4},{4,0},{8,12},{12,8},{16,20},{20,16},{24,28},{28,24},{1,5},{5... | collective-permute-start | bytes 393224 | tf_op jit(solution)/shard_map/ppermute | solution.py:336
  164.6 6.8 %collective-permute-start.53 = (f32[256,128]{1,0:T(8,128)S(1)}, f32[256,128]{1,0:T(8,128)S(1)}, u32[]{:S(2)}, u32[]{:S(2)}) collective-permute-start(f32[256,128]{1,0:T(8,128)S(1)} %get-tuple-element.97), channel_id=1, source_target_pairs={{0,8},{4,12},{8,16},{12,20},{16,24},{20,28},{24,0},{28,4},{1,9},{5... | collective-permute-start | bytes 393224 | tf_op jit(solution)/shard_map/ppermute | solution.py:340
  167.7 10.1 %collective-permute-start.54 = (f32[512,128]{1,0:T(8,128)S(1)}, f32[512,128]{1,0:T(8,128)S(1)}, u32[]{:S(2)}, u32[]{:S(2)}) collective-permute-start(f32[512,128]{1,0:T(8,128)S(1)} %constant_dynamic-update-slice_fusion.6.refs_7_), channel_id=1, source_target_pairs={{0,4},{4,0},{8,12},{12,8},{16,20},{20,16},{24,28},{28,24},{1,5},{5... | collective-permute-start | bytes 786440 | tf_op jit(solution)/shard_map/ppermute | solution.py:336
  (22 other events, 114.6 us)

commit v5 on v4

--- a/solution.py
+++ b/solution.py
@@ -234,9 +234,18 @@
     mixing = None
     for turn in range(NS_STEPS):
         factor = 1.5 * eye - 0.5 * inner
-        mixing = product(mixing, factor) if turn else factor * scale
-        if turn < NS_STEPS - 1:
-            inner = product(product(inner, factor), factor)
+        high, low = split(factor)
+        pair = jnp.concatenate([high, low], axis=1)
+        last = turn == NS_STEPS - 1
+        if turn and not last:
+            both = wide_product(jnp.concatenate([inner, mixing], axis=0), pair, size)
+            inner, mixing = both[:size], both[size:]
+        elif turn:
+            mixing = wide_product(mixing, pair, size)
+        else:
+            inner, mixing = wide_product(inner, pair, size), factor * scale
+        if not last:
+            inner = wide_product(inner, pair, size)
     return mixing
 
 

time: 195 us -> 196 us (level)
  transfers between devices with their start and end apart: 62 -> 62, of which waited for: 29 -> 28; matrix products, arithmetic and copies ran while one was open for 0% -> 0% of each run, Pallas kernels for 13% -> 13%
where the time goes in v5:
time: 196 us; the launch traced here: 195 us
  starting transfers between devices  74 us (38%)
  waiting for transfers between devices  70.4 us (36%)
  Pallas kernels  37 us (19%)
  local copies, waits for them, and re-layouts  12.4 us (6%)
    ppermute x24, starting transfers between devices, along(): lax.ppermute(block, 'cohort', [(i, (i + step) % self.cohorts) for i in ra...  33.9 us
    ppermute x20, starting transfers between devices, across(): lax.ppermute(block, 'cohort', [(i, i ^ 1) for i in range(self.cohorts)])  27.5 us
    ppermute x24, waiting for transfers between devices, along(): lax.ppermute(block, 'cohort', [(i, (i + step) % self.cohorts) for i in ra...  25.6 us
    ppermute x18, waiting for transfers between devices, feat_swap(): lax.ppermute(block, 'feat', [(i, i ^ bit) for i in range(self.feats)])  22.6 us
    ppermute x20, waiting for transfers between devices, across(): lax.ppermute(block, 'cohort', [(i, i ^ 1) for i in range(self.cohorts)])  22.2 us
    ppermute x18, starting transfers between devices, feat_swap(): lax.ppermute(block, 'feat', [(i, i ^ bit) for i in range(self.feats)])  12.5 us
    unnamed x16, local copies, waits for them, and re-layouts  12.2 us
    pallas_call x4, Pallas kernels, panel_terms(): pl.pallas_call(functools.partial(panel_kernel, sizes, squares), in_specs=...  12.1 us
  transfers between devices with their start and end apart: 62, of which 28 were waited for; matrix products, arithmetic and copies ran while one was open for 0% of the time, Pallas kernels for 13%

profile of v5, /device:TPU:0, one launch (start us, length us, event | category | flops | bytes accessed | tf_op | source)
XLA Modules:
  0.0 195.4 jit_solution(5752795148856876395)
XLA Ops:
  0.0 3.5 %copy-done.2 = f32[4,256,2048]{2,1,0:T(8,128)S(1)} copy-done((f32[4,256,2048]{2,1,0:T(8,128)S(1)}, f32[4,256,2048]{2,1,0:T(8,128)}, u32[]{:S(2)}) %copy-start.2) | copy-done | bytes 8388632
  3.5 1.8 copy-done.4
  5.4 2.6 %first_coef.2 = (f32[512,128]{1,0:T(8,128)S(1)}, f32[512,128]{1,0:T(8,128)S(1)}) custom-call(s32[1]{0:T(128)} %bitcast.8.half, f32[2048,256]{1,0:T(8,128)S(1)} %copy-done.4, f32[1024,2048]{1,0:T(8,128)S(1)} %bitcast.16), custom_call_target="tpu_custom_call" | custom-call | flops 2147483648 | bytes 8388608 | tf_op jit(solution)/shard_map/first_coef/pallas_call | solution.py:88
  8.5 2.6 %first_coef.3 = (f32[512,128]{1,0:T(8,128)S(1)}, f32[512,128]{1,0:T(8,128)S(1)}) custom-call(s32[1]{0:T(128)} %bitcast.8.half, f32[2048,256]{1,0:T(8,128)S(1)} %copy-done.4, f32[1024,2048]{1,0:T(8,128)S(1)} %bitcast.17, f32[4,2048,256]{2,1,0:T(8,128)S(1)} %copy-done), custom_call_target="tpu_custom_call" | custom-call | flops 2147483648 | bytes 8388608 | tf_op jit(solution)/shard_map/first_coef/pallas_call | solution.py:88
  11.3 3.0 %collective-permute-start.1 = (f32[512,128]{1,0:T(8,128)S(1)}, f32[512,128]{1,0:T(8,128)S(1)}, u32[]{:S(2)}, u32[]{:S(2)}) collective-permute-start(f32[512,128]{1,0:T(8,128)S(1)} %add.227), channel_id=1, source_target_pairs={{0,2},{1,3},{2,0},{3,1},{4,6},{5,7},{6,4},{7,5},{8,10},{9,11},{10,... | collective-permute-start | bytes 786440 | tf_op jit(solution)/shard_map/ppermute | solution.py:352
  14.3 6.4 %collective-permute-done.1 = f32[512,128]{1,0:T(8,128)S(1)} collective-permute-done((f32[512,128]{1,0:T(8,128)S(1)}, f32[512,128]{1,0:T(8,128)S(1)}, u32[]{:S(2)}, u32[]{:S(2)}) %collective-permute-start.1) | collective-permute-done | bytes 262176 | tf_op jit(solution)/shard_map/ppermute | solution.py:352
  22.8 3.4 %copy-done.1 = f32[4,2048,256]{2,1,0:T(8,128)S(1)} copy-done((f32[4,2048,256]{2,1,0:T(8,128)S(1)}, f32[4,2048,256]{2,1,0:T(8,128)}, u32[]{:S(2)}) %copy-start.1) | copy-done | bytes 8388632
  26.2 3.0 %panel.4 = (f32[512,128]{1,0:T(8,128)S(1)}, f32[512,128]{1,0:T(8,128)S(1)}, f32[256,128]{1,0:T(8,128)S(1)}, f32[256,128]{1,0:T(8,128)S(1)}, f32[256,128]{1,0:T(8,128)S(1)}, /*index=5*/f32[256,128]{1,0:T(8,128)S(1)}) custom-call(s32[8]{0:T(128)S(1)} %stack.53.where, s32[1]{0:T(128)} %bitcast.8.half, s32[4]{0:T(128)S(1)} %copy-done.5, ...), custom_call_target="tpu_custom_call" | custom-call | flops 2147483648 | bytes 8388608 | tf_op jit(solution)/shard_map/panel/pallas_call | solution.py:176
  29.8 1.8 collective-permute-start.4
  31.6 3.0 %panel.6 = (f32[512,128]{1,0:T(8,128)S(1)}, f32[512,128]{1,0:T(8,128)S(1)}, f32[256,128]{1,0:T(8,128)S(1)}, f32[256,128]{1,0:T(8,128)S(1)}, f32[256,128]{1,0:T(8,128)S(1)}, /*index=5*/f32[256,128]{1,0:T(8,128)S(1)}) custom-call(s32[8]{0:T(128)S(1)} %stack.53.where, s32[1]{0:T(128)} %bitcast.8.half, s32[4]{0:T(128)S(1)} %copy-done.5, ...), custom_call_target="tpu_custom_call" | custom-call | flops 2147483648 | bytes 8388608 | tf_op jit(solution)/shard_map/panel/pallas_call | solution.py:176
  34.7 3.9 %collective-permute-done.4 = f32[512,128]{1,0:T(8,128)S(1)} collective-permute-done((f32[512,128]{1,0:T(8,128)S(1)}, f32[512,128]{1,0:T(8,128)S(1)}, u32[]{:S(2)}, u32[]{:S(2)}) %collective-permute-start.4) | collective-permute-done | bytes 262176 | tf_op jit(solution)/shard_map/ppermute | solution.py:345
  38.5 1.8 collective-permute-start.32
  40.7 1.9 collective-permute-start.5
  42.5 2.1 %collective-permute-start.7 = (f32[256,128]{1,0:T(8,128)S(1)}, f32[256,128]{1,0:T(8,128)S(1)}, u32[]{:S(2)}, u32[]{:S(2)}) collective-permute-start(f32[256,128]{1,0:T(8,128)S(1)} %get-tuple-element.96), channel_id=1, source_target_pairs={{0,24},{4,28},{8,0},{12,4},{16,8},{20,12},{24,16},{28,20},{1,25},{... | collective-permute-start | bytes 393224 | tf_op jit(solution)/shard_map/ppermute | solution.py:349
  47.9 1.9 collective-permute-start.33
  49.7 3.7 %collective-permute-done.3 = f32[512,128]{1,0:T(8,128)S(1)} collective-permute-done((f32[512,128]{1,0:T(8,128)S(1)}, f32[512,128]{1,0:T(8,128)S(1)}, u32[]{:S(2)}, u32[]{:S(2)}) %collective-permute-start.3) | collective-permute-done | bytes 262176 | tf_op jit(solution)/shard_map/ppermute | solution.py:345
  53.5 1.9 collective-permute-start.6
  55.4 2.1 %collective-permute-start.35 = (f32[256,128]{1,0:T(8,128)S(1)}, f32[256,128]{1,0:T(8,128)S(1)}, u32[]{:S(2)}, u32[]{:S(2)}) collective-permute-start(f32[256,128]{1,0:T(8,128)S(1)} %get-tuple-element.94), channel_id=1, source_target_pairs={{0,24},{4,28},{8,0},{12,4},{16,8},{20,12},{24,16},{28,20},{1,25},{... | collective-permute-start | bytes 393224 | tf_op jit(solution)/shard_map/ppermute | solution.py:349
  57.8 1.9 collective-permute-start.34
  60.5 1.8 collective-permute-start.10
  69.1 2.4 %collective-permute-done.8 = f32[256,128]{1,0:T(8,128)S(1)} collective-permute-done((f32[256,128]{1,0:T(8,128)S(1)}, f32[256,128]{1,0:T(8,128)S(1)}, u32[]{:S(2)}, u32[]{:S(2)}) %collective-permute-start.8) | collective-permute-done | bytes 131104 | tf_op jit(solution)/shard_map/ppermute | solution.py:349
  73.9 3.4 %collective-permute-start.37 = (f32[256,128]{1,0:T(8,128)S(1)}, f32[256,128]{1,0:T(8,128)S(1)}, u32[]{:S(2)}, u32[]{:S(2)}) collective-permute-start(f32[256,128]{1,0:T(8,128)S(1)} %fusion.5.refs_0_.refs_6_), channel_id=1, source_target_pairs={{0,24},{4,28},{8,0},{12,4},{16,8},{20,12},{24,16},{28,20},{1,25},{... | collective-permute-start | bytes 393224 | tf_op jit(solution)/shard_map/ppermute | solution.py:349
  79.0 2.3 %collective-permute-start.13 = (f32[256,128]{1,0:T(8,128)S(1)}, f32[256,128]{1,0:T(8,128)S(1)}, u32[]{:S(2)}, u32[]{:S(2)}) collective-permute-start(f32[256,128]{1,0:T(8,128)S(1)} %collective-permute-done.11.refs_2_), channel_id=1, source_target_pairs={{0,4},{4,0},{8,12},{12,8},{16,20},{20,16},{24,28},{28,24},{1,5},{5... | collective-permute-start | bytes 393224 | tf_op jit(solution)/shard_map/ppermute | solution.py:345
  85.6 3.4 %copy-done.3 = f32[4,256,2048]{2,1,0:T(8,128)S(1)} copy-done((f32[4,256,2048]{2,1,0:T(8,128)S(1)}, f32[4,256,2048]{2,1,0:T(8,128)}, u32[]{:S(2)}) %copy-start.3) | copy-done | bytes 8388632
  89.0 3.2 %coef.2 = (f32[520,128]{1,0:T(8,128)S(1)}, f32[520,128]{1,0:T(8,128)S(1)}) custom-call(s32[8]{0:T(128)S(1)} %stack.50.where, s32[1]{0:T(128)} %bitcast.8.half, f32[1024,2048]{1,0:T(8,128)S(1)} %bitcast.18, f32[256,128]{1,0:T(8,128)S(1)} %fusion.11.refs_0_, f32[512,128]{1,0:T(8,128)S(1)} %constant_dynamic-update-slice_fusion.refs_1_, ...), custom_call_target="tpu_custom_call" | custom-call | flops 2147483648 | bytes 8388608 | tf_op jit(solution)/shard_map/coef/pallas_call | solution.py:127
  92.3 3.2 %coef.3 = (f32[520,128]{1,0:T(8,128)S(1)}, f32[520,128]{1,0:T(8,128)S(1)}) custom-call(s32[8]{0:T(128)S(1)} %stack.50.where, s32[1]{0:T(128)} %bitcast.8.half, f32[1024,2048]{1,0:T(8,128)S(1)} %bitcast.19, f32[256,128]{1,0:T(8,128)S(1)} %fusion.5.refs_0_.refs_6_, f32[512,128]{1,0:T(8,128)S(1)} %constant_dynamic-update-slice_fusion.4.refs_1_.refs_7_, ...), custom_call_target="tpu_custom_call" | custom-call | flops 2147483648 | bytes 8388608 | tf_op jit(solution)/shard_map/coef/pallas_call | solution.py:127
  97.6 6.8 %collective-permute-done.15 = f32[520,128]{1,0:T(8,128)S(1)} collective-permute-done((f32[520,128]{1,0:T(8,128)S(1)}, f32[520,128]{1,0:T(8,128)S(1)}, u32[]{:S(2)}, u32[]{:S(2)}) %collective-permute-start.15) | collective-permute-done | bytes 266272 | tf_op jit(solution)/shard_map/ppermute | solution.py:352
  106.2 3.0 %panel.5 = (f32[512,128]{1,0:T(8,128)S(1)}, f32[512,128]{1,0:T(8,128)S(1)}, f32[256,128]{1,0:T(8,128)S(1)}, f32[256,128]{1,0:T(8,128)S(1)}, f32[256,128]{1,0:T(8...) custom-call(s32[8]{0:T(128)S(1)} %stack.53.where, s32[1]{0:T(128)} %bitcast.8.half, s32[4]{0:T(128)S(1)} %copy-done.5, ...), custom_call_target="tpu_custom_call" | custom-call | flops 2147483648 | bytes 8388608 | tf_op jit(solution)/shard_map/panel/pallas_call | solution.py:176
  109.2 2.2 %collective-permute-start.18 = (f32[512,128]{1,0:T(8,128)S(1)}, f32[512,128]{1,0:T(8,128)S(1)}, u32[]{:S(2)}, u32[]{:S(2)}) collective-permute-start(f32[512,128]{1,0:T(8,128)S(1)} %get-tuple-element.56), channel_id=1, source_target_pairs={{0,4},{4,0},{8,12},{12,8},{16,20},{20,16},{24,28},{28,24},{1,5},{5... | collective-permute-start | bytes 786440 | tf_op jit(solution)/shard_map/ppermute | solution.py:345
  111.4 2.0 %collective-permute-done.43 = f32[520,128]{1,0:T(8,128)S(1)} collective-permute-done((f32[520,128]{1,0:T(8,128)S(1)}, f32[520,128]{1,0:T(8,128)S(1)}, u32[]{:S(2)}, u32[]{:S(2)}) %collective-permute-start.43) | collective-permute-done | bytes 266272 | tf_op jit(solution)/shard_map/ppermute | solution.py:352
  113.6 2.2 %collective-permute-start.17 = (f32[512,128]{1,0:T(8,128)S(1)}, f32[512,128]{1,0:T(8,128)S(1)}, u32[]{:S(2)}, u32[]{:S(2)}) collective-permute-start(f32[512,128]{1,0:T(8,128)S(1)} %get-tuple-element.53), channel_id=1, source_target_pairs={{0,4},{4,0},{8,12},{12,8},{16,20},{20,16},{24,28},{28,24},{1,5},{5... | collective-permute-start | bytes 786440 | tf_op jit(solution)/shard_map/ppermute | solution.py:345
  115.9 2.7 %collective-permute-done.18 = f32[512,128]{1,0:T(8,128)S(1)} collective-permute-done((f32[512,128]{1,0:T(8,128)S(1)}, f32[512,128]{1,0:T(8,128)S(1)}, u32[]{:S(2)}, u32[]{:S(2)}) %collective-permute-start.18) | collective-permute-done | bytes 262176 | tf_op jit(solution)/shard_map/ppermute | solution.py:345
  118.6 3.8 %collective-permute-start.21 = (f32[256,128]{1,0:T(8,128)S(1)}, f32[256,128]{1,0:T(8,128)S(1)}, u32[]{:S(2)}, u32[]{:S(2)}) collective-permute-start(f32[256,128]{1,0:T(8,128)S(1)} %get-tuple-element.92), channel_id=1, source_target_pairs={{0,24},{4,28},{8,0},{12,4},{16,8},{20,12},{24,16},{28,20},{1,25},{... | collective-permute-start | bytes 393224 | tf_op jit(solution)/shard_map/ppermute | solution.py:349
  122.4 3.0 %panel.7 = (f32[512,128]{1,0:T(8,128)S(1)}, f32[512,128]{1,0:T(8,128)S(1)}, f32[256,128]{1,0:T(8,128)S(1)}, f32[256,128]{1,0:T(8,128)S(1)}, f32[256,128]{1,0:T(8...) custom-call(s32[8]{0:T(128)S(1)} %stack.53.where, s32[1]{0:T(128)} %bitcast.8.half, s32[4]{0:T(128)S(1)} %copy-done.5, ...), custom_call_target="tpu_custom_call" | custom-call | flops 2147483648 | bytes 8388608 | tf_op jit(solution)/shard_map/panel/pallas_call | solution.py:176
  125.5 2.1 %collective-permute-start.45 = (f32[512,128]{1,0:T(8,128)S(1)}, f32[512,128]{1,0:T(8,128)S(1)}, u32[]{:S(2)}, u32[]{:S(2)}) collective-permute-start(f32[512,128]{1,0:T(8,128)S(1)} %get-tuple-element.69), channel_id=1, source_target_pairs={{0,4},{4,0},{8,12},{12,8},{16,20},{20,16},{24,28},{28,24},{1,5},{5... | collective-permute-start | bytes 786440 | tf_op jit(solution)/shard_map/ppermute | solution.py:345
  128.1 6.4 %collective-permute-done.20 = f32[256,128]{1,0:T(8,128)S(1)} collective-permute-done((f32[256,128]{1,0:T(8,128)S(1)}, f32[256,128]{1,0:T(8,128)S(1)}, u32[]{:S(2)}, u32[]{:S(2)}) %collective-permute-start.20) | collective-permute-done | bytes 131104 | tf_op jit(solution)/shard_map/ppermute | solution.py:349
  139.6 3.7 %collective-permute-start.23 = (f32[256,128]{1,0:T(8,128)S(1)}, f32[256,128]{1,0:T(8,128)S(1)}, u32[]{:S(2)}, u32[]{:S(2)}) collective-permute-start(f32[256,128]{1,0:T(8,128)S(1)} %get-tuple-element.82.refs_0_), channel_id=1, source_target_pairs={{0,24},{4,28},{8,0},{12,4},{16,8},{20,12},{24,16},{28,20},{1,25},{... | collective-permute-start | bytes 393224 | tf_op jit(solution)/shard_map/ppermute | solution.py:349
  143.4 3.9 %collective-permute-start.49 = (f32[256,128]{1,0:T(8,128)S(1)}, f32[256,128]{1,0:T(8,128)S(1)}, u32[]{:S(2)}, u32[]{:S(2)}) collective-permute-start(f32[256,128]{1,0:T(8,128)S(1)} %get-tuple-element.90), channel_id=1, source_target_pairs={{0,24},{4,28},{8,0},{12,4},{16,8},{20,12},{24,16},{28,20},{1,25},{... | collective-permute-start | bytes 393224 | tf_op jit(solution)/shard_map/ppermute | solution.py:349
  148.7 3.4 %collective-permute-done.22 = f32[256,128]{1,0:T(8,128)S(1)} collective-permute-done((f32[256,128]{1,0:T(8,128)S(1)}, f32[256,128]{1,0:T(8,128)S(1)}, u32[]{:S(2)}, u32[]{:S(2)}) %collective-permute-start.22) | collective-permute-done | bytes 131104 | tf_op jit(solution)/shard_map/ppermute | solution.py:349
  152.6 4.2 %collective-permute-done.48 = f32[256,128]{1,0:T(8,128)S(1)} collective-permute-done((f32[256,128]{1,0:T(8,128)S(1)}, f32[256,128]{1,0:T(8,128)S(1)}, u32[]{:S(2)}, u32[]{:S(2)}) %collective-permute-start.48) | collective-permute-done | bytes 131104 | tf_op jit(solution)/shard_map/ppermute | solution.py:349
  159.9 1.9 collective-permute-done.52.refs_9_
  161.9 1.9 collective-permute-start.51
  164.9 3.2 %mixing.2.before = f32[256,256]{1,0:T(8,128)S(1)} custom-call(s32[1]{0:T(128)} %bitcast.8.half, f32[128,256]{1,0:T(8,128)S(1)} %add.264.mine, f32[128,256]{1,0:T(8,128)S(1)} %collective-permute-done.57.partner), custom_call_target="tpu_custom_call" | custom-call | flops 1509949440 | bytes 786432 | tf_op jit(solution)/shard_map/mixing/pallas_call | solution.py:276
  169.5 2.2 %collective-permute-done.53.refs_8_ = f32[256,128]{1,0:T(8,128)S(1)} collective-permute-done((f32[256,128]{1,0:T(8,128)S(1)}, f32[256,128]{1,0:T(8,128)S(1)}, u32[]{:S(2)}, u32[]{:S(2)}) %collective-permute-start.53) | collective-permute-done | bytes 131104 | tf_op jit(solution)/shard_map/ppermute | solution.py:349
  173.0 5.4 %collective-permute-done.58.refs_11_ = f32[256,128]{1,0:T(8,128)S(1)} collective-permute-done((f32[256,128]{1,0:T(8,128)S(1)}, f32[256,128]{1,0:T(8,128)S(1)}, u32[]{:S(2)}, u32[]{:S(2)}) %collective-permute-start.58) | collective-permute-done | bytes 131104 | tf_op jit(solution)/shard_map/ppermute | solution.py:345
  183.0 4.2 %collective-permute-done.60 = f32[128,256]{1,0:T(8,128)S(1)} collective-permute-done((f32[128,256]{1,0:T(8,128)S(1)}, f32[128,256]{1,0:T(8,128)S(1)}, u32[]{:S(2)}, u32[]{:S(2)}) %collective-permute-start.60) | collective-permute-done | bytes 131104 | tf_op jit(solution)/shard_map/ppermute | solution.py:352
  188.6 4.2 %mixing.3 = f32[256,256]{1,0:T(8,128)S(1)} custom-call(s32[1]{0:T(128)} %bitcast.8.half, f32[128,256]{1,0:T(8,128)S(1)} %add.266.mine, f32[128,256]{1,0:T(8,128)S(1)} %collective-permute-done.61.partner, f32[256,256]{1,0:T(8,128)S(1)} %mixing.2.before, f32[8,128]{1,0:T(8,128)S(1)} %get-tuple-element.79.refs_0_, f32[8,128]{1,0:T(8,128)S(1)} %get-tuple-element.80.refs_1_), custom_call_target="tpu_custom_call" | custom-call | flops 1509949440 | bytes 786432 | tf_op jit(solution)/shard_map/mixing/pallas_call | solution.py:276
  192.8 2.5 %apply.1 = f32[2048,256]{1,0:T(8,128)} custom-call(s32[8]{0:T(128)S(1)} %stack.50.where, f32[256,256]{1,0:T(8,128)S(1)} %mixing.3, f32[256,128]{1,0:T(8,128)S(1)} %get-tuple-element.82.refs_0_, f32[512,128]{1,0:T(8,128)S(1)} %constant_dynamic-update-slice_fusion.2.refs_1_, f32[256,128]{1,0:T(8,128)S(1)} %collective-permute-done.25.refs_2_, ...), custom_call_target="tpu_custom_call" | custom-call | flops 805306368 | bytes 4194304 | tf_op jit(solution)/shard_map/apply/pallas_call | solution.py:308
  (144 shorter events, 47.7 us)
Async XLA Ops:
  11.3 9.5 %collective-permute-start.1 = (f32[512,128]{1,0:T(8,128)S(1)}, f32[512,128]{1,0:T(8,128)S(1)}, u32[]{:S(2)}, u32[]{:S(2)}) collective-permute-start(f32[512,128]{1,0:T(8,128)S(1)} %add.227), channel_id=1, source_target_pairs={{0,2},{1,3},{2,0},{3,1},{4,6},{5,7},{6,4},{7,5},{8,10},{9,11},{10,... | collective-permute-start | bytes 786440 | tf_op jit(solution)/shard_map/ppermute | solution.py:352
  20.9 8.7 %collective-permute-start.29 = (f32[512,128]{1,0:T(8,128)S(1)}, f32[512,128]{1,0:T(8,128)S(1)}, u32[]{:S(2)}, u32[]{:S(2)}) collective-permute-start(f32[512,128]{1,0:T(8,128)S(1)} %get-tuple-element.87), channel_id=1, source_target_pairs={{0,2},{1,3},{2,0},{3,1},{4,6},{5,7},{6,4},{7,5},{8,10},{9,11},{10,... | collective-permute-start | bytes 786440 | tf_op jit(solution)/shard_map/ppermute | solution.py:352
  29.8 8.7 %collective-permute-start.4 = (f32[512,128]{1,0:T(8,128)S(1)}, f32[512,128]{1,0:T(8,128)S(1)}, u32[]{:S(2)}, u32[]{:S(2)}) collective-permute-start(f32[512,128]{1,0:T(8,128)S(1)} %get-tuple-element.48), channel_id=1, source_target_pairs={{0,4},{4,0},{8,12},{12,8},{16,20},{20,16},{24,28},{28,24},{1,5},{5... | collective-permute-start | bytes 786440 | tf_op jit(solution)/shard_map/ppermute | solution.py:345
  38.5 9.3 %collective-permute-start.32 = (f32[512,128]{1,0:T(8,128)S(1)}, f32[512,128]{1,0:T(8,128)S(1)}, u32[]{:S(2)}, u32[]{:S(2)}) collective-permute-start(f32[512,128]{1,0:T(8,128)S(1)} %broadcast_select_fusion.1), channel_id=1, source_target_pairs={{0,4},{4,0},{8,12},{12,8},{16,20},{20,16},{24,28},{28,24},{1,5},{5... | collective-permute-start | bytes 786440 | tf_op jit(solution)/shard_map/ppermute | solution.py:345
  40.4 13.1 %collective-permute-start.3 = (f32[512,128]{1,0:T(8,128)S(1)}, f32[512,128]{1,0:T(8,128)S(1)}, u32[]{:S(2)}, u32[]{:S(2)}) collective-permute-start(f32[512,128]{1,0:T(8,128)S(1)} %get-tuple-element.45), channel_id=1, source_target_pairs={{0,4},{4,0},{8,12},{12,8},{16,20},{20,16},{24,28},{28,24},{1,5},{5... | collective-permute-start | bytes 786440 | tf_op jit(solution)/shard_map/ppermute | solution.py:345
  40.7 12.8 %collective-permute-start.5 = (f32[256,128]{1,0:T(8,128)S(1)}, f32[256,128]{1,0:T(8,128)S(1)}, u32[]{:S(2)}, u32[]{:S(2)}) collective-permute-start(f32[256,128]{1,0:T(8,128)S(1)} %get-tuple-element.95), channel_id=1, source_target_pairs={{0,8},{4,12},{8,16},{12,20},{16,24},{20,28},{24,0},{28,4},{1,9},{5... | collective-permute-start | bytes 393224 | tf_op jit(solution)/shard_map/ppermute | solution.py:349
  42.5 17.1 %collective-permute-start.7 = (f32[256,128]{1,0:T(8,128)S(1)}, f32[256,128]{1,0:T(8,128)S(1)}, u32[]{:S(2)}, u32[]{:S(2)}) collective-permute-start(f32[256,128]{1,0:T(8,128)S(1)} %get-tuple-element.96), channel_id=1, source_target_pairs={{0,24},{4,28},{8,0},{12,4},{16,8},{20,12},{24,16},{28,20},{1,25},{... | collective-permute-start | bytes 393224 | tf_op jit(solution)/shard_map/ppermute | solution.py:349
  44.6 13.1 %collective-permute-start.31 = (f32[512,128]{1,0:T(8,128)S(1)}, f32[512,128]{1,0:T(8,128)S(1)}, u32[]{:S(2)}, u32[]{:S(2)}) collective-permute-start(f32[512,128]{1,0:T(8,128)S(1)} %get-tuple-element.61), channel_id=1, source_target_pairs={{0,4},{4,0},{8,12},{12,8},{16,20},{20,16},{24,28},{28,24},{1,5},{5... | collective-permute-start | bytes 786440 | tf_op jit(solution)/shard_map/ppermute | solution.py:345
  47.9 9.9 %collective-permute-start.33 = (f32[256,128]{1,0:T(8,128)S(1)}, f32[256,128]{1,0:T(8,128)S(1)}, u32[]{:S(2)}, u32[]{:S(2)}) collective-permute-start(f32[256,128]{1,0:T(8,128)S(1)} %get-tuple-element.93), channel_id=1, source_target_pairs={{0,8},{4,12},{8,16},{12,20},{16,24},{20,28},{24,0},{28,4},{1,9},{5... | collective-permute-start | bytes 393224 | tf_op jit(solution)/shard_map/ppermute | solution.py:349
  53.5 6.9 %collective-permute-start.6 = (f32[256,128]{1,0:T(8,128)S(1)}, f32[256,128]{1,0:T(8,128)S(1)}, u32[]{:S(2)}, u32[]{:S(2)}) collective-permute-start(f32[256,128]{1,0:T(8,128)S(1)} %fusion.9), channel_id=1, source_target_pairs={{0,8},{4,12},{8,16},{12,20},{16,24},{20,28},{24,0},{28,4},{1,9},{5... | collective-permute-start | bytes 393224 | tf_op jit(solution)/shard_map/ppermute | solution.py:349
  55.4 9.0 %collective-permute-start.35 = (f32[256,128]{1,0:T(8,128)S(1)}, f32[256,128]{1,0:T(8,128)S(1)}, u32[]{:S(2)}, u32[]{:S(2)}) collective-permute-start(f32[256,128]{1,0:T(8,128)S(1)} %get-tuple-element.94), channel_id=1, source_target_pairs={{0,24},{4,28},{8,0},{12,4},{16,8},{20,12},{24,16},{28,20},{1,25},{... | collective-permute-start | bytes 393224 | tf_op jit(solution)/shard_map/ppermute | solution.py:349
  57.8 8.4 %collective-permute-start.34 = (f32[256,128]{1,0:T(8,128)S(1)}, f32[256,128]{1,0:T(8,128)S(1)}, u32[]{:S(2)}, u32[]{:S(2)}) collective-permute-start(f32[256,128]{1,0:T(8,128)S(1)} %fusion.3), channel_id=1, source_target_pairs={{0,8},{4,12},{8,16},{12,20},{16,24},{20,28},{24,0},{28,4},{1,9},{5... | collective-permute-start | bytes 393224 | tf_op jit(solution)/shard_map/ppermute | solution.py:349
  60.5 8.7 %collective-permute-start.10 = (f32[256,128]{1,0:T(8,128)S(1)}, f32[256,128]{1,0:T(8,128)S(1)}, u32[]{:S(2)}, u32[]{:S(2)}) collective-permute-start(f32[256,128]{1,0:T(8,128)S(1)} %fusion.11.refs_0_), channel_id=1, source_target_pairs={{0,4},{4,0},{8,12},{12,8},{16,20},{20,16},{24,28},{28,24},{1,5},{5... | collective-permute-start | bytes 393224 | tf_op jit(solution)/shard_map/ppermute | solution.py:345
  62.3 10.4 %collective-permute-start.9 = (f32[256,128]{1,0:T(8,128)S(1)}, f32[256,128]{1,0:T(8,128)S(1)}, u32[]{:S(2)}, u32[]{:S(2)}) collective-permute-start(f32[256,128]{1,0:T(8,128)S(1)} %fusion.11.refs_0_), channel_id=1, source_target_pairs={{0,24},{4,28},{8,0},{12,4},{16,8},{20,12},{24,16},{28,20},{1,25},{... | collective-permute-start | bytes 393224 | tf_op jit(solution)/shard_map/ppermute | solution.py:349
  64.0 7.6 %collective-permute-start.8 = (f32[256,128]{1,0:T(8,128)S(1)}, f32[256,128]{1,0:T(8,128)S(1)}, u32[]{:S(2)}, u32[]{:S(2)}) collective-permute-start(f32[256,128]{1,0:T(8,128)S(1)} %fusion.11.refs_0_), channel_id=1, source_target_pairs={{0,8},{4,12},{8,16},{12,20},{16,24},{20,28},{24,0},{28,4},{1,9},{5... | collective-permute-start | bytes 393224 | tf_op jit(solution)/shard_map/ppermute | solution.py:349
  66.2 11.2 %collective-permute-start.38 = (f32[256,128]{1,0:T(8,128)S(1)}, f32[256,128]{1,0:T(8,128)S(1)}, u32[]{:S(2)}, u32[]{:S(2)}) collective-permute-start(f32[256,128]{1,0:T(8,128)S(1)} %fusion.5.refs_0_.refs_6_), channel_id=1, source_target_pairs={{0,4},{4,0},{8,12},{12,8},{16,20},{20,16},{24,28},{28,24},{1,5},{5... | collective-permute-start | bytes 393224 | tf_op jit(solution)/shard_map/ppermute | solution.py:345
  67.8 9.5 %collective-permute-start.36 = (f32[256,128]{1,0:T(8,128)S(1)}, f32[256,128]{1,0:T(8,128)S(1)}, u32[]{:S(2)}, u32[]{:S(2)}) collective-permute-start(f32[256,128]{1,0:T(8,128)S(1)} %fusion.5.refs_0_.refs_6_), channel_id=1, source_target_pairs={{0,8},{4,12},{8,16},{12,20},{16,24},{20,28},{24,0},{28,4},{1,9},{5... | collective-permute-start | bytes 393224 | tf_op jit(solution)/shard_map/ppermute | solution.py:349
  71.6 7.5 %collective-permute-start.11 = (f32[256,128]{1,0:T(8,128)S(1)}, f32[256,128]{1,0:T(8,128)S(1)}, u32[]{:S(2)}, u32[]{:S(2)}) collective-permute-start(f32[256,128]{1,0:T(8,128)S(1)} %get-tuple-element.101), channel_id=1, source_target_pairs={{0,8},{4,12},{8,16},{12,20},{16,24},{20,28},{24,0},{28,4},{1,9},{5... | collective-permute-start | bytes 393224 | tf_op jit(solution)/shard_map/ppermute | solution.py:349
  72.7 12.9 %collective-permute-start.12 = (f32[512,128]{1,0:T(8,128)S(1)}, f32[512,128]{1,0:T(8,128)S(1)}, u32[]{:S(2)}, u32[]{:S(2)}) collective-permute-start(f32[512,128]{1,0:T(8,128)S(1)} %constant_dynamic-update-slice_fusion.refs_1_), channel_id=1, source_target_pairs={{0,4},{4,0},{8,12},{12,8},{16,20},{20,16},{24,28},{28,24},{1,5},{5... | collective-permute-start | bytes 786440 | tf_op jit(solution)/shard_map/ppermute | solution.py:345
  73.9 7.8 %collective-permute-start.37 = (f32[256,128]{1,0:T(8,128)S(1)}, f32[256,128]{1,0:T(8,128)S(1)}, u32[]{:S(2)}, u32[]{:S(2)}) collective-permute-start(f32[256,128]{1,0:T(8,128)S(1)} %fusion.5.refs_0_.refs_6_), channel_id=1, source_target_pairs={{0,24},{4,28},{8,0},{12,4},{16,8},{20,12},{24,16},{28,20},{1,25},{... | collective-permute-start | bytes 393224 | tf_op jit(solution)/shard_map/ppermute | solution.py:349
  77.4 6.8 %collective-permute-start.39 = (f32[256,128]{1,0:T(8,128)S(1)}, f32[256,128]{1,0:T(8,128)S(1)}, u32[]{:S(2)}, u32[]{:S(2)}) collective-permute-start(f32[256,128]{1,0:T(8,128)S(1)} %get-tuple-element.103), channel_id=1, source_target_pairs={{0,8},{4,12},{8,16},{12,20},{16,24},{20,28},{24,0},{28,4},{1,9},{5... | collective-permute-start | bytes 393224 | tf_op jit(solution)/shard_map/ppermute | solution.py:349
  81.7 10.6 %collective-permute-start.40 = (f32[512,128]{1,0:T(8,128)S(1)}, f32[512,128]{1,0:T(8,128)S(1)}, u32[]{:S(2)}, u32[]{:S(2)}) collective-permute-start(f32[512,128]{1,0:T(8,128)S(1)} %constant_dynamic-update-slice_fusion.4.refs_1_.refs_7_), channel_id=1, source_target_pairs={{0,4},{4,0},{8,12},{12,8},{16,20},{20,16},{24,28},{28,24},{1,5},{5... | collective-permute-start | bytes 786440 | tf_op jit(solution)/shard_map/ppermute | solution.py:345
  84.2 8.1 %collective-permute-start.41 = (f32[256,128]{1,0:T(8,128)S(1)}, f32[256,128]{1,0:T(8,128)S(1)}, u32[]{:S(2)}, u32[]{:S(2)}) collective-permute-start(f32[256,128]{1,0:T(8,128)S(1)} %collective-permute-done.39.refs_2_.refs_8_), channel_id=1, source_target_pairs={{0,4},{4,0},{8,12},{12,8},{16,20},{20,16},{24,28},{28,24},{1,5},{5... | collective-permute-start | bytes 393224 | tf_op jit(solution)/shard_map/ppermute | solution.py:345
  96.1 8.4 %collective-permute-start.15 = (f32[520,128]{1,0:T(8,128)S(1)}, f32[520,128]{1,0:T(8,128)S(1)}, u32[]{:S(2)}, u32[]{:S(2)}) collective-permute-start(f32[520,128]{1,0:T(8,128)S(1)} %add.236), channel_id=1, source_target_pairs={{0,2},{1,3},{2,0},{3,1},{4,6},{5,7},{6,4},{7,5},{8,10},{9,11},{10,... | collective-permute-start | bytes 798728 | tf_op jit(solution)/shard_map/ppermute | solution.py:352
  104.6 8.8 %collective-permute-start.43 = (f32[520,128]{1,0:T(8,128)S(1)}, f32[520,128]{1,0:T(8,128)S(1)}, u32[]{:S(2)}, u32[]{:S(2)}) collective-permute-start(f32[520,128]{1,0:T(8,128)S(1)} %get-tuple-element.83), channel_id=1, source_target_pairs={{0,2},{1,3},{2,0},{3,1},{4,6},{5,7},{6,4},{7,5},{8,10},{9,11},{10,... | collective-permute-start | bytes 798728 | tf_op jit(solution)/shard_map/ppermute | solution.py:352
  109.2 9.3 %collective-permute-start.18 = (f32[512,128]{1,0:T(8,128)S(1)}, f32[512,128]{1,0:T(8,128)S(1)}, u32[]{:S(2)}, u32[]{:S(2)}) collective-permute-start(f32[512,128]{1,0:T(8,128)S(1)} %get-tuple-element.56), channel_id=1, source_target_pairs={{0,4},{4,0},{8,12},{12,8},{16,20},{20,16},{24,28},{28,24},{1,5},{5... | collective-permute-start | bytes 786440 | tf_op jit(solution)/shard_map/ppermute | solution.py:345
  113.6 8.9 %collective-permute-start.44 = (f32[520,128]{1,0:T(8,128)S(1)}, f32[520,128]{1,0:T(8,128)S(1)}, u32[]{:S(2)}, u32[]{:S(2)}) collective-permute-start(f32[520,128]{1,0:T(8,128)S(1)} %pad_maximum_fusion), channel_id=1, source_target_pairs={{0,1},{1,0},{2,3},{3,2},{4,5},{5,4},{6,7},{7,6},{8,9},{9,8},{10,11... | collective-permute-start | bytes 798728 | tf_op jit(solution)/shard_map/ppermute | solution.py:352
  113.6 14.0 %collective-permute-start.17 = (f32[512,128]{1,0:T(8,128)S(1)}, f32[512,128]{1,0:T(8,128)S(1)}, u32[]{:S(2)}, u32[]{:S(2)}) collective-permute-start(f32[512,128]{1,0:T(8,128)S(1)} %get-tuple-element.53), channel_id=1, source_target_pairs={{0,4},{4,0},{8,12},{12,8},{16,20},{20,16},{24,28},{28,24},{1,5},{5... | collective-permute-start | bytes 786440 | tf_op jit(solution)/shard_map/ppermute | solution.py:345
  118.6 9.0 %collective-permute-start.19 = (f32[256,128]{1,0:T(8,128)S(1)}, f32[256,128]{1,0:T(8,128)S(1)}, u32[]{:S(2)}, u32[]{:S(2)}) collective-permute-start(f32[256,128]{1,0:T(8,128)S(1)} %get-tuple-element.91), channel_id=1, source_target_pairs={{0,8},{4,12},{8,16},{12,20},{16,24},{20,28},{24,0},{28,4},{1,9},{5... | collective-permute-start | bytes 393224 | tf_op jit(solution)/shard_map/ppermute | solution.py:349
  118.6 9.4 %collective-permute-start.21 = (f32[256,128]{1,0:T(8,128)S(1)}, f32[256,128]{1,0:T(8,128)S(1)}, u32[]{:S(2)}, u32[]{:S(2)}) collective-permute-start(f32[256,128]{1,0:T(8,128)S(1)} %get-tuple-element.92), channel_id=1, source_target_pairs={{0,24},{4,28},{8,0},{12,4},{16,8},{20,12},{24,16},{28,20},{1,25},{... | collective-permute-start | bytes 393224 | tf_op jit(solution)/shard_map/ppermute | solution.py:349
  125.5 17.9 %collective-permute-start.45 = (f32[512,128]{1,0:T(8,128)S(1)}, f32[512,128]{1,0:T(8,128)S(1)}, u32[]{:S(2)}, u32[]{:S(2)}) collective-permute-start(f32[512,128]{1,0:T(8,128)S(1)} %get-tuple-element.69), channel_id=1, source_target_pairs={{0,4},{4,0},{8,12},{12,8},{16,20},{20,16},{24,28},{28,24},{1,5},{5... | collective-permute-start | bytes 786440 | tf_op jit(solution)/shard_map/ppermute | solution.py:345
  127.6 6.8 %collective-permute-start.20 = (f32[256,128]{1,0:T(8,128)S(1)}, f32[256,128]{1,0:T(8,128)S(1)}, u32[]{:S(2)}, u32[]{:S(2)}) collective-permute-start(f32[256,128]{1,0:T(8,128)S(1)} %fusion.6), channel_id=1, source_target_pairs={{0,8},{4,12},{8,16},{12,20},{16,24},{20,28},{24,0},{28,4},{1,9},{5... | collective-permute-start | bytes 393224 | tf_op jit(solution)/shard_map/ppermute | solution.py:349
  127.7 10.3 %collective-permute-start.46 = (f32[512,128]{1,0:T(8,128)S(1)}, f32[512,128]{1,0:T(8,128)S(1)}, u32[]{:S(2)}, u32[]{:S(2)}) collective-permute-start(f32[512,128]{1,0:T(8,128)S(1)} %broadcast_select_fusion), channel_id=1, source_target_pairs={{0,4},{4,0},{8,12},{12,8},{16,20},{20,16},{24,28},{28,24},{1,5},{5... | collective-permute-start | bytes 786440 | tf_op jit(solution)/shard_map/ppermute | solution.py:345
  136.3 7.1 %collective-permute-start.55 = (f32[128,256]{1,0:T(8,128)S(1)}, f32[128,256]{1,0:T(8,128)S(1)}, u32[]{:S(2)}, u32[]{:S(2)}) collective-permute-start(f32[128,256]{1,0:T(8,128)S(1)} %get-tuple-element.76), channel_id=1, source_target_pairs={{0,1},{1,0},{2,3},{3,2},{4,5},{5,4},{6,7},{7,6},{8,9},{9,8},{10,11... | collective-permute-start | bytes 393224 | tf_op jit(solution)/shard_map/ppermute | solution.py:352
  138.0 9.2 %collective-permute-start.47 = (f32[256,128]{1,0:T(8,128)S(1)}, f32[256,128]{1,0:T(8,128)S(1)}, u32[]{:S(2)}, u32[]{:S(2)}) collective-permute-start(f32[256,128]{1,0:T(8,128)S(1)} %get-tuple-element.89), channel_id=1, source_target_pairs={{0,8},{4,12},{8,16},{12,20},{16,24},{20,28},{24,0},{28,4},{1,9},{5... | collective-permute-start | bytes 393224 | tf_op jit(solution)/shard_map/ppermute | solution.py:349
  138.1 10.5 %collective-permute-start.24 = (f32[256,128]{1,0:T(8,128)S(1)}, f32[256,128]{1,0:T(8,128)S(1)}, u32[]{:S(2)}, u32[]{:S(2)}) collective-permute-start(f32[256,128]{1,0:T(8,128)S(1)} %get-tuple-element.82.refs_0_), channel_id=1, source_target_pairs={{0,4},{4,0},{8,12},{12,8},{16,20},{20,16},{24,28},{28,24},{1,5},{5... | collective-permute-start | bytes 393224 | tf_op jit(solution)/shard_map/ppermute | solution.py:345
  139.6 18.1 %collective-permute-start.23 = (f32[256,128]{1,0:T(8,128)S(1)}, f32[256,128]{1,0:T(8,128)S(1)}, u32[]{:S(2)}, u32[]{:S(2)}) collective-permute-start(f32[256,128]{1,0:T(8,128)S(1)} %get-tuple-element.82.refs_0_), channel_id=1, source_target_pairs={{0,24},{4,28},{8,0},{12,4},{16,8},{20,12},{24,16},{28,20},{1,25},{... | collective-permute-start | bytes 393224 | tf_op jit(solution)/shard_map/ppermute | solution.py:349
  143.3 8.8 %collective-permute-start.22 = (f32[256,128]{1,0:T(8,128)S(1)}, f32[256,128]{1,0:T(8,128)S(1)}, u32[]{:S(2)}, u32[]{:S(2)}) collective-permute-start(f32[256,128]{1,0:T(8,128)S(1)} %get-tuple-element.82.refs_0_), channel_id=1, source_target_pairs={{0,8},{4,12},{8,16},{12,20},{16,24},{20,28},{24,0},{28,4},{1,9},{5... | collective-permute-start | bytes 393224 | tf_op jit(solution)/shard_map/ppermute | solution.py:349
  143.4 9.2 %collective-permute-start.49 = (f32[256,128]{1,0:T(8,128)S(1)}, f32[256,128]{1,0:T(8,128)S(1)}, u32[]{:S(2)}, u32[]{:S(2)}) collective-permute-start(f32[256,128]{1,0:T(8,128)S(1)} %get-tuple-element.90), channel_id=1, source_target_pairs={{0,24},{4,28},{8,0},{12,4},{16,8},{20,12},{24,16},{28,20},{1,25},{... | collective-permute-start | bytes 393224 | tf_op jit(solution)/shard_map/ppermute | solution.py:349
  147.3 11.8 %collective-permute-start.56 = (f32[128,256]{1,0:T(8,128)S(1)}, f32[128,256]{1,0:T(8,128)S(1)}, u32[]{:S(2)}, u32[]{:S(2)}) collective-permute-start(f32[128,256]{1,0:T(8,128)S(1)} %add.263), channel_id=1, source_target_pairs={{0,2},{1,3},{2,0},{3,1},{4,6},{5,7},{6,4},{7,5},{8,10},{9,11},{10,... | collective-permute-start | bytes 393224 | tf_op jit(solution)/shard_map/ppermute | solution.py:352
  148.7 8.1 %collective-permute-start.48 = (f32[256,128]{1,0:T(8,128)S(1)}, f32[256,128]{1,0:T(8,128)S(1)}, u32[]{:S(2)}, u32[]{:S(2)}) collective-permute-start(f32[256,128]{1,0:T(8,128)S(1)} %fusion), channel_id=1, source_target_pairs={{0,8},{4,12},{8,16},{12,20},{16,24},{20,28},{24,0},{28,4},{1,9},{5... | collective-permute-start | bytes 393224 | tf_op jit(solution)/shard_map/ppermute | solution.py:349
  152.1 7.2 %collective-permute-start.25 = (f32[256,128]{1,0:T(8,128)S(1)}, f32[256,128]{1,0:T(8,128)S(1)}, u32[]{:S(2)}, u32[]{:S(2)}) collective-permute-start(f32[256,128]{1,0:T(8,128)S(1)} %get-tuple-element.99), channel_id=1, source_target_pairs={{0,8},{4,12},{8,16},{12,20},{16,24},{20,28},{24,0},{28,4},{1,9},{5... | collective-permute-start | bytes 393224 | tf_op jit(solution)/shard_map/ppermute | solution.py:349
  157.7 6.9 %collective-permute-start.50 = (f32[256,128]{1,0:T(8,128)S(1)}, f32[256,128]{1,0:T(8,128)S(1)}, u32[]{:S(2)}, u32[]{:S(2)}) collective-permute-start(f32[256,128]{1,0:T(8,128)S(1)} %fusion.2.refs_6_), channel_id=1, source_target_pairs={{0,8},{4,12},{8,16},{12,20},{16,24},{20,28},{24,0},{28,4},{1,9},{5... | collective-permute-start | bytes 393224 | tf_op jit(solution)/shard_map/ppermute | solution.py:349
  157.7 15.3 %collective-permute-start.26 = (f32[512,128]{1,0:T(8,128)S(1)}, f32[512,128]{1,0:T(8,128)S(1)}, u32[]{:S(2)}, u32[]{:S(2)}) collective-permute-start(f32[512,128]{1,0:T(8,128)S(1)} %constant_dynamic-update-slice_fusion.2.refs_1_), channel_id=1, source_target_pairs={{0,4},{4,0},{8,12},{12,8},{16,20},{20,16},{24,28},{28,24},{1,5},{5... | collective-permute-start | bytes 786440 | tf_op jit(solution)/shard_map/ppermute | solution.py:345
  159.3 13.7 %collective-permute-start.27 = (f32[256,128]{1,0:T(8,128)S(1)}, f32[256,128]{1,0:T(8,128)S(1)}, u32[]{:S(2)}, u32[]{:S(2)}) collective-permute-start(f32[256,128]{1,0:T(8,128)S(1)} %collective-permute-done.25.refs_2_), channel_id=1, source_target_pairs={{0,4},{4,0},{8,12},{12,8},{16,20},{20,16},{24,28},{28,24},{1,5},{5... | collective-permute-start | bytes 393224 | tf_op jit(solution)/shard_map/ppermute | solution.py:345
  164.6 7.1 %collective-permute-start.53 = (f32[256,128]{1,0:T(8,128)S(1)}, f32[256,128]{1,0:T(8,128)S(1)}, u32[]{:S(2)}, u32[]{:S(2)}) collective-permute-start(f32[256,128]{1,0:T(8,128)S(1)} %get-tuple-element.97), channel_id=1, source_target_pairs={{0,8},{4,12},{8,16},{12,20},{16,24},{20,28},{24,0},{28,4},{1,9},{5... | collective-permute-start | bytes 393224 | tf_op jit(solution)/shard_map/ppermute | solution.py:349
  168.2 10.2 %collective-permute-start.54 = (f32[512,128]{1,0:T(8,128)S(1)}, f32[512,128]{1,0:T(8,128)S(1)}, u32[]{:S(2)}, u32[]{:S(2)}) collective-permute-start(f32[512,128]{1,0:T(8,128)S(1)} %constant_dynamic-update-slice_fusion.6.refs_7_), channel_id=1, source_target_pairs={{0,4},{4,0},{8,12},{12,8},{16,20},{20,16},{24,28},{28,24},{1,5},{5... | collective-permute-start | bytes 786440 | tf_op jit(solution)/shard_map/ppermute | solution.py:345
  171.7 6.7 %collective-permute-start.58 = (f32[256,128]{1,0:T(8,128)S(1)}, f32[256,128]{1,0:T(8,128)S(1)}, u32[]{:S(2)}, u32[]{:S(2)}) collective-permute-start(f32[256,128]{1,0:T(8,128)S(1)} %slice_select_fusion.1), channel_id=1, source_target_pairs={{0,4},{4,0},{8,12},{12,8},{16,20},{20,16},{24,28},{28,24},{1,5},{5... | collective-permute-start | bytes 393224 | tf_op jit(solution)/shard_map/ppermute | solution.py:345
  (22 other events, 115.6 us)
